TPU v7x, 128 devices: a whole 4x4x4 slice. The times are simulated.
128 devices in a mesh: ep: 8 (over y, z_hi), dp: 16 (over z_lo, x, core).
Axes of the slice: x: 4, y: 4, z: 4 (z_hi: 2, z_lo: 2; z = z_hi * 2 + z_lo), core: 2. Of those that a mesh axis runs over, the one named last changes fastest.
Arguments:
- checkpoint: bfloat16 [16384, 2048], P('ep', 'dp'), may hold values from -6 to 6
- cotangent: bfloat16 [16384, 2048], P(('ep', 'dp')), may hold values from -6 to 6
- routes: int32 [16384, 2], P(('ep', 'dp')), may hold values from 0 to 7, all different within a row; in each aligned block of 128 rows (0 to 127, 128 to 255, ...) at most 64 rows name the same one
- gates: float32 [16384, 2], P(('ep', 'dp')), may hold values from 0.1 to 1
- w_gate: bfloat16 [8, 2048, 1024], P('ep'), may hold values from -0.125 to 0.125
- w_up: bfloat16 [8, 2048, 1024], P('ep'), may hold values from -0.125 to 0.125
- w_down: bfloat16 [8, 2048, 1024], P('ep'), may hold values from -0.1875 to 0.1875
Outputs:
- layer_out: bfloat16 [16384, 2048], P(('ep', 'dp'))
- grad_input: bfloat16 [16384, 2048], P(('ep', 'dp'))
- grad_gates: float32 [16384, 2], P(('ep', 'dp'))
- grad_w_gate: float32 [8, 2048, 1024], P('ep', 'dp')
- grad_w_up: float32 [8, 2048, 1024], P('ep', 'dp')
- grad_w_down: float32 [8, 2048, 1024], P('ep', 'dp')
Inputs may be any that keep to these rules, and one draw needn't show every extreme that they name: `routes`: among the 128 rows of one device, no expert is named by more than 64 rows, and in every draw some expert is named by exactly 64 of them; a token names 2 different experts.
All inputs are finite; a program needn't handle non-finite values.
Results may differ from a plain program's by a relative error of at most 0.022.
Values may be sent and summed in bfloat16 or wider, within the bound.
No kernel may reach another device: no remote copies, remote signals or barrier semaphores. Data moves between devices by JAX's collectives and lax.ppermute only.
A program may use at most 128 MiB of HBM per device.

v0:
```python
import jax
import jax.numpy as jnp
from jax import lax
from jax.sharding import PartitionSpec as P


def shards(checkpoint, cotangent, routes, gates, w_gate, w_up, w_down):
    tok_rows = cotangent.shape[0]
    features = cotangent.shape[1]
    top_count = routes.shape[1]
    local_experts = w_gate.shape[0]
    hidden_units = w_gate.shape[2]
    ep_size = lax.axis_size("ep")
    experts_all = local_experts * ep_size
    capacity = tok_rows * top_count * 2 // experts_all
    pair_count = tok_rows * top_count
    gathered = lax.all_gather(checkpoint, "dp", axis=1, tiled=True)
    inputs = lax.dynamic_slice_in_dim(gathered, lax.axis_index("dp") * tok_rows, tok_rows, 0)
    flat_routes = routes.reshape(-1)
    one_hot = (flat_routes[:, None] == jnp.arange(experts_all, dtype=jnp.int32)[None, :]).astype(
        jnp.int32
    )
    slot_index = jnp.sum(jnp.cumsum(one_hot, axis=0) * one_hot, axis=1) - 1
    position = flat_routes * capacity + slot_index
    source = jnp.full((experts_all * capacity,), pair_count, jnp.int32)
    source = source.at[position].set(jnp.arange(pair_count, dtype=jnp.int32))
    token_index = jnp.minimum(source // top_count, tok_rows)
    x_padded = jnp.concatenate([inputs, jnp.zeros((1, features), jnp.bfloat16)], axis=0)
    grad_out = (gates[:, :, None] * cotangent[:, None, :].astype(jnp.float32)).astype(jnp.bfloat16)
    grad_padded = jnp.concatenate(
        [grad_out.reshape(pair_count, features), jnp.zeros((1, features), jnp.bfloat16)], axis=0
    )
    x_send = x_padded[token_index].reshape(ep_size, local_experts, capacity, features)
    d_send = grad_padded[source].reshape(ep_size, local_experts, capacity, features)
    expert_x_rows = lax.all_to_all(x_send, "ep", split_axis=0, concat_axis=0, tiled=True)
    expert_d_rows = lax.all_to_all(d_send, "ep", split_axis=0, concat_axis=0, tiled=True)
    pre_gate = jnp.einsum(
        "sxnd,xdf->sxnf", expert_x_rows, w_gate, preferred_element_type=jnp.float32
    )
    pre_up = jnp.einsum("sxnd,xdf->sxnf", expert_x_rows, w_up, preferred_element_type=jnp.float32)
    activated = jax.nn.silu(pre_gate)
    expert_hidden = (activated * pre_up).astype(jnp.bfloat16)
    outputs = jnp.einsum(
        "sxnf,xdf->sxnd", expert_hidden, w_down, preferred_element_type=jnp.float32
    ).astype(jnp.bfloat16)
    hidden_grad = jnp.einsum(
        "sxnd,xdf->sxnf", expert_d_rows, w_down, preferred_element_type=jnp.float32
    )
    sigmoid_gate = jax.nn.sigmoid(pre_gate)
    expert_gate_grad = (
        hidden_grad * pre_up * sigmoid_gate * (1.0 + pre_gate * (1.0 - sigmoid_gate))
    ).astype(jnp.bfloat16)
    expert_up_grad = (hidden_grad * activated).astype(jnp.bfloat16)
    input_part = (
        jnp.einsum("sxnf,xdf->sxnd", expert_gate_grad, w_gate, preferred_element_type=jnp.float32)
        + jnp.einsum("sxnf,xdf->sxnd", expert_up_grad, w_up, preferred_element_type=jnp.float32)
    ).astype(jnp.bfloat16)
    outputs, input_part, hidden, gate_grad, up_grad, x_rows, d_rows = (
        outputs,
        input_part,
        expert_hidden,
        expert_gate_grad,
        expert_up_grad,
        expert_x_rows,
        expert_d_rows,
    )
    returned_out, returned_part = (
        lax.all_to_all(outputs, "ep", split_axis=0, concat_axis=0, tiled=True),
        lax.all_to_all(input_part, "ep", split_axis=0, concat_axis=0, tiled=True),
    )

    def term_of(left, right):
        return jnp.einsum("sxnd,sxnf->dxf", left, right, preferred_element_type=jnp.float32)

    summed = lax.psum_scatter(
        jnp.concatenate(
            [term_of(x_rows, gate_grad), term_of(x_rows, up_grad), term_of(d_rows, hidden)], axis=2
        ).astype(jnp.bfloat16),
        "dp",
        scatter_dimension=0,
        tiled=True,
    ).astype(jnp.float32)
    summed = jnp.transpose(summed, (1, 0, 2))
    grad_w_gate = summed[:, :, :hidden_units]
    grad_w_up = summed[:, :, hidden_units : 2 * hidden_units]
    grad_w_down = summed[:, :, 2 * hidden_units :]
    out_flat = returned_out.reshape(experts_all * capacity, features)
    part_flat = returned_part.reshape(experts_all * capacity, features)
    expert_out = out_flat[position].reshape(tok_rows, top_count, features).astype(jnp.float32)
    input_parts = part_flat[position].reshape(tok_rows, top_count, features).astype(jnp.float32)
    layer_out = jnp.sum(gates[:, :, None] * expert_out, axis=1).astype(jnp.bfloat16)
    grad_gates = jnp.sum(cotangent.astype(jnp.float32)[:, None, :] * expert_out, axis=-1)
    grad_input = jnp.sum(input_parts, axis=1).astype(jnp.bfloat16)
    return (layer_out, grad_input, grad_gates, grad_w_gate, grad_w_up, grad_w_down)


def solution(mesh):
    in_specs = (
        P("ep", "dp"),
        P(("ep", "dp"), None),
        P(("ep", "dp"), None),
        P(("ep", "dp"), None),
        P("ep", None, None),
        P("ep", None, None),
        P("ep", None, None),
    )
    out_specs = (
        P(("ep", "dp"), None),
        P(("ep", "dp"), None),
        P(("ep", "dp"), None),
        P("ep", "dp", None),
        P("ep", "dp", None),
        P("ep", "dp", None),
    )
    return jax.shard_map(shards, mesh=mesh, in_specs=in_specs, out_specs=out_specs, check_vma=False)
```

profile of v0, /device:TPU:1, one launch (start us, length us, event | category | flops | bytes accessed | tf_op | source)
XLA Modules:
  0.0 357.7 jit_solution(11015078676232284038)
XLA Ops:
  9.0 2.1 mul.91
  11.1 2.4 mul.92
  14.9 1.8 multiply_convert_fusion
  16.9 1.4 scatter_custom_fusion
  18.3 3.3 gather_fusion.2
  21.6 8.3 %all-to-all-start.2 = ((bf16[8,1,64,2048]{3,2,1,0:T(8,128)(2,1)}), bf16[8,1,64,2048]{3,2,1,0:T(8,128)(2,1)S(1)}, u32[]{:S(2)}, u32[]{:S(2)}) async-start(bf16[8,1,64,2048]{3,2,1,0:T(8,128)(2,1)} %bitcast.28), calls=%async_computation.2 | async-start | bytes 4194304 | tf_op jit(solution)/shard_map/all_to_all | solution.py:36
  30.0 65.2 %all-gather.2.cloned.1.call-done = bf16[2048,2048]{1,0:T(8,128)(2,1)} async-done(((bf16[2048,128]{1,0:T(8,128)(2,1)}), bf16[2048,2048]{1,0:T(8,128)(2,1)}) %all-gather.2.cloned.1.call-update) | async-done | bytes 8388624 | tf_op jit(solution)/shard_map/all_gather | solution.py:17
  96.3 3.3 gather_fusion
  99.6 6.3 %all-to-all-start = ((bf16[8,1,64,2048]{3,2,1,0:T(8,128)(2,1)}), bf16[8,1,64,2048]{3,2,1,0:T(8,128)(2,1)}, u32[]{:S(2)}, u32[]{:S(2)}) async-start(bf16[8,1,64,2048]{3,2,1,0:T(8,128)(2,1)} %bitcast.5), calls=%async_computation | async-start | bytes 4194304 | tf_op jit(solution)/shard_map/all_to_all | solution.py:35
  106.4 5.8 %fusion = f32[8,64,1024]{2,1,0:T(8,128)} fusion(bf16[1,2048,1024]{2,1,0:T(8,128)(2,1)} %param.13, bf16[8,1,64,2048]{3,2,1,0:T(8,128)(2,1)S(1)} %all-to-all-done.2), kind=kOutput, calls=%fused_computation.9 | convolution fusion | flops 2147483648 | bytes 8388608 | tf_op jit(solution)/shard_map/sxnd,xdf->sxnf/dot_general | solution.py:46
  112.2 24.7 %all-to-all-done = bf16[8,1,64,2048]{3,2,1,0:T(8,128)(2,1)} async-done(((bf16[8,1,64,2048]{3,2,1,0:T(8,128)(2,1)}), bf16[8,1,64,2048]{3,2,1,0:T(8,128)(2,1)}, u32[]{:S(2)}, u32[]{:S(2)}) %all-to-all-start) | async-done | bytes 2097184 | tf_op jit(solution)/shard_map/all_to_all | solution.py:35
  137.0 5.3 %fusion.6 = f32[8,64,1024]{2,1,0:T(8,128)S(1)} fusion(bf16[1,2048,1024]{2,1,0:T(8,128)(2,1)} %param.12, bf16[8,1,64,2048]{3,2,1,0:T(8,128)(2,1)} %all-to-all-done), kind=kOutput, calls=%fused_computation.15 | convolution fusion | flops 2147483648 | bytes 8388608 | tf_op jit(solution)/shard_map/sxnd,xdf->sxnf/dot_general | solution.py:40
  142.3 4.8 %fusion.28 = (bf16[8,1,64,1024]{3,2,0,1:T(8,128)(2,1)S(1)}, bf16[8,64,1024]{2,1,0:T(8,128)(2,1)S(1)}, bf16[8,64,1024]{2,1,0:T(8,128)(2,1)S(1)}) fusion(f32[8,64,1024]{2,1,0:T(8,128)S(1)} %copy-done.8, f32[8,64,1024]{2,1,0:T(8,128)S(1)} %fusion.6, bf16[1,2048,1024]{2,1,0:T(8,128)(2,1)S(1)} %copy-done.4, bf16[8,1,64,2048]{3,2,1,0:T(8,128)(2,1)} %all-to-all-done), kind=kOutput, calls=%fused_computation.32 | convolution fusion | flops 2155347968 | bytes 13631488 | tf_op jit(solution)/shard_map/sxnd,xdf->sxnf/dot_general | solution.py:37
  147.1 2.4 fusion.14
  149.5 4.0 %fusion.13 = bf16[2048,1,1024]{0,2,1:T(8,128)(2,1)S(1)} fusion(bf16[8,64,1024]{2,1,0:T(8,128)(2,1)S(1)} %get-tuple-element.28, bf16[8,1,64,2048]{3,2,1,0:T(8,128)(2,1)} %all-to-all-done), kind=kOutput, calls=%fused_computation.23 | convolution fusion | flops 2149580800 | bytes 7340032 | tf_op jit(solution)/shard_map/sxnd,sxnf->dxf/dot_general | solution.py:73
  153.5 4.2 %fusion.12 = bf16[2048,1,1024]{0,2,1:T(8,128)(2,1)S(1)} fusion(bf16[8,1,64,2048]{3,2,1,0:T(8,128)(2,1)} %all-to-all-done, bf16[8,1,64,1024]{3,2,0,1:T(8,128)(2,1)S(1)} %get-tuple-element.26), kind=kOutput, calls=%fused_computation.22 | convolution fusion | flops 2149580800 | bytes 7340032 | tf_op jit(solution)/shard_map/sxnd,sxnf->dxf/dot_general | solution.py:73
  157.7 21.0 %maximum_bitcast_fusion = bf16[2048,3072]{0,1:T(8,128)(2,1)} fusion(bf16[2048,1,1024]{0,2,1:T(8,128)(2,1)S(1)} %fusion.14, bf16[2048,1,1024]{0,2,1:T(8,128)(2,1)S(1)} %fusion.13, bf16[2048,1,1024]{0,2,1:T(8,128)(2,1)S(1)} %fusion.12), kind=kLoop, calls=%fused_computation.5 | loop fusion | flops 37748736 | bytes 25165824
  178.7 16.6 %copy.40 = bf16[2048,3072]{1,0:T(8,128)(2,1)} copy(bf16[2048,3072]{0,1:T(8,128)(2,1)} %maximum_bitcast_fusion) | data formatting | bytes 25165824
  196.6 5.9 %fusion.23 = bf16[8,1,64,2048]{3,2,1,0:T(8,128)(2,1)} fusion(bf16[8,64,1024]{2,1,0:T(8,128)(2,1)S(1)} %copy-done.11, bf16[1,2048,1024]{2,1,0:T(8,128)(2,1)} %param.13), kind=kOutput, calls=%fused_computation.27 | convolution fusion | flops 2148532224 | bytes 7340032 | tf_op jit(solution)/shard_map/sxnf,xdf->sxnd/dot_general | solution.py:43
  202.5 3.6 %all-to-all-start.1 = ((bf16[8,1,64,2048]{3,2,1,0:T(8,128)(2,1)}), bf16[8,1,64,2048]{3,2,1,0:T(8,128)(2,1)S(1)}, u32[]{:S(2)}, u32[]{:S(2)}) async-start(bf16[8,1,64,2048]{3,2,1,0:T(8,128)(2,1)} %fusion.23), calls=%async_computation.1 | async-start | bytes 4194304 | tf_op jit(solution)/shard_map/all_to_all | solution.py:68
  206.1 5.1 %fusion.4 = f32[8,64,2048]{2,1,0:T(8,128)S(1)} fusion(bf16[8,64,1024]{2,1,0:T(8,128)(2,1)} %copy-done.9, bf16[1,2048,1024]{2,1,0:T(8,128)(2,1)} %param.12), kind=kOutput, calls=%fused_computation.13 | convolution fusion | flops 2147483648 | bytes 9437184 | tf_op jit(solution)/shard_map/sxnf,xdf->sxnd/dot_general | solution.py:56
  211.2 3.7 %fusion.20 = bf16[8,1,64,2048]{3,2,1,0:T(8,128)(2,1)} fusion(f32[8,64,2048]{2,1,0:T(8,128)S(1)} %fusion.4, bf16[1,2048,1024]{2,1,0:T(8,128)(2,1)S(1)} %copy-done.5, bf16[8,1,64,1024]{3,2,0,1:T(8,128)(2,1)S(1)} %copy-done.7), kind=kOutput, calls=%fused_computation.26 | convolution fusion | flops 2149580800 | bytes 11534336 | tf_op jit(solution)/shard_map/sxnf,xdf->sxnd/dot_general | solution.py:55
  214.9 79.5 %all-to-all-done.1 = bf16[8,1,64,2048]{3,2,1,0:T(8,128)(2,1)S(1)} async-done(((bf16[8,1,64,2048]{3,2,1,0:T(8,128)(2,1)}), bf16[8,1,64,2048]{3,2,1,0:T(8,128)(2,1)S(1)}, u32[]{:S(2)}, u32[]{:S(2)}) %all-to-all-start.1) | async-done | bytes 2097184 | tf_op jit(solution)/shard_map/all_to_all | solution.py:68
  294.4 4.6 %all-to-all-start.3 = ((bf16[8,1,64,2048]{3,2,1,0:T(8,128)(2,1)}), bf16[8,1,64,2048]{3,2,1,0:T(8,128)(2,1)}, u32[]{:S(2)}, u32[]{:S(2)}) async-start(bf16[8,1,64,2048]{3,2,1,0:T(8,128)(2,1)} %fusion.20), calls=%async_computation.3 | async-start | bytes 4194304 | tf_op jit(solution)/shard_map/all_to_all | solution.py:69
  300.0 1.4 gather_fusion.1
  301.4 1.3 reshape.201
  302.8 27.2 %all-to-all-done.3 = bf16[8,1,64,2048]{3,2,1,0:T(8,128)(2,1)} async-done(((bf16[8,1,64,2048]{3,2,1,0:T(8,128)(2,1)}), bf16[8,1,64,2048]{3,2,1,0:T(8,128)(2,1)}, u32[]{:S(2)}, u32[]{:S(2)}) %all-to-all-start.3) | async-done | bytes 2097184 | tf_op jit(solution)/shard_map/all_to_all | solution.py:69
  330.0 4.2 %gather_fusion.3 = bf16[256,2048]{1,0:T(8,128)(2,1)S(1)} fusion(bf16[512,2048]{1,0:T(8,128)(2,1)} %bitcast.43, s32[1024]{0:T(1024)S(1)} %pad_clamp_fusion.1), kind=kCustom, calls=%fused_computation.3 | custom fusion | bytes 2098176 | tf_op jit(solution)/shard_map/gather | solution.py:90
  334.2 1.5 reshape.200
  335.8 4.6 %reduce_sum.41 = bf16[128,2048]{1,0:T(8,128)(2,1)} reduce(bf16[128,2,2048]{2,1,0:T(2,128)(2,1)} %reshape.200, bf16[]{:T(256)} %constant.20.clone.1), dimensions={1}, to_apply=%region_5.6 | reduce | flops 262144 | bytes 1572866 | tf_op jit(solution)/shard_map/reduce_sum | solution.py:93
  340.4 4.9 %multiply_reduce_fusion = (f32[128,2]{1,0:T(8,128)S(1)}, bf16[128,2048]{1,0:T(8,128)(2,1)}) fusion(f32[128,2,2048]{2,1,0:T(2,128)S(1)} %reshape.201, f32[128,2048]{1,0:T(8,128)S(1)} %copy-done, f32[128,2]{1,0:T(8,128)S(1)} %copy.25), kind=kLoop, calls=%fused_computation.49 | loop fusion | flops 1834752 | bytes 3672064 | tf_op jit(solution)/shard_map/reduce_sum | solution.py:92
  346.0 1.5 copy.41
  (61 shorter events, 11.2 us)
Async XLA Ops:
  7.2 88.0 %all-gather.2.cloned.1.call-start = ((), (), s32[]{:S(2)}) async-start(), calls=%async_computation.5 | async-start | bytes 8912896 | tf_op jit(solution)/shard_map/all_gather | solution.py:17
  11.1 2.4 copy-start.3
  11.1 2.7 copy-start.2
  21.6 78.0 %all-to-all-start.2 = ((bf16[8,1,64,2048]{3,2,1,0:T(8,128)(2,1)}), bf16[8,1,64,2048]{3,2,1,0:T(8,128)(2,1)S(1)}, u32[]{:S(2)}, u32[]{:S(2)}) async-start(bf16[8,1,64,2048]{3,2,1,0:T(8,128)(2,1)} %bitcast.28), calls=%async_computation.2 | async-start | bytes 4194304 | tf_op jit(solution)/shard_map/all_to_all | solution.py:36
  99.6 37.4 %all-to-all-start = ((bf16[8,1,64,2048]{3,2,1,0:T(8,128)(2,1)}), bf16[8,1,64,2048]{3,2,1,0:T(8,128)(2,1)}, u32[]{:S(2)}, u32[]{:S(2)}) async-start(bf16[8,1,64,2048]{3,2,1,0:T(8,128)(2,1)} %bitcast.5), calls=%async_computation | async-start | bytes 4194304 | tf_op jit(solution)/shard_map/all_to_all | solution.py:35
  105.9 240.1 %reduce-scatter.4.cloned.1.call-start = ((), (), s32[]{:S(2)}) async-start(), calls=%async_computation.6 | async-start | bytes 13369344
  137.0 5.3 %copy-start.4 = (bf16[1,2048,1024]{2,1,0:T(8,128)(2,1)S(1)}, bf16[1,2048,1024]{2,1,0:T(8,128)(2,1)}, u32[]{:S(2)}) copy-start(bf16[1,2048,1024]{2,1,0:T(8,128)(2,1)} %param.11) | copy-start | bytes 12582916
  137.0 5.3 %copy-start.8 = (f32[8,64,1024]{2,1,0:T(8,128)S(1)}, f32[8,64,1024]{2,1,0:T(8,128)}, u32[]{:S(2)}) copy-start(f32[8,64,1024]{2,1,0:T(8,128)} %fusion) | copy-start | bytes 6291460
  147.1 2.4 copy-start.10
  147.1 2.4 copy-start.9
  147.1 6.4 %copy-start.6 = (bf16[8,1,64,1024]{3,2,0,1:T(8,128)(2,1)}, bf16[8,1,64,1024]{3,2,0,1:T(8,128)(2,1)S(1)}, u32[]{:S(2)}) copy-start(bf16[8,1,64,1024]{3,2,0,1:T(8,128)(2,1)S(1)} %get-tuple-element.26) | copy-start | bytes 3145732
  195.3 1.2 copy-start.11
  202.5 91.9 %all-to-all-start.1 = ((bf16[8,1,64,2048]{3,2,1,0:T(8,128)(2,1)}), bf16[8,1,64,2048]{3,2,1,0:T(8,128)(2,1)S(1)}, u32[]{:S(2)}, u32[]{:S(2)}) async-start(bf16[8,1,64,2048]{3,2,1,0:T(8,128)(2,1)} %fusion.23), calls=%async_computation.1 | async-start | bytes 4194304 | tf_op jit(solution)/shard_map/all_to_all | solution.py:68
  206.1 5.1 %copy-start.5 = (bf16[1,2048,1024]{2,1,0:T(8,128)(2,1)S(1)}, bf16[1,2048,1024]{2,1,0:T(8,128)(2,1)}, u32[]{:S(2)}) copy-start(bf16[1,2048,1024]{2,1,0:T(8,128)(2,1)} %param.11) | copy-start | bytes 12582916
  206.1 5.1 %copy-start.7 = (bf16[8,1,64,1024]{3,2,0,1:T(8,128)(2,1)S(1)}, bf16[8,1,64,1024]{3,2,0,1:T(8,128)(2,1)}, u32[]{:S(2)}) copy-start(bf16[8,1,64,1024]{3,2,0,1:T(8,128)(2,1)} %copy-done.6) | copy-start | bytes 3145732
  214.9 84.1 %copy-start.1 = (bf16[128,2048]{1,0:T(8,128)(2,1)S(1)}, bf16[128,2048]{1,0:T(8,128)(2,1)}, u32[]{:S(2)}) copy-start(bf16[128,2048]{1,0:T(8,128)(2,1)} %param.8) | copy-start | bytes 1572868
  294.4 35.6 %all-to-all-start.3 = ((bf16[8,1,64,2048]{3,2,1,0:T(8,128)(2,1)}), bf16[8,1,64,2048]{3,2,1,0:T(8,128)(2,1)}, u32[]{:S(2)}, u32[]{:S(2)}) async-start(bf16[8,1,64,2048]{3,2,1,0:T(8,128)(2,1)} %fusion.20), calls=%async_computation.3 | async-start | bytes 4194304 | tf_op jit(solution)/shard_map/all_to_all | solution.py:69
  335.8 4.6 %copy-start = (f32[128,2048]{1,0:T(8,128)S(1)}, f32[128,2048]{1,0:T(8,128)}, u32[]{:S(2)}) copy-start(f32[128,2048]{1,0:T(8,128)} %convert_element_type.81) | copy-start | bytes 3145732
Sparse Core Ops, SparseCore 0:
  9.6 85.4 all-gather.1
  195.5 93.7 reduce-scatter.3
where the time goes:
time: 363 us; the launch traced here: 358 us
  waiting for transfers between devices  197 us (54%)
  local copies, waits for them, and re-layouts  47 us (13%)
  matrix products  41.1 us (11%)
  other arithmetic  34.3 us (9%)
  starting transfers between devices  23.3 us (6%)
  between operations  14.6 us (4%)
    all_to_all x1, waiting for transfers between devices, shards(): lax.all_to_all(outputs, 'ep', split_axis=0, concat_axis=0, tiled=True)  79.5 us
    all_gather x1, waiting for transfers between devices, shards(): gathered = lax.all_gather(checkpoint, 'dp', axis=1, tiled=True)  65.2 us
    all_to_all x1, waiting for transfers between devices, shards(): lax.all_to_all(input_part, 'ep', split_axis=0, concat_axis=0, tiled=True)  27.2 us
    all_to_all x1, waiting for transfers between devices, shards(): lax.all_to_all(x_send, 'ep', split_axis=0, concat_axis=0, tiled=True)  24.7 us
    unnamed x32, local copies, waits for them, and re-layouts  23.9 us
    unnamed x1, other arithmetic  21 us
    dot_general x3, matrix products, term_of(): jnp.einsum('sxnd,sxnf->dxf', left, right, preferred_element_type=jnp.floa...  10.5 us
    all_to_all x1, starting transfers between devices, shards(): lax.all_to_all(d_send, 'ep', split_axis=0, concat_axis=0, tiled=True)  8.33 us
  transfers between devices with their start and end apart: 6, of which 4 were waited for; matrix products, arithmetic and copies ran while one was open for 16% of the time, Pallas kernels for 0%

commit v1 on v0

v1 whole, which is shorter than its diff:
```python
import functools

import jax
import jax.numpy as jnp
from jax import lax
from jax.experimental import pallas as pl
from jax.experimental.pallas import tpu as pltpu
from jax.sharding import PartitionSpec as P

F32 = jnp.float32
BF16 = jnp.bfloat16
NT = (((1,), (1,)), ((), ()))
TN = (((0,), (0,)), ((), ()))
NN = (((1,), (0,)), ((), ()))
MIB = 1 << 20


def dot(a, b, dims=NN):
    return lax.dot_general(a, b, dims, preferred_element_type=F32)


def call(body, grid, in_specs, out_specs, out_shape, flops, moved, vmem=32):
    return pl.pallas_call(
        body,
        grid=grid,
        in_specs=in_specs,
        out_specs=out_specs,
        out_shape=out_shape,
        cost_estimate=pl.CostEstimate(flops=flops, bytes_accessed=moved, transcendentals=0),
        compiler_params=pltpu.CompilerParams(vmem_limit_bytes=vmem * MIB),
    )


def places(routes_ref, experts):
    tokens = routes_ref.shape[1]
    expert = lax.broadcasted_iota(jnp.int32, (experts, tokens), 0)
    first = (routes_ref[0:1, :] == expert).astype(F32)
    second = (routes_ref[1:2, :] == expert).astype(F32)
    chosen = first + second
    row = lax.broadcasted_iota(jnp.int32, (tokens, tokens), 0)
    col = lax.broadcasted_iota(jnp.int32, (tokens, tokens), 1)
    before = (row < col).astype(BF16)
    slot = dot(chosen.astype(BF16), before)
    return first, second, chosen, slot


def pick(mask, slot, e, cap):
    tokens = slot.shape[1]
    index = lax.broadcasted_iota(jnp.int32, (cap, tokens), 0).astype(F32)
    return jnp.where(index == slot[e : e + 1, :], mask[e : e + 1, :], 0.0)


def pack_kernel(experts, cap, scaled, routes_ref, gates_ref, rows_ref, out_ref):
    first, second, chosen, slot = places(routes_ref, experts)
    rows = rows_ref[...]
    weight = gates_ref[0:1, :] * first + gates_ref[1:2, :] * second
    for e in range(experts):
        sel = pick(chosen, slot, e, cap)
        picked = dot(sel.astype(BF16), rows)
        if scaled:
            picked = picked * jnp.sum(sel * weight[e : e + 1, :], axis=1, keepdims=True)
        out_ref[e * cap : (e + 1) * cap, :] = picked.astype(BF16)


def pack(routes, gates, rows, experts, cap, scaled):
    tokens, features = rows.shape
    whole = pl.BlockSpec(memory_space=pltpu.VMEM)
    return call(
        functools.partial(pack_kernel, experts, cap, scaled),
        (),
        [whole] * 3,
        whole,
        jax.ShapeDtypeStruct((experts * cap, features), BF16),
        2 * experts * cap * tokens * features,
        (experts * cap + tokens) * features * 2,
    )(routes, gates, rows)


def gather_sel(mask, slot, cap):
    experts = slot.shape[0]
    return jnp.concatenate([pick(mask, slot, e, cap) for e in range(experts)], axis=0)


def out_kernel(experts, cap, routes_ref, gates_ref, cot_ref, rows_ref, out_ref, grad_ref):
    first, second, _, slot = places(routes_ref, experts)
    rows = rows_ref[...]
    cot = cot_ref[...].astype(F32)
    gates = gates_ref[...]
    total = None
    columns = []
    for k, mask in enumerate((first, second)):
        sel = gather_sel(mask, slot, cap).astype(BF16)
        mine = dot(sel, rows, TN)
        columns.append(jnp.sum(cot * mine, axis=1, keepdims=True))
        term = gates[:, k : k + 1] * mine
        total = term if total is None else total + term
    out_ref[...] = total.astype(BF16)
    grad_ref[...] = jnp.concatenate(columns, axis=1)


def part_kernel(experts, cap, routes_ref, rows_ref, out_ref):
    _, _, chosen, slot = places(routes_ref, experts)
    sel = gather_sel(chosen, slot, cap).astype(BF16)
    out_ref[...] = dot(sel, rows_ref[...], TN).astype(BF16)


def hidden_grad_kernel(d_ref, w_ref, out_ref):
    out_ref[...] = dot(d_ref[...], w_ref[...])


def hidden_kernel(x_ref, wg_ref, wu_ref, hg_ref, h_ref, gg_ref, ug_ref):
    x = x_ref[...]
    pre_gate = dot(x, wg_ref[...])
    pre_up = dot(x, wu_ref[...])
    hidden_grad = hg_ref[...]
    s = 1.0 / (1.0 + jnp.exp(-pre_gate))
    silu = pre_gate * s
    h_ref[...] = (silu * pre_up).astype(BF16)
    gg_ref[...] = (hidden_grad * pre_up * s * (1.0 + pre_gate * (1.0 - s))).astype(BF16)
    ug_ref[...] = (hidden_grad * silu).astype(BF16)


def terms_kernel(ff, x_ref, d_ref, gg_ref, ug_ref, h_ref, out_ref):
    x = x_ref[...]
    d = d_ref[...]
    out_ref[:, 0:ff] = dot(x, gg_ref[...], TN).astype(BF16)
    out_ref[:, ff : 2 * ff] = dot(x, ug_ref[...], TN).astype(BF16)
    out_ref[:, 2 * ff : 3 * ff] = dot(d, h_ref[...], TN).astype(BF16)


def outputs_kernel(h_ref, w_ref, out_ref):
    out_ref[...] = dot(h_ref[...], w_ref[...], NT).astype(BF16)


def parts_kernel(gg_ref, ug_ref, wg_ref, wu_ref, out_ref):
    total = dot(gg_ref[...], wg_ref[...], NT) + dot(ug_ref[...], wu_ref[...], NT)
    out_ref[...] = total.astype(BF16)


def shards(checkpoint, cotangent, routes, gates, w_gate, w_up, w_down):
    tokens, features = cotangent.shape
    ep = lax.axis_size("ep")
    dp = lax.axis_size("dp")
    experts = ep * w_gate.shape[0]
    ff = w_gate.shape[2]
    cap = tokens * routes.shape[1] * 2 // experts
    rows = ep * cap
    block = 256
    whole = pl.BlockSpec(memory_space=pltpu.VMEM)
    w_gate, w_up, w_down = w_gate[0], w_up[0], w_down[0]
    routes_t = routes.T
    gates_t = gates.T
    mm = 2 * rows * features * ff

    slices = lax.all_to_all(
        checkpoint.reshape(dp, tokens, features // dp), "dp", split_axis=0, concat_axis=0, tiled=True
    )
    d_send = pack(routes_t, gates_t, cotangent, experts, cap, True)
    d_rows = lax.all_to_all(
        d_send.reshape(ep, cap, features), "ep", split_axis=0, concat_axis=0, tiled=True
    ).reshape(rows, features)
    inputs = jnp.transpose(slices, (1, 0, 2)).reshape(tokens, features)
    x_send = pack(routes_t, gates_t, inputs, experts, cap, False)
    x_rows = lax.all_to_all(
        x_send.reshape(ep, cap, features), "ep", split_axis=0, concat_axis=0, tiled=True
    ).reshape(rows, features)

    full_rows = pl.BlockSpec((rows, features), lambda i: (0, 0))
    full_hidden = pl.BlockSpec((rows, ff), lambda i: (0, 0))
    w_cols = pl.BlockSpec((features, block), lambda i: (0, i))
    w_rows = pl.BlockSpec((block, ff), lambda i: (i, 0))
    r_cols = pl.BlockSpec((rows, block), lambda i: (0, i))

    hidden_grad = call(
        hidden_grad_kernel,
        (ff // block,),
        [full_rows, w_cols],
        r_cols,
        jax.ShapeDtypeStruct((rows, ff), F32),
        mm,
        10 * MIB,
    )(d_rows, w_down)
    hidden, gate_grad, up_grad = call(
        hidden_kernel,
        (ff // block,),
        [full_rows, w_cols, w_cols, r_cols],
        [r_cols] * 3,
        [jax.ShapeDtypeStruct((rows, ff), BF16)] * 3,
        2 * mm,
        16 * MIB,
    )(x_rows, w_gate, w_up, hidden_grad)
    terms = call(
        functools.partial(terms_kernel, ff),
        (features // block,),
        [r_cols, r_cols, full_hidden, full_hidden, full_hidden],
        pl.BlockSpec((block, 3 * ff), lambda i: (i, 0)),
        jax.ShapeDtypeStruct((features, 3 * ff), BF16),
        3 * mm,
        19 * MIB,
    )(x_rows, d_rows, gate_grad, up_grad, hidden)
    summed = lax.psum_scatter(terms, "dp", scatter_dimension=0, tiled=True)
    outputs = call(
        outputs_kernel,
        (features // block,),
        [full_hidden, w_rows],
        r_cols,
        jax.ShapeDtypeStruct((rows, features), BF16),
        mm,
        7 * MIB,
    )(hidden, w_down)
    returned_out = lax.all_to_all(
        outputs.reshape(ep, cap, features), "ep", split_axis=0, concat_axis=0, tiled=True
    ).reshape(rows, features)
    parts = call(
        parts_kernel,
        (features // block,),
        [full_hidden, full_hidden, w_rows, w_rows],
        r_cols,
        jax.ShapeDtypeStruct((rows, features), BF16),
        2 * mm,
        12 * MIB,
    )(gate_grad, up_grad, w_gate, w_up)
    returned_part = lax.all_to_all(
        parts.reshape(ep, cap, features), "ep", split_axis=0, concat_axis=0, tiled=True
    ).reshape(rows, features)
    layer_out, grad_gates = call(
        functools.partial(out_kernel, experts, cap),
        (),
        [whole] * 4,
        [whole] * 2,
        [
            jax.ShapeDtypeStruct((tokens, features), BF16),
            jax.ShapeDtypeStruct((tokens, 2), F32),
        ],
        4 * rows * tokens * features,
        3 * MIB,
    )(routes_t, gates, cotangent, returned_out)
    grad_input = call(
        functools.partial(part_kernel, experts, cap),
        (),
        [whole] * 2,
        whole,
        jax.ShapeDtypeStruct((tokens, features), BF16),
        2 * rows * tokens * features,
        3 * MIB,
    )(routes_t, returned_part)
    grads = [summed[None, :, i * ff : (i + 1) * ff].astype(F32) for i in range(3)]
    return (layer_out, grad_input, grad_gates, *grads)


def solution(mesh):
    tok = P(("ep", "dp"), None)
    weight = P("ep", None, None)
    grad = P("ep", "dp", None)
    return jax.shard_map(
        shards,
        mesh=mesh,
        in_specs=(P("ep", "dp"), tok, tok, tok, weight, weight, weight),
        out_specs=(tok, tok, tok, grad, grad, grad),
        check_vma=False,
    )
```

time: 363 us -> 275 us (0.76); the launches traced: 358 us -> 274 us
  matrix products: 41.1 us -> 0 us
  waiting for transfers between devices: 197 us -> 156 us
  Pallas kernels: 0 us -> 40.8 us
  other arithmetic: 34.3 us -> 2.3 us
  local copies, waits for them, and re-layouts: 47 us -> 33.2 us
  starting transfers between devices: 23.3 us -> 27 us
    all_gather x1 -> x0, waiting for transfers between devices: 65.2 us -> none  [shards(): gathered = lax.all_gather(checkpoint, 'dp', axis=1, tiled=True)]
    dot_general x9 -> x0, matrix products: 41.1 us -> none  [the longest x3 10.5 us: term_of(): jnp.einsum('sxnd,sxnf->dxf', left, right, preferred_element_type=jnp.floa...]
    pallas_call x0 -> x9, Pallas kernels: none -> 40.8 us  [the longest x1 9.31 us: shards(): call(functools.partial(terms_kernel, ff), (features // block,), [r_cols,...]
    all_to_all x4 -> x5, waiting for transfers between devices: 131 us -> 156 us  [the longest x1 72.9 us: shards(): lax.all_to_all(outputs.reshape(ep, cap, features), 'ep', split_axis=0, co...]
    unnamed x1 -> x0, other arithmetic: 21 us -> none
    gather x4 -> x0, local copies, waits for them, and re-layouts: 12.1 us -> none  [the longest x1 4.22 us: shards(): part_flat[position].reshape(tok_rows, top_count, features)]
    reduce_sum x3 -> x0, other arithmetic: 9.64 us -> none  [the longest x1 4.91 us: shards(): jnp.sum(cotangent.astype(jnp.float32)[:, None, :] * expert_out, axis=-1)]
    unnamed x32 -> x48, local copies, waits for them, and re-layouts: 23.9 us -> 33.2 us
  transfers between devices with their start and end apart: 6 -> 6, of which waited for: 4 -> 5; matrix products, arithmetic and copies ran while one was open for 16% -> 0% of each run, Pallas kernels for 0% -> 8%
where the time goes in v1:
time: 275 us; the launch traced here: 274 us
  waiting for transfers between devices  156 us (57%)
  Pallas kernels  40.8 us (15%)
  local copies, waits for them, and re-layouts  33.2 us (12%)
  starting transfers between devices  27 us (10%)
  between operations  14.2 us (5%)
    all_to_all x1, waiting for transfers between devices, shards(): lax.all_to_all(outputs.reshape(ep, cap, features), 'ep', split_axis=0, co...  72.9 us
    unnamed x48, local copies, waits for them, and re-layouts  33.2 us
    all_to_all x1, waiting for transfers between devices, shards(): lax.all_to_all(parts.reshape(ep, cap, features), 'ep', split_axis=0, conc...  28.4 us
    all_to_all x1, waiting for transfers between devices, shards(): lax.all_to_all(d_send.reshape(ep, cap, features), 'ep', split_axis=0, con...  27.7 us
    all_to_all x1, waiting for transfers between devices, shards(): lax.all_to_all(x_send.reshape(ep, cap, features), 'ep', split_axis=0, con...  22.1 us
    pallas_call x1, Pallas kernels, shards(): call(functools.partial(terms_kernel, ff), (features // block,), [r_cols,...  9.31 us
    pallas_call x1, Pallas kernels, shards(): call(hidden_kernel, (ff // block,), [full_rows, w_cols, w_cols, r_cols],...  8.56 us
    all_to_all x1, starting transfers between devices, shards(): lax.all_to_all(d_send.reshape(ep, cap, features), 'ep', split_axis=0, con...  7.34 us
  transfers between devices with their start and end apart: 6, of which 5 were waited for; matrix products, arithmetic and copies ran while one was open for 0% of the time, Pallas kernels for 8%

profile of v1, /device:TPU:1, one launch (start us, length us, event | category | flops | bytes accessed | tf_op | source)
XLA Modules:
  0.0 274.0 jit_solution(7605028195058190906)
XLA Ops:
  7.2 7.2 %all-to-all-start = ((bf16[16,128,128]{2,1,0:T(8,128)(2,1)}), bf16[16,128,128]{2,1,0:T(8,128)(2,1)S(1)}, u32[]{:S(2)}, u32[]{:S(2)}) async-start(bf16[16,128,128]{2,1,0:T(8,128)(2,1)} %bitcast.52), calls=%async_computation | async-start | bytes 1048576 | tf_op jit(solution)/shard_map/all_to_all | solution.py:155
  16.7 2.2 shard_map.119
  18.9 5.3 %all-to-all-done = bf16[16,128,128]{2,1,0:T(8,128)(2,1)S(1)} async-done(((bf16[16,128,128]{2,1,0:T(8,128)(2,1)}), bf16[16,128,128]{2,1,0:T(8,128)(2,1)S(1)}, u32[]{:S(2)}, u32[]{:S(2)}) %all-to-all-start) | async-done | bytes 524320 | tf_op jit(solution)/shard_map/all_to_all | solution.py:155
  24.2 7.3 %all-to-all-start.2 = ((bf16[8,64,2048]{2,1,0:T(8,128)(2,1)}), bf16[8,64,2048]{2,1,0:T(8,128)(2,1)S(1)}, u32[]{:S(2)}, u32[]{:S(2)}) async-start(bf16[8,64,2048]{2,1,0:T(8,128)(2,1)} %bitcast.8), calls=%async_computation.2 | async-start | bytes 4194304 | tf_op jit(solution)/shard_map/all_to_all | solution.py:159
  31.7 2.2 shard_map.118
  33.8 27.7 %all-to-all-done.2 = bf16[8,64,2048]{2,1,0:T(8,128)(2,1)S(1)} async-done(((bf16[8,64,2048]{2,1,0:T(8,128)(2,1)}), bf16[8,64,2048]{2,1,0:T(8,128)(2,1)S(1)}, u32[]{:S(2)}, u32[]{:S(2)}) %all-to-all-start.2) | async-done | bytes 2097184 | tf_op jit(solution)/shard_map/all_to_all | solution.py:159
  61.5 4.3 %all-to-all-start.1 = ((bf16[8,64,2048]{2,1,0:T(8,128)(2,1)}), bf16[8,64,2048]{2,1,0:T(8,128)(2,1)}, u32[]{:S(2)}, u32[]{:S(2)}) async-start(bf16[8,64,2048]{2,1,0:T(8,128)(2,1)} %bitcast.4), calls=%async_computation.1 | async-start | bytes 4194304 | tf_op jit(solution)/shard_map/all_to_all | solution.py:164
  65.9 2.2 copy-done.1
  68.1 3.6 %shard_map.120.hg_ref = f32[512,1024]{1,0:T(8,128)S(1)} custom-call(bf16[512,2048]{1,0:T(8,128)(2,1)S(1)} %bitcast.36, bf16[2048,1024]{1,0:T(8,128)(2,1)S(1)} %bitcast.38), custom_call_target="tpu_custom_call" | custom-call | flops 2147483648 | bytes 10485760 | tf_op jit(solution)/shard_map/pallas_call | solution.py:174
  71.7 1.4 copy-done.7
  73.1 22.1 %all-to-all-done.1 = bf16[8,64,2048]{2,1,0:T(8,128)(2,1)} async-done(((bf16[8,64,2048]{2,1,0:T(8,128)(2,1)}), bf16[8,64,2048]{2,1,0:T(8,128)(2,1)}, u32[]{:S(2)}, u32[]{:S(2)}) %all-to-all-start.1) | async-done | bytes 2097184 | tf_op jit(solution)/shard_map/all_to_all | solution.py:164
  95.2 1.6 copy-done.8
  96.8 2.2 copy-done.13
  99.0 2.2 copy-done.15
  101.2 8.6 %shard_map.121 = (bf16[512,1024]{1,0:T(8,128)(2,1)S(1)}, bf16[512,1024]{1,0:T(8,128)(2,1)S(1)}, bf16[512,1024]{1,0:T(8,128)(2,1)S(1)}) custom-call(bf16[512,2048]{1,0:T(8,128)(2,1)} %bitcast.5.x_ref, bf16[2048,1024]{1,0:T(8,128)(2,1)S(1)} %bitcast.48, bf16[2048,1024]{1,0:T(8,128)(2,1)S(1)} %bitcast.50, f32[512,1024]{1,0:T(8,128)S(1)} %copy-done.8), custom_call_target="tpu_custom_call" | custom-call | flops 4294967296 | bytes 16777216 | tf_op jit(solution)/shard_map/pallas_call | solution.py:183
  109.7 9.3 %shard_map.126 = bf16[2048,3072]{1,0:T(8,128)(2,1)S(1)} custom-call(bf16[512,2048]{1,0:T(8,128)(2,1)} %bitcast.5.x_ref, bf16[512,2048]{1,0:T(8,128)(2,1)S(1)} %bitcast.37, bf16[512,1024]{1,0:T(8,128)(2,1)S(1)} %get-tuple-element.13.gg_ref, bf16[512,1024]{1,0:T(8,128)(2,1)S(1)} %get-tuple-element.14.ug_ref, bf16[512,1024]{1,0:T(8,128)(2,1)S(1)} %get-tuple-element.11.h_ref), custom_call_target="tpu_custom_call" | custom-call | flops 6442450944 | bytes 19922944 | tf_op jit(solution)/shard_map/pallas_call | solution.py:192
  119.1 4.5 %copy-done = bf16[2048,3072]{1,0:T(8,128)(2,1)} copy-done((bf16[2048,3072]{1,0:T(8,128)(2,1)}, bf16[2048,3072]{1,0:T(8,128)(2,1)S(1)}, u32[]{:S(2)}) %copy-start) | copy-done | bytes 12582936
  127.8 2.2 copy-done.2
  129.9 4.0 %shard_map.122 = bf16[512,2048]{1,0:T(8,128)(2,1)S(1)} custom-call(bf16[512,1024]{1,0:T(8,128)(2,1)S(1)} %copy-done.18, bf16[2048,1024]{1,0:T(8,128)(2,1)S(1)} %bitcast.39), custom_call_target="tpu_custom_call" | custom-call | flops 2147483648 | bytes 7340032 | tf_op jit(solution)/shard_map/pallas_call | solution.py:202
  134.0 1.3 copy-done.4
  135.3 3.6 %all-to-all-start.3 = ((bf16[8,64,2048]{2,1,0:T(8,128)(2,1)}), bf16[8,64,2048]{2,1,0:T(8,128)(2,1)S(1)}, u32[]{:S(2)}, u32[]{:S(2)}) async-start(bf16[8,64,2048]{2,1,0:T(8,128)(2,1)} %bitcast.41), calls=%async_computation.3 | async-start | bytes 4194304 | tf_op jit(solution)/shard_map/all_to_all | solution.py:211
  138.9 2.2 copy-done.14
  141.2 2.3 copy-done.16
  143.4 1.3 copy-done.20
  145.9 6.2 %shard_map.124 = bf16[512,2048]{1,0:T(8,128)(2,1)S(1)} custom-call(bf16[512,1024]{1,0:T(8,128)(2,1)S(1)} %copy-done.20, bf16[512,1024]{1,0:T(8,128)(2,1)S(1)} %copy-done.22, bf16[2048,1024]{1,0:T(8,128)(2,1)S(1)} %bitcast.49, bf16[2048,1024]{1,0:T(8,128)(2,1)S(1)} %bitcast.51), custom_call_target="tpu_custom_call" | custom-call | flops 4294967296 | bytes 12582912 | tf_op jit(solution)/shard_map/pallas_call | solution.py:214
  152.1 1.3 copy-done.3
  153.4 72.9 %all-to-all-done.3 = bf16[8,64,2048]{2,1,0:T(8,128)(2,1)S(1)} async-done(((bf16[8,64,2048]{2,1,0:T(8,128)(2,1)}), bf16[8,64,2048]{2,1,0:T(8,128)(2,1)S(1)}, u32[]{:S(2)}, u32[]{:S(2)}) %all-to-all-start.3) | async-done | bytes 2097184 | tf_op jit(solution)/shard_map/all_to_all | solution.py:211
  226.3 4.5 %all-to-all-start.4 = ((bf16[8,64,2048]{2,1,0:T(8,128)(2,1)}), bf16[8,64,2048]{2,1,0:T(8,128)(2,1)}, u32[]{:S(2)}, u32[]{:S(2)}) async-start(bf16[8,64,2048]{2,1,0:T(8,128)(2,1)} %bitcast.40), calls=%async_computation.4 | async-start | bytes 4194304 | tf_op jit(solution)/shard_map/all_to_all | solution.py:223
  230.9 1.8 shard_map.123
  233.4 28.4 %all-to-all-done.4 = bf16[8,64,2048]{2,1,0:T(8,128)(2,1)} async-done(((bf16[8,64,2048]{2,1,0:T(8,128)(2,1)}), bf16[8,64,2048]{2,1,0:T(8,128)(2,1)}, u32[]{:S(2)}, u32[]{:S(2)}) %all-to-all-start.4) | async-done | bytes 2097184 | tf_op jit(solution)/shard_map/all_to_all | solution.py:223
  261.9 3.0 %shard_map.125 = bf16[128,2048]{1,0:T(8,128)(2,1)} custom-call(s32[2,128]{1,0:T(2,128)S(1)} %bitcast.45, bf16[512,2048]{1,0:T(8,128)(2,1)} %bitcast.14.rows_ref), custom_call_target="tpu_custom_call" | custom-call | flops 268435456 | bytes 3145728 | tf_op jit(solution)/shard_map/pallas_call | solution.py:238
  264.9 2.3 fusion
  (40 shorter events, 8.7 us)
Async XLA Ops:
  7.2 17.1 %all-to-all-start = ((bf16[16,128,128]{2,1,0:T(8,128)(2,1)}), bf16[16,128,128]{2,1,0:T(8,128)(2,1)S(1)}, u32[]{:S(2)}, u32[]{:S(2)}) async-start(bf16[16,128,128]{2,1,0:T(8,128)(2,1)} %bitcast.52), calls=%async_computation | async-start | bytes 1048576 | tf_op jit(solution)/shard_map/all_to_all | solution.py:155
  14.3 1.0 copy-start.5
  15.4 0.7 copy-start.9
  16.1 0.7 copy-start.11
  24.2 7.4 %copy-start.10 = (s32[128,2]{0,1:T(2,128)S(1)}, s32[128,2]{0,1:T(2,128)}, u32[]{:S(2)}) copy-start(s32[128,2]{0,1:T(2,128)} %param.9) | copy-start | bytes 3076
  24.2 7.4 %copy-start.12 = (f32[128,2]{0,1:T(2,128)S(1)}, f32[128,2]{0,1:T(2,128)}, u32[]{:S(2)}) copy-start(f32[128,2]{0,1:T(2,128)} %param.10) | copy-start | bytes 3076
  24.2 37.3 %all-to-all-start.2 = ((bf16[8,64,2048]{2,1,0:T(8,128)(2,1)}), bf16[8,64,2048]{2,1,0:T(8,128)(2,1)S(1)}, u32[]{:S(2)}, u32[]{:S(2)}) async-start(bf16[8,64,2048]{2,1,0:T(8,128)(2,1)} %bitcast.8), calls=%async_computation.2 | async-start | bytes 4194304 | tf_op jit(solution)/shard_map/all_to_all | solution.py:159
  61.5 33.7 %all-to-all-start.1 = ((bf16[8,64,2048]{2,1,0:T(8,128)(2,1)}), bf16[8,64,2048]{2,1,0:T(8,128)(2,1)}, u32[]{:S(2)}, u32[]{:S(2)}) async-start(bf16[8,64,2048]{2,1,0:T(8,128)(2,1)} %bitcast.4), calls=%async_computation.1 | async-start | bytes 4194304 | tf_op jit(solution)/shard_map/all_to_all | solution.py:164
  65.9 199.0 %reduce-scatter.2.cloned.1.call-start = ((), (), s32[]{:S(2)}) async-start(), calls=%async_computation.6 | async-start | bytes 13369344 | tf_op jit(solution)/shard_map/reduce_scatter | solution.py:201
  65.9 2.2 copy-start.1
  71.7 1.4 copy-start.7
  95.2 1.6 copy-start.8
  96.8 2.2 copy-start.13
  99.0 2.2 copy-start.15
  119.1 4.5 %copy-start = (bf16[2048,3072]{1,0:T(8,128)(2,1)}, bf16[2048,3072]{1,0:T(8,128)(2,1)S(1)}, u32[]{:S(2)}) copy-start(bf16[2048,3072]{1,0:T(8,128)(2,1)S(1)} %shard_map.126) | copy-start | bytes 37748740
  123.6 1.0 copy-start.17
  124.6 1.0 copy-start.19
  125.6 1.0 copy-start.21
  126.5 1.2 copy-start.18
  127.8 2.2 copy-start.2
  134.0 1.3 copy-start.4
  135.3 91.0 %all-to-all-start.3 = ((bf16[8,64,2048]{2,1,0:T(8,128)(2,1)}), bf16[8,64,2048]{2,1,0:T(8,128)(2,1)S(1)}, u32[]{:S(2)}, u32[]{:S(2)}) async-start(bf16[8,64,2048]{2,1,0:T(8,128)(2,1)} %bitcast.41), calls=%async_computation.3 | async-start | bytes 4194304 | tf_op jit(solution)/shard_map/all_to_all | solution.py:211
  138.9 2.3 copy-start.14
  141.2 2.3 copy-start.16
  143.4 1.3 copy-start.20
  144.7 1.2 copy-start.22
  152.1 1.3 copy-start.3
  226.3 4.6 %copy-start.6 = (bf16[128,2048]{1,0:T(8,128)(2,1)S(1)}, bf16[128,2048]{1,0:T(8,128)(2,1)}, u32[]{:S(2)}) copy-start(bf16[128,2048]{1,0:T(8,128)(2,1)} %cot_ref.1) | copy-start | bytes 1572868
  226.3 35.5 %all-to-all-start.4 = ((bf16[8,64,2048]{2,1,0:T(8,128)(2,1)}), bf16[8,64,2048]{2,1,0:T(8,128)(2,1)}, u32[]{:S(2)}, u32[]{:S(2)}) async-start(bf16[8,64,2048]{2,1,0:T(8,128)(2,1)} %bitcast.40), calls=%async_computation.4 | async-start | bytes 4194304 | tf_op jit(solution)/shard_map/all_to_all | solution.py:223
Sparse Core Ops, SparseCore 0:
  126.7 94.5 reduce-scatter.1

commit v2 on v0

v2 whole, which is shorter than its diff:
```python
import functools

import jax
import jax.numpy as jnp
from jax import lax
from jax.experimental import pallas as pl
from jax.experimental.pallas import tpu as pltpu
from jax.sharding import PartitionSpec as P

F32 = jnp.float32
BF16 = jnp.bfloat16
NT = (((1,), (1,)), ((), ()))
TN = (((0,), (0,)), ((), ()))
NN = (((1,), (0,)), ((), ()))
MIB = 1 << 20

Y, Z, L, X, C = 4, 2, 2, 4, 2
EP_SWAP = [(i, i ^ 1) for i in range(Y * Z)]
DP_SWAP_L = [(i, i ^ (X * C)) for i in range(L * X * C)]
DP_SWAP_C = [(i, i ^ 1) for i in range(L * X * C)]
VMEM = pl.BlockSpec(memory_space=pltpu.VMEM)
ANY = pl.BlockSpec(memory_space=pl.ANY)
SMEM = pl.BlockSpec(memory_space=pltpu.SMEM)


def y_shift(k):
    return [(y * Z + z, (y + k) % Y * Z + z) for y in range(Y) for z in range(Z)]


def x_shift(k):
    return [
        ((line * X + x) * C + c, (line * X + (x + k) % X) * C + c)
        for line in range(L)
        for x in range(X)
        for c in range(C)
    ]


def struct(*shape, dtype=BF16):
    return jax.ShapeDtypeStruct(shape, dtype)


def dot(a, b, dims=NN):
    return lax.dot_general(a, b, dims, preferred_element_type=F32)


def spec(shape, index=None):
    zeros = (0,) * len(shape)
    return pl.BlockSpec(shape, index or (lambda *_: zeros))


def call(body, out_shape, args, flops=0, in_specs=None, out_specs=None, vmem=32, scratch=()):
    in_specs = in_specs or [None] * len(args)
    out_specs = out_specs or [None] * len(out_shape)
    return pl.pallas_call(
        body,
        in_specs=[s or VMEM for s in in_specs],
        out_specs=[s or VMEM for s in out_specs],
        out_shape=out_shape,
        scratch_shapes=scratch,
        cost_estimate=pl.CostEstimate(
            flops=flops,
            bytes_accessed=sum(a.size * a.dtype.itemsize for a in args),
            transcendentals=0,
        ),
        compiler_params=pltpu.CompilerParams(vmem_limit_bytes=vmem * MIB),
    )(*args)


def streamed(body, out_shape, args, flops, scratch, in_count, out_count, in_specs=None):
    sems = [pltpu.SemaphoreType.DMA((in_count,)), pltpu.SemaphoreType.DMA((out_count,))]
    return call(
        body,
        out_shape,
        args,
        flops,
        in_specs=in_specs or [ANY] * len(args),
        out_specs=[ANY] * len(out_shape),
        vmem=56,
        scratch=[pltpu.VMEM(shape, dtype) for shape, dtype in scratch] + sems,
    )


def started(pairs, sems):
    copies = [pltpu.make_async_copy(a, b, sems.at[n]) for n, (a, b) in enumerate(pairs)]
    for copy in copies:
        copy.start()
    return copies


def places(code_ref, count):
    tokens = code_ref.shape[1]
    expert = lax.broadcasted_iota(jnp.int32, (count, tokens), 0)
    first = (code_ref[0:1, :] == expert).astype(F32)
    second = (code_ref[1:2, :] == expert).astype(F32)
    row = lax.broadcasted_iota(jnp.int32, (tokens, tokens), 0)
    col = lax.broadcasted_iota(jnp.int32, (tokens, tokens), 1)
    before = (row < col).astype(BF16)
    slot = dot((first + second).astype(BF16), before)
    return first, second, slot


def pick(mask, slot, cap):
    count, tokens = slot.shape
    index = lax.broadcasted_iota(jnp.int32, (cap, tokens), 0).astype(F32)
    return jnp.concatenate(
        [jnp.where(index == slot[e : e + 1, :], mask[e : e + 1, :], 0.0) for e in range(count)], axis=0
    )


def pack_d_kernel(cap, code_ref, gates_ref, rows_ref, *out_refs):
    first, second, slot = places(code_ref, Y)
    sel = pick(first + second, slot, cap)
    weight = gates_ref[0:1, :] * first + gates_ref[1:2, :] * second
    scale = jnp.concatenate(
        [
            jnp.sum(sel[e * cap : (e + 1) * cap, :] * weight[e : e + 1, :], axis=1, keepdims=True)
            for e in range(Y)
        ],
        axis=0,
    )
    picked = (dot(sel.astype(BF16), rows_ref[...]) * scale).astype(BF16)
    for e, out_ref in enumerate(out_refs):
        out_ref[...] = picked[e * cap : (e + 1) * cap, :]


def pack_x_kernel(cap, routes_ref, slices_ref, *refs):
    first, second, slot = places(routes_ref, Y * Z)
    sel = pick(first + second, slot, cap).astype(BF16)
    out_ref = refs[-1]
    width = slices_ref.shape[2]
    for j in range(slices_ref.shape[0]):
        out_ref[:, j * width : (j + 1) * width] = dot(sel, slices_ref[j]).astype(BF16)


def hidden_grad_kernel(at_ref, *refs):
    *d_refs, w_ref, out_ref, rows_ref, d, w, out, ins, outs = refs
    cap = d_refs[0].shape[0]
    cuts = [slice(0, 512), slice(512, 1024)]
    pairs = [(r, d.at[pl.ds(pl.multiple_of(at_ref[n] * cap, cap), cap)]) for n, r in enumerate(d_refs)]
    copies = started(pairs + [(w_ref.at[:, c], w.at[:, c]) for c in cuts], ins)
    for copy in copies[: len(pairs)]:
        copy.wait()
    back = [pltpu.make_async_copy(d, rows_ref, outs.at[2])]
    back[0].start()
    for n, c in enumerate(cuts):
        copies[len(pairs) + n].wait()
        out[:, c] = dot(d[...], w[:, c])
        back.append(pltpu.make_async_copy(out.at[:, c], out_ref.at[:, c], outs.at[n]))
        back[-1].start()
    for copy in back:
        copy.wait()


def hidden_kernel(x_ref, wg_ref, wu_ref, hg_ref, out_ref, x, wg, wu, hg, out, ins, outs):
    cuts = [slice(0, 256), slice(256, 512), slice(512, 1024)]
    pairs = [(x_ref, x)]
    for c in cuts:
        pairs += [(a.at[:, c], b.at[:, c]) for a, b in ((wg_ref, wg), (wu_ref, wu), (hg_ref, hg))]
    copies = started(pairs, ins)
    copies[0].wait()
    back = []
    for n, c in enumerate(cuts):
        for copy in copies[1 + 3 * n : 4 + 3 * n]:
            copy.wait()
        pre_gate = dot(x[...], wg[:, c])
        pre_up = dot(x[...], wu[:, c])
        hidden_grad = hg[:, c]
        s = 0.5 * jnp.tanh(0.5 * pre_gate) + 0.5
        silu = pre_gate * s
        out[0, :, c] = (hidden_grad * pre_up * s * (1.0 + pre_gate * (1.0 - s))).astype(BF16)
        out[1, :, c] = (hidden_grad * silu).astype(BF16)
        out[2, :, c] = (silu * pre_up).astype(BF16)
        back.append(pltpu.make_async_copy(out.at[:, :, c], out_ref.at[:, :, c], outs.at[n]))
        back[-1].start()
    for copy in back:
        copy.wait()


def turn_kernel(start_ref, rows_ref, own_ref, other_ref):
    width = own_ref.shape[0] // (L * X)
    for n, out_ref in enumerate((own_ref, other_ref)):
        for j in range(L * X):
            begin = pl.multiple_of(start_ref[n * L * X + j], width)
            out_ref[j * width : (j + 1) * width, :] = rows_ref[:, pl.ds(begin, width)].T


def terms_kernel(n, xo_ref, xp_ref, do_ref, dp_ref, ho_ref, hp_ref, *refs):
    out_refs, (xo, xp, do, dp, ho, hp, out, ins, outs) = refs[1:6], refs[6:]
    size = xo.shape[0]
    rows = slice(n * size, (n + 1) * size)
    pairs = [
        (xo_ref.at[rows], xo),
        (ho_ref.at[0], ho.at[0]),
        (xp_ref.at[rows], xp),
        (hp_ref.at[0], hp.at[0]),
        (ho_ref.at[1], ho.at[1]),
        (hp_ref.at[1], hp.at[1]),
        (do_ref.at[rows], do),
        (ho_ref.at[2], ho.at[2]),
        (dp_ref.at[rows], dp),
        (hp_ref.at[2], hp.at[2]),
    ]
    copies = started(pairs, ins)
    back = []
    for i, (own, peer, ready) in enumerate(((xo, xp, copies[:4]), (xo, xp, copies[4:6]), (do, dp, copies[6:]))):
        for copy in ready:
            copy.wait()
        out[i] = (dot(own[...], ho[i]) + dot(peer[...], hp[i])).astype(BF16)
        begin = 0
        for r in out_refs:
            count = r.shape[1]
            back.append(pltpu.make_async_copy(out.at[i, begin : begin + count], r.at[i], outs.at[len(back)]))
            back[-1].start()
            begin += count
    for copy in back:
        copy.wait()


def near_kernel(up_ref, down_ref, own_up_ref, own_down_ref, *refs):
    to_up_ref, to_down_ref = refs[-2:]
    half = up_ref.shape[1]
    for own_ref, got_ref, out_ref, rows in (
        (own_up_ref, up_ref, to_up_ref, slice(0, half)),
        (own_down_ref, down_ref, to_down_ref, slice(half, 2 * half)),
    ):
        out_ref[...] = own_ref[...]
        out_ref[:, rows, :] = (own_ref[:, rows, :].astype(F32) + got_ref[...].astype(F32)).astype(BF16)


def line_kernel(own_ref, from_up_ref, from_down_ref, *refs):
    line_ref = refs[-3]
    for i in range(3):
        total = own_ref[i].astype(F32) + from_up_ref[i].astype(F32) + from_down_ref[i].astype(F32)
        line_ref[i] = total.astype(BF16)
    near_kernel(*refs[:4], *refs[-2:])


def sum_kernel(*refs):
    *in_refs, gate_ref, up_ref, down_ref = refs
    for i, out_ref in enumerate((gate_ref, up_ref, down_ref)):
        total = in_refs[0][i].astype(F32)
        for r in in_refs[1:]:
            total = total + r[i].astype(F32)
        out_ref[0] = total


def outputs_kernel(cap, hid_ref, wd_ref, wg_ref, wu_ref, out_ref, hid, wd, wg, wu, out, ins, outs):
    cuts = [slice(n * 512, (n + 1) * 512) for n in range(wd.shape[0] // 512)]
    pairs = [(hid_ref.at[2], hid.at[2]), (wd_ref.at[cuts[0]], wd.at[cuts[0]])]
    pairs += [(hid_ref.at[0:2], hid.at[0:2])]
    pairs += [(wg_ref.at[cuts[0]], wg.at[cuts[0]]), (wu_ref.at[cuts[0]], wu.at[cuts[0]])]
    for c in cuts[1:]:
        pairs += [(a.at[c], b.at[c]) for a, b in ((wd_ref, wd), (wg_ref, wg), (wu_ref, wu))]
    copies = started(pairs, ins)
    back = []
    for n, c in enumerate(cuts):
        first = copies[:2] if n == 0 else copies[3 * n + 2 : 3 * n + 3]
        then = copies[2:5] if n == 0 else copies[3 * n + 3 : 3 * n + 5]
        for copy in first:
            copy.wait()
        term = dot(hid[2], wd[c], NT).astype(BF16)
        for s in range(Y * Z):
            out[s, 0, :, c] = term[s * cap : (s + 1) * cap, :]
        for copy in then:
            copy.wait()
        term = (dot(hid[0], wg[c], NT) + dot(hid[1], wu[c], NT)).astype(BF16)
        for s in range(Y * Z):
            out[s, 1, :, c] = term[s * cap : (s + 1) * cap, :]
        back.append(pltpu.make_async_copy(out.at[:, :, :, c], out_ref.at[:, :, :, c], outs.at[n]))
        back[-1].start()
    for copy in back:
        copy.wait()


def combine_kernel(routes_ref, gates_ref, cot_ref, rows_ref, out_ref, part_ref, grad_ref):
    cap = rows_ref.shape[2]
    first, second, slot = places(routes_ref, Y * Z)
    outs = jnp.concatenate([rows_ref[e, 0] for e in range(Y * Z)], axis=0)
    parts = jnp.concatenate([rows_ref[e, 1] for e in range(Y * Z)], axis=0)
    cot = cot_ref[...].astype(F32)
    total, columns = None, []
    for k, mask in enumerate((first, second)):
        mine = dot(pick(mask, slot, cap).astype(BF16), outs, TN)
        columns.append(jnp.sum(cot * mine, axis=1, keepdims=True))
        term = gates_ref[:, k : k + 1] * mine
        total = term if total is None else total + term
    out_ref[...] = total.astype(BF16)
    part_ref[...] = dot(pick(first + second, slot, cap).astype(BF16), parts, TN).astype(BF16)
    grad_ref[...] = jnp.concatenate(columns, axis=1)


def shards(checkpoint, cotangent, routes, gates, w_gate, w_up, w_down):
    tokens, features = cotangent.shape
    dp = lax.axis_size("dp")
    ff = w_gate.shape[2]
    experts = Y * Z
    cap = tokens * routes.shape[1] * 2 // experts
    rows = experts * cap
    w_gate, w_up, w_down = w_gate[0], w_up[0], w_down[0]
    mm = 2 * rows * features * ff
    y, z = lax.axis_index("ep") // Z, lax.axis_index("ep") % Z
    mine = lax.axis_index("dp")
    line, x_at, core = mine // (X * C), mine // C % X, mine % C
    step = jnp.arange(C * L * X, dtype=jnp.int32)
    block_at = (line ^ (1 - step // X % L)) * X + (x_at + step) % X
    start = (block_at * C + (core ^ (step // (L * X)))).astype(jnp.int32) * (features // dp)
    piece_at = ((y - step[: Y * Z]) % Y * Z + (z ^ (step[: Y * Z] // Y))).astype(jnp.int32)

    routes_t, gates_t = routes.T, gates.T
    slices = lax.all_to_all(
        checkpoint.reshape(dp, tokens, features // dp), "dp", split_axis=0, concat_axis=0, tiled=True
    )
    info = lax.ppermute(jnp.concatenate([routes_t.astype(F32), gates_t], axis=0), "ep", EP_SWAP)
    cot_p = lax.ppermute(cotangent, "ep", EP_SWAP)

    def codes(route):
        return jnp.where(route % Z == z, (route // Z - y) % Y, -1)

    code_o, code_p = codes(routes_t), codes(info[:2].astype(jnp.int32))

    def pack_d(code, gate, source):
        return call(
            functools.partial(pack_d_kernel, cap),
            [struct(cap, features)] * Y,
            [code, gate, source],
            2 * Y * cap * tokens * features,
            vmem=16,
        )

    def to_experts(packed):
        return [packed[0]] + [lax.ppermute(packed[k], "ep", y_shift(k)) for k in range(1, Y)]

    d_own = to_experts(pack_d(code_o, gates_t, cotangent))
    (x_send,) = call(
        functools.partial(pack_x_kernel, cap),
        [struct(rows, features)],
        [routes_t, slices, cot_p, info, *d_own],
        2 * rows * tokens * features,
        in_specs=[None, None] + [ANY] * (2 + Y),
        vmem=16,
    )
    x_rows = lax.all_to_all(
        x_send.reshape(experts, cap, features), "ep", split_axis=0, concat_axis=0, tiled=True
    ).reshape(rows, features)
    d_pieces = d_own + to_experts(pack_d(code_p, info[2:], cot_p))

    hidden_grad, d_rows = streamed(
        hidden_grad_kernel,
        [struct(rows, ff, dtype=F32), struct(rows, features)],
        [piece_at, *d_pieces, w_down],
        mm,
        [((rows, features), BF16), ((features, ff), BF16), ((rows, ff), F32)],
        experts + 2,
        3,
        in_specs=[SMEM] + [ANY] * (experts + 1),
    )

    def turn(array):
        own, other = call(
            turn_kernel,
            [struct(features // C, rows)] * 2,
            [start, array],
            in_specs=[SMEM, None],
            vmem=24,
        )
        return own, lax.ppermute(other, "dp", DP_SWAP_C)

    d_turned = turn(d_rows)
    weight = ((features, ff), BF16)
    (hid,) = streamed(
        hidden_kernel,
        [struct(3, rows, ff)],
        [x_rows, w_gate, w_up, hidden_grad],
        2 * mm,
        [((rows, features), BF16), weight, weight, ((rows, ff), F32), ((3, rows, ff), BF16)],
        10,
        3,
    )
    hid_peer = lax.ppermute(hid, "dp", DP_SWAP_C)
    x_turned = turn(x_rows)
    (outs,) = streamed(
        functools.partial(outputs_kernel, cap),
        [struct(experts, 2, cap, features)],
        [hid, w_down, w_gate, w_up],
        3 * mm,
        [((3, rows, ff), BF16), weight, weight, weight, ((experts, 2, cap, features), BF16)],
        14,
        4,
    )
    back = lax.all_to_all(outs, "ep", split_axis=0, concat_axis=0, tiled=True)

    half = tokens // 2
    sizes = (tokens, tokens, half, half, tokens)

    def terms_of(n, after):
        size = X * tokens
        return streamed(
            functools.partial(terms_kernel, n),
            [struct(3, count, ff) for count in sizes],
            [*x_turned, *d_turned, hid, hid_peer, after],
            3 * mm // 2,
            [((size, rows), BF16)] * 4 + [((3, rows, ff), BF16)] * 2 + [((3, size, ff), BF16)],
            10,
            15,
        )

    def small(body, count, arrays, after=()):
        return call(
            body,
            [struct(3, tokens, ff)] * count,
            [*arrays, *after],
            in_specs=[None] * len(arrays) + [ANY] * len(after),
            vmem=24,
        )

    def shift(array, k):
        return lax.ppermute(array, "dp", x_shift(k))

    there = terms_of(0, outs)
    there_up, there_down = shift(there[2], 1), shift(there[3], -1)
    here = terms_of(1, there[0])
    here_up, here_down = shift(here[2], 1), shift(here[3], -1)
    to_up, to_down = small(near_kernel, 2, (there_up, there_down, there[1], there[4]), here[:1])
    there_up, there_down = shift(to_up, 1), shift(to_down, -1)
    other, to_up, to_down = small(
        line_kernel, 3, (there[0], there_up, there_down, here_up, here_down, here[1], here[4])
    )
    other = lax.ppermute(other, "dp", DP_SWAP_L)
    here_up, here_down = shift(to_up, 1), shift(to_down, -1)
    grads = call(
        sum_kernel, [struct(1, tokens, ff, dtype=F32)] * 3, [here[0], here_up, here_down, other], vmem=24
    )
    layer_out, grad_input, grad_gates = call(
        combine_kernel,
        [struct(tokens, features), struct(tokens, features), struct(tokens, 2, dtype=F32)],
        [routes_t, gates, cotangent, back],
        6 * rows * tokens * features,
        vmem=32,
    )
    return (layer_out, grad_input, grad_gates, *grads)


def solution(mesh):
    tok = P(("ep", "dp"), None)
    weight = P("ep", None, None)
    grad = P("ep", "dp", None)
    return jax.shard_map(
        shards,
        mesh=mesh,
        in_specs=(P("ep", "dp"), tok, tok, tok, weight, weight, weight),
        out_specs=(tok, tok, tok, grad, grad, grad),
        check_vma=False,
    )
```

time: 363 us -> 199 us (0.55)
  waiting for transfers between devices: 197 us -> 81.2 us
  Pallas kernels: 0 us -> 53.7 us
  matrix products: 41.1 us -> 0 us
  local copies, waits for them, and re-layouts: 47 us -> 13.2 us
  other arithmetic: 34.3 us -> 1.95 us
  starting transfers between devices: 23.3 us -> 44.6 us
  between operations: 14.6 us -> 1 us
    all_to_all x4 -> x3, waiting for transfers between devices: 131 us -> 0.01 us  [the longest x1 0.01 us: shards(): lax.all_to_all(checkpoint.reshape(dp, tokens, features // dp), 'dp', spli...]
    ppermute x0 -> x20, waiting for transfers between devices: none -> 81.1 us  [the longest x6 35 us: to_experts(): lax.ppermute(packed[k], 'ep', y_shift(k))]
    all_gather x1 -> x0, waiting for transfers between devices: 65.2 us -> none  [shards(): gathered = lax.all_gather(checkpoint, 'dp', axis=1, tiled=True)]
    pallas_call x0 -> x14, Pallas kernels: none -> 53.7 us  [call(): pl.pallas_call(body, in_specs=[s or VMEM for s in in_specs], out_specs=[s...]
    dot_general x9 -> x0, matrix products: 41.1 us -> none  [the longest x3 10.5 us: term_of(): jnp.einsum('sxnd,sxnf->dxf', left, right, preferred_element_type=jnp.floa...]
    ppermute x0 -> x20, starting transfers between devices: none -> 28.8 us  [the longest x8 11.3 us: shift(): return lax.ppermute(array, 'dp', x_shift(k))]
    unnamed x1 -> x0, other arithmetic: 21 us -> none
    gather x4 -> x0, local copies, waits for them, and re-layouts: 12.1 us -> none  [the longest x1 4.22 us: shards(): part_flat[position].reshape(tok_rows, top_count, features)]
  transfers between devices with their start and end apart: 6 -> 23, of which waited for: 4 -> 9; matrix products, arithmetic and copies ran while one was open for 16% -> 1% of each run, Pallas kernels for 0% -> 21%
where the time goes in v2:
time: 199 us; the launch traced here: 196 us
  waiting for transfers between devices  81.2 us (41%)
  Pallas kernels  53.7 us (27%)
  starting transfers between devices  44.6 us (22%)
  local copies, waits for them, and re-layouts  13.2 us (7%)
    pallas_call x14, Pallas kernels, call(): pl.pallas_call(body, in_specs=[s or VMEM for s in in_specs], out_specs=[s...  53.7 us
    ppermute x6, waiting for transfers between devices, to_experts(): lax.ppermute(packed[k], 'ep', y_shift(k))  35 us
    ppermute x8, waiting for transfers between devices, shift(): return lax.ppermute(array, 'dp', x_shift(k))  33.5 us
    unnamed x64, local copies, waits for them, and re-layouts  13.2 us
    ppermute x8, starting transfers between devices, shift(): return lax.ppermute(array, 'dp', x_shift(k))  11.3 us
    ppermute x6, starting transfers between devices, to_experts(): lax.ppermute(packed[k], 'ep', y_shift(k))  10.1 us
    ppermute x1, waiting for transfers between devices, shards(): lax.ppermute(jnp.concatenate([routes_t.astype(F32), gates_t], axis=0), 'e...  9.3 us
    all_to_all x1, starting transfers between devices, shards(): lax.all_to_all(checkpoint.reshape(dp, tokens, features // dp), 'dp', spli...  7.18 us
  transfers between devices with their start and end apart: 23, of which 9 were waited for; matrix products, arithmetic and copies ran while one was open for 1% of the time, Pallas kernels for 21%

profile of v2, /device:TPU:1, one launch (start us, length us, event | category | flops | bytes accessed | tf_op | source)
XLA Modules:
  0.0 195.6 jit_solution(5674766749637866439)
XLA Ops:
  0.6 7.2 %all-to-all-start = ((bf16[16,128,128]{2,1,0:T(8,128)(2,1)}), bf16[16,128,128]{2,1,0:T(8,128)(2,1)S(1)}, u32[]{:S(2)}, u32[]{:S(2)}) async-start(bf16[16,128,128]{2,1,0:T(8,128)(2,1)} %bitcast.17), calls=%async_computation | async-start | bytes 1048576 | tf_op jit(solution)/shard_map/all_to_all | solution.py:311
  7.8 3.3 %collective-permute-start = (bf16[128,2048]{1,0:T(8,128)(2,1)}, bf16[128,2048]{1,0:T(8,128)(2,1)S(1)}, u32[]{:S(2)}, u32[]{:S(2)}) collective-permute-start(bf16[128,2048]{1,0:T(8,128)(2,1)} %cot_ref.1), channel_id=1, source_target_pairs={{0,16},{16,0},{32,48},{48,32},{64,80},{80,64},{96,112},{112,96},{1... | collective-permute-start | bytes 1572872 | tf_op jit(solution)/shard_map/ppermute | solution.py:315
  14.1 1.4 collective-permute-start.2
  15.5 2.6 %collective-permute-start.3 = (bf16[64,2048]{1,0:T(8,128)(2,1)S(1)}, bf16[64,2048]{1,0:T(8,128)(2,1)S(1)}, u32[]{:S(2)}, u32[]{:S(2)}) collective-permute-start(bf16[64,2048]{1,0:T(8,128)(2,1)S(1)} %get-tuple-element.43), channel_id=1, source_target_pairs={{0,64},{16,80},{32,96},{48,112},{64,0},{80,16},{96,32},{112,48},{1... | collective-permute-start | bytes 786440 | tf_op jit(solution)/shard_map/ppermute | solution.py:332
  20.0 9.3 %collective-permute-done.1.refs_1_ = f32[4,128]{1,0:T(4,128)S(1)} collective-permute-done((f32[4,128]{1,0:T(4,128)S(1)}, f32[4,128]{1,0:T(4,128)S(1)}, u32[]{:S(2)}, u32[]{:S(2)}) %collective-permute-start.1) | collective-permute-done | bytes 2080 | tf_op jit(solution)/shard_map/ppermute | solution.py:314
  31.2 1.3 copy-done.2
  32.6 4.0 %all-to-all-start.1 = ((bf16[8,64,2048]{2,1,0:T(8,128)(2,1)}), bf16[8,64,2048]{2,1,0:T(8,128)(2,1)S(1)}, u32[]{:S(2)}, u32[]{:S(2)}) async-start(bf16[8,64,2048]{2,1,0:T(8,128)(2,1)} %bitcast.12), calls=%async_computation.1 | async-start | bytes 4194304 | tf_op jit(solution)/shard_map/all_to_all | solution.py:343
  37.8 1.5 collective-permute-start.5
  39.3 2.4 %collective-permute-start.6 = (bf16[64,2048]{1,0:T(8,128)(2,1)S(1)}, bf16[64,2048]{1,0:T(8,128)(2,1)S(1)}, u32[]{:S(2)}, u32[]{:S(2)}) collective-permute-start(bf16[64,2048]{1,0:T(8,128)(2,1)S(1)} %get-tuple-element.47), channel_id=1, source_target_pairs={{0,64},{16,80},{32,96},{48,112},{64,0},{80,16},{96,32},{112,48},{1... | collective-permute-start | bytes 786440 | tf_op jit(solution)/shard_map/ppermute | solution.py:332
  43.4 23.9 %collective-permute-done.5.refs_5_ = bf16[64,2048]{1,0:T(8,128)(2,1)S(1)} collective-permute-done((bf16[64,2048]{1,0:T(8,128)(2,1)S(1)}, bf16[64,2048]{1,0:T(8,128)(2,1)S(1)}, u32[]{:S(2)}, u32[]{:S(2)}) %collective-permute-start.5) | collective-permute-done | bytes 262176 | tf_op jit(solution)/shard_map/ppermute | solution.py:332
  67.3 10.7 %collective-permute-done.6.refs_6_ = bf16[64,2048]{1,0:T(8,128)(2,1)S(1)} collective-permute-done((bf16[64,2048]{1,0:T(8,128)(2,1)S(1)}, bf16[64,2048]{1,0:T(8,128)(2,1)S(1)}, u32[]{:S(2)}, u32[]{:S(2)}) %collective-permute-start.6) | collective-permute-done | bytes 262176 | tf_op jit(solution)/shard_map/ppermute | solution.py:332
  78.8 6.7 %shard_map.121 = (f32[512,1024]{1,0:T(8,128)}, bf16[512,2048]{1,0:T(8,128)(2,1)}) custom-call(s32[8]{0:T(128)} %fusion.7.at_ref, bf16[64,2048]{1,0:T(8,128)(2,1)} %copy-done.15, bf16[64,2048]{1,0:T(8,128)(2,1)} %copy-done.16, bf16[64,2048]{1,0:T(8,128)(2,1)} %copy-done.17, bf16[64,2048]{1,0:T(8,128)(2,1)} %copy-done.18, bf16[64,2048]{1,0:T(8,128)(2,1)} %copy-done.23, ...), custom_call_target="tpu_custom_call" | custom-call | flops 2147483648 | bytes 6291488 | tf_op jit(solution)/shard_map/pallas_call | solution.py:55
  86.8 9.0 %shard_map.122.hid_ref.ho_ref = bf16[3,512,1024]{2,1,0:T(8,128)(2,1)} custom-call(bf16[512,2048]{1,0:T(8,128)(2,1)} %bitcast.10, bf16[2048,1024]{1,0:T(8,128)(2,1)} %bitcast.18, bf16[2048,1024]{1,0:T(8,128)(2,1)} %bitcast.20, f32[512,1024]{1,0:T(8,128)} %get-tuple-element.49.hg_ref), custom_call_target="tpu_custom_call" | custom-call | flops 4294967296 | bytes 12582912 | tf_op jit(solution)/shard_map/pallas_call | solution.py:55
  95.8 2.0 %collective-permute-start.10 = (bf16[3,512,1024]{2,1,0:T(8,128)(2,1)}, bf16[3,512,1024]{2,1,0:T(8,128)(2,1)}, u32[]{:S(2)}, u32[]{:S(2)}) collective-permute-start(bf16[3,512,1024]{2,1,0:T(8,128)(2,1)} %shard_map.122.hid_ref.ho_ref), channel_id=1, source_target_pairs={{0,1},{1,0},{2,3},{3,2},{4,5},{5,4},{6,7},{7,6},{8,9},{9,8},{10,11... | collective-permute-start | bytes 9437192 | tf_op jit(solution)/shard_map/ppermute | solution.py:380
  97.8 11.4 %shard_map.123.refs_0_ = bf16[8,2,64,2048]{3,2,1,0:T(8,128)(2,1)} custom-call(bf16[3,512,1024]{2,1,0:T(8,128)(2,1)} %shard_map.122.hid_ref.ho_ref, bf16[2048,1024]{1,0:T(8,128)(2,1)} %bitcast.23, bf16[2048,1024]{1,0:T(8,128)(2,1)} %bitcast.19, bf16[2048,1024]{1,0:T(8,128)(2,1)} %bitcast.21), custom_call_target="tpu_custom_call" | custom-call | flops 6442450944 | bytes 15728640 | tf_op jit(solution)/shard_map/pallas_call | solution.py:55
  109.2 4.6 %all-to-all-start.2 = ((bf16[8,2,64,2048]{3,2,1,0:T(8,128)(2,1)}), bf16[8,2,64,2048]{3,2,1,0:T(8,128)(2,1)}, u32[]{:S(2)}, u32[]{:S(2)}) async-start(bf16[8,2,64,2048]{3,2,1,0:T(8,128)(2,1)} %shard_map.123.refs_0_), calls=%async_computation.2 | async-start | bytes 8388608 | tf_op jit(solution)/shard_map/all_to_all | solution.py:391
  113.8 1.7 copy-done.5
  120.4 2.3 %collective-permute-done.8.xp_ref = bf16[1024,512]{1,0:T(8,128)(2,1)S(1)} collective-permute-done((bf16[1024,512]{1,0:T(8,128)(2,1)S(1)}, bf16[1024,512]{1,0:T(8,128)(2,1)S(1)}, u32[]{:S(2)}, u32[]{:S(2)}) %collective-permute-start.8) | collective-permute-done | bytes 1048608 | tf_op jit(solution)/shard_map/ppermute | solution.py:367
  123.6 6.8 %shard_map.127 = (bf16[3,128,1024]{2,1,0:T(8,128)(2,1)}, bf16[3,128,1024]{2,1,0:T(8,128)(2,1)}, bf16[3,64,1024]{2,1,0:T(8,128)(2,1)}, bf16[3,64,1024]{2,1,0:T(8,128)(2,1)}, bf16[3,128,1024]{2,1,0:T(8,128)(2,1)}) custom-call(bf16[1024,512]{1,0:T(8,128)(2,1)} %copy-done.9, bf16[1024,512]{1,0:T(8,128)(2,1)} %copy-done.25, bf16[1024,512]{1,0:T(8,128)(2,1)} %copy-done.8, ...), custom_call_target="tpu_custom_call" | custom-call | flops 3221225472 | bytes 14680064 | tf_op jit(solution)/shard_map/pallas_call | solution.py:55
  130.4 1.5 collective-permute-start.11
  131.9 1.5 collective-permute-start.12
  133.4 6.9 %shard_map.128 = (bf16[3,128,1024]{2,1,0:T(8,128)(2,1)}, bf16[3,128,1024]{2,1,0:T(8,128)(2,1)}, bf16[3,64,1024]{2,1,0:T(8,128)(2,1)}, bf16[3,64,1024]{2,1,0:T(8,128)(2,1)}, bf16[3,128,1024]{2,1,0:T(8,128)(2,1)}) custom-call(bf16[1024,512]{1,0:T(8,128)(2,1)} %copy-done.9, bf16[1024,512]{1,0:T(8,128)(2,1)} %copy-done.25, bf16[1024,512]{1,0:T(8,128)(2,1)} %copy-done.8, ...), custom_call_target="tpu_custom_call" | custom-call | flops 3221225472 | bytes 11272192 | tf_op jit(solution)/shard_map/pallas_call | solution.py:55
  140.4 2.0 %collective-permute-done.11.up_ref = bf16[3,64,1024]{2,1,0:T(8,128)(2,1)S(1)} collective-permute-done((bf16[3,64,1024]{2,1,0:T(8,128)(2,1)}, bf16[3,64,1024]{2,1,0:T(8,128)(2,1)S(1)}, u32[]{:S(2)}, u32[]{:S(2)}) %collective-permute-start.11) | collective-permute-done | bytes 393248 | tf_op jit(solution)/shard_map/ppermute | solution.py:418
  144.9 1.9 collective-permute-start.14
  146.8 2.7 %collective-permute-start.16 = (bf16[3,64,1024]{2,1,0:T(8,128)(2,1)S(1)}, bf16[3,64,1024]{2,1,0:T(8,128)(2,1)S(1)}, u32[]{:S(2)}, u32[]{:S(2)}) collective-permute-start(bf16[3,64,1024]{2,1,0:T(8,128)(2,1)S(1)} %copy-done.26), channel_id=1, source_target_pairs={{0,6},{1,7},{2,0},{3,1},{4,2},{5,3},{6,4},{7,5},{8,14},{9,15},{10,... | collective-permute-start | bytes 1179656 | tf_op jit(solution)/shard_map/ppermute | solution.py:418
  149.5 22.2 %collective-permute-done.15.refs_0_ = bf16[3,64,1024]{2,1,0:T(8,128)(2,1)S(1)} collective-permute-done((bf16[3,64,1024]{2,1,0:T(8,128)(2,1)S(1)}, bf16[3,64,1024]{2,1,0:T(8,128)(2,1)S(1)}, u32[]{:S(2)}, u32[]{:S(2)}) %collective-permute-start.15) | collective-permute-done | bytes 393248 | tf_op jit(solution)/shard_map/ppermute | solution.py:418
  171.7 1.8 shard_map.130
  174.1 2.1 %collective-permute-start.18 = (bf16[3,128,1024]{2,1,0:T(8,128)(2,1)}, bf16[3,128,1024]{2,1,0:T(8,128)(2,1)S(1)}, u32[]{:S(2)}, u32[]{:S(2)}) collective-permute-start(bf16[3,128,1024]{2,1,0:T(8,128)(2,1)} %get-tuple-element.71), channel_id=1, source_target_pairs={{0,6},{1,7},{2,0},{3,1},{4,2},{5,3},{6,4},{7,5},{8,14},{9,15},{10,... | collective-permute-start | bytes 2359304 | tf_op jit(solution)/shard_map/ppermute | solution.py:418
  176.2 1.5 collective-permute-start.19
  177.9 4.3 %shard_map.124 = (bf16[128,2048]{1,0:T(8,128)(2,1)}, bf16[128,2048]{1,0:T(8,128)(2,1)}, f32[128,2]{1,0:T(8,128)S(1)}) custom-call(s32[2,128]{1,0:T(2,128)S(1)} %bitcast.14, f32[128,2]{1,0:T(8,128)S(1)} %copy.13.gates_ref, bf16[128,2048]{1,0:T(8,128)(2,1)S(1)} %copy-done.7, bf16[8,2,64,2048]{3,2,1,0:T(8,128)(2,1)} %all-to-all-done.2.rows_ref), custom_call_target="tpu_custom_call" | custom-call | flops 805306368 | bytes 4720640 | tf_op jit(solution)/shard_map/pallas_call | solution.py:55
  182.8 9.3 %collective-permute-done.17.refs_1_ = bf16[3,128,1024]{2,1,0:T(8,128)(2,1)S(1)} collective-permute-done((bf16[3,128,1024]{2,1,0:T(8,128)(2,1)}, bf16[3,128,1024]{2,1,0:T(8,128)(2,1)S(1)}, u32[]{:S(2)}, u32[]{:S(2)}) %collective-permute-start.17) | collective-permute-done | bytes 786464 | tf_op jit(solution)/shard_map/ppermute | solution.py:418
  193.2 2.4 %shard_map.131 = (f32[1,128,1024]{2,1,0:T(8,128)}, f32[1,128,1024]{2,1,0:T(8,128)}, f32[1,128,1024]{2,1,0:T(8,128)}) custom-call(bf16[3,128,1024]{2,1,0:T(8,128)(2,1)S(1)} %copy-done.4, bf16[3,128,1024]{2,1,0:T(8,128)(2,1)S(1)} %collective-permute-done.17.refs_1_, bf16[3,128,1024]{2,1,0:T(8,128)(2,1)S(1)} %collective-permute-done.18.refs_2_, ...), custom_call_target="tpu_custom_call" | custom-call | bytes 3145728 | tf_op jit(solution)/shard_map/pallas_call | solution.py:55
  (100 shorter events, 22.5 us)
Async XLA Ops:
  0.6 29.0 %all-to-all-start = ((bf16[16,128,128]{2,1,0:T(8,128)(2,1)}), bf16[16,128,128]{2,1,0:T(8,128)(2,1)S(1)}, u32[]{:S(2)}, u32[]{:S(2)}) async-start(bf16[16,128,128]{2,1,0:T(8,128)(2,1)} %bitcast.17), calls=%async_computation | async-start | bytes 1048576 | tf_op jit(solution)/shard_map/all_to_all | solution.py:311
  7.8 21.8 %collective-permute-start = (bf16[128,2048]{1,0:T(8,128)(2,1)}, bf16[128,2048]{1,0:T(8,128)(2,1)S(1)}, u32[]{:S(2)}, u32[]{:S(2)}) collective-permute-start(bf16[128,2048]{1,0:T(8,128)(2,1)} %cot_ref.1), channel_id=1, source_target_pairs={{0,16},{16,0},{32,48},{48,32},{64,80},{80,64},{96,112},{112,96},{1... | collective-permute-start | bytes 1572872 | tf_op jit(solution)/shard_map/ppermute | solution.py:315
  14.1 18.5 %copy-start.15 = (bf16[64,2048]{1,0:T(8,128)(2,1)}, bf16[64,2048]{1,0:T(8,128)(2,1)S(1)}, u32[]{:S(2)}) copy-start(bf16[64,2048]{1,0:T(8,128)(2,1)S(1)} %get-tuple-element.41.refs_2_.refs_0_) | copy-start | bytes 786436
  14.1 15.2 %collective-permute-start.2 = (bf16[64,2048]{1,0:T(8,128)(2,1)S(1)}, bf16[64,2048]{1,0:T(8,128)(2,1)S(1)}, u32[]{:S(2)}, u32[]{:S(2)}) collective-permute-start(bf16[64,2048]{1,0:T(8,128)(2,1)S(1)} %get-tuple-element.42), channel_id=1, source_target_pairs={{0,32},{16,48},{32,64},{48,80},{64,96},{80,112},{96,0},{112,16},{1... | collective-permute-start | bytes 786440 | tf_op jit(solution)/shard_map/ppermute | solution.py:332
  15.5 14.2 %collective-permute-start.3 = (bf16[64,2048]{1,0:T(8,128)(2,1)S(1)}, bf16[64,2048]{1,0:T(8,128)(2,1)S(1)}, u32[]{:S(2)}, u32[]{:S(2)}) collective-permute-start(bf16[64,2048]{1,0:T(8,128)(2,1)S(1)} %get-tuple-element.43), channel_id=1, source_target_pairs={{0,64},{16,80},{32,96},{48,112},{64,0},{80,16},{96,32},{112,48},{1... | collective-permute-start | bytes 786440 | tf_op jit(solution)/shard_map/ppermute | solution.py:332
  18.1 11.6 %collective-permute-start.4 = (bf16[64,2048]{1,0:T(8,128)(2,1)S(1)}, bf16[64,2048]{1,0:T(8,128)(2,1)S(1)}, u32[]{:S(2)}, u32[]{:S(2)}) collective-permute-start(bf16[64,2048]{1,0:T(8,128)(2,1)S(1)} %get-tuple-element.44), channel_id=1, source_target_pairs={{0,96},{16,112},{32,0},{48,16},{64,32},{80,48},{96,64},{112,80},{1... | collective-permute-start | bytes 786440 | tf_op jit(solution)/shard_map/ppermute | solution.py:332
  19.8 9.4 %collective-permute-start.1 = (f32[4,128]{1,0:T(4,128)S(1)}, f32[4,128]{1,0:T(4,128)S(1)}, u32[]{:S(2)}, u32[]{:S(2)}) collective-permute-start(f32[4,128]{1,0:T(4,128)S(1)} %pad_maximum_fusion), channel_id=1, source_target_pairs={{0,16},{16,0},{32,48},{48,32},{64,80},{80,64},{96,112},{112,96},{1... | collective-permute-start | bytes 6152 | tf_op jit(solution)/shard_map/ppermute | solution.py:314
  32.6 52.9 %all-to-all-start.1 = ((bf16[8,64,2048]{2,1,0:T(8,128)(2,1)}), bf16[8,64,2048]{2,1,0:T(8,128)(2,1)S(1)}, u32[]{:S(2)}, u32[]{:S(2)}) async-start(bf16[8,64,2048]{2,1,0:T(8,128)(2,1)} %bitcast.12), calls=%async_computation.1 | async-start | bytes 4194304 | tf_op jit(solution)/shard_map/all_to_all | solution.py:343
  37.8 29.5 %collective-permute-start.5 = (bf16[64,2048]{1,0:T(8,128)(2,1)S(1)}, bf16[64,2048]{1,0:T(8,128)(2,1)S(1)}, u32[]{:S(2)}, u32[]{:S(2)}) collective-permute-start(bf16[64,2048]{1,0:T(8,128)(2,1)S(1)} %get-tuple-element.46), channel_id=1, source_target_pairs={{0,32},{16,48},{32,64},{48,80},{64,96},{80,112},{96,0},{112,16},{1... | collective-permute-start | bytes 786440 | tf_op jit(solution)/shard_map/ppermute | solution.py:332
  39.3 38.7 %collective-permute-start.6 = (bf16[64,2048]{1,0:T(8,128)(2,1)S(1)}, bf16[64,2048]{1,0:T(8,128)(2,1)S(1)}, u32[]{:S(2)}, u32[]{:S(2)}) collective-permute-start(bf16[64,2048]{1,0:T(8,128)(2,1)S(1)} %get-tuple-element.47), channel_id=1, source_target_pairs={{0,64},{16,80},{32,96},{48,112},{64,0},{80,16},{96,32},{112,48},{1... | collective-permute-start | bytes 786440 | tf_op jit(solution)/shard_map/ppermute | solution.py:332
  41.7 36.3 %collective-permute-start.7 = (bf16[64,2048]{1,0:T(8,128)(2,1)S(1)}, bf16[64,2048]{1,0:T(8,128)(2,1)S(1)}, u32[]{:S(2)}, u32[]{:S(2)}) collective-permute-start(bf16[64,2048]{1,0:T(8,128)(2,1)S(1)} %get-tuple-element.48), channel_id=1, source_target_pairs={{0,96},{16,112},{32,0},{48,16},{64,32},{80,48},{96,64},{112,80},{1... | collective-permute-start | bytes 786440 | tf_op jit(solution)/shard_map/ppermute | solution.py:332
  67.3 10.7 %copy-start.28 = (bf16[64,2048]{1,0:T(8,128)(2,1)}, bf16[64,2048]{1,0:T(8,128)(2,1)S(1)}, u32[]{:S(2)}) copy-start(bf16[64,2048]{1,0:T(8,128)(2,1)S(1)} %collective-permute-done.5.refs_5_) | copy-start | bytes 786436
  95.8 26.8 %collective-permute-start.10 = (bf16[3,512,1024]{2,1,0:T(8,128)(2,1)}, bf16[3,512,1024]{2,1,0:T(8,128)(2,1)}, u32[]{:S(2)}, u32[]{:S(2)}) collective-permute-start(bf16[3,512,1024]{2,1,0:T(8,128)(2,1)} %shard_map.122.hid_ref.ho_ref), channel_id=1, source_target_pairs={{0,1},{1,0},{2,3},{3,2},{4,5},{5,4},{6,7},{7,6},{8,9},{9,8},{10,11... | collective-permute-start | bytes 9437192 | tf_op jit(solution)/shard_map/ppermute | solution.py:380
  109.2 68.7 %all-to-all-start.2 = ((bf16[8,2,64,2048]{3,2,1,0:T(8,128)(2,1)}), bf16[8,2,64,2048]{3,2,1,0:T(8,128)(2,1)}, u32[]{:S(2)}, u32[]{:S(2)}) async-start(bf16[8,2,64,2048]{3,2,1,0:T(8,128)(2,1)} %shard_map.123.refs_0_), calls=%async_computation.2 | async-start | bytes 8388608 | tf_op jit(solution)/shard_map/all_to_all | solution.py:391
  117.7 2.7 %collective-permute-start.9 = (bf16[1024,512]{1,0:T(8,128)(2,1)S(1)}, bf16[1024,512]{1,0:T(8,128)(2,1)S(1)}, u32[]{:S(2)}, u32[]{:S(2)}) collective-permute-start(bf16[1024,512]{1,0:T(8,128)(2,1)S(1)} %get-tuple-element.57), channel_id=1, source_target_pairs={{0,1},{1,0},{2,3},{3,2},{4,5},{5,4},{6,7},{7,6},{8,9},{9,8},{10,11... | collective-permute-start | bytes 3145736 | tf_op jit(solution)/shard_map/ppermute | solution.py:367
  119.8 2.8 %collective-permute-start.8 = (bf16[1024,512]{1,0:T(8,128)(2,1)S(1)}, bf16[1024,512]{1,0:T(8,128)(2,1)S(1)}, u32[]{:S(2)}, u32[]{:S(2)}) collective-permute-start(bf16[1024,512]{1,0:T(8,128)(2,1)S(1)} %get-tuple-element.54), channel_id=1, source_target_pairs={{0,1},{1,0},{2,3},{3,2},{4,5},{5,4},{6,7},{7,6},{8,9},{9,8},{10,11... | collective-permute-start | bytes 3145736 | tf_op jit(solution)/shard_map/ppermute | solution.py:367
  130.4 11.9 %collective-permute-start.11 = (bf16[3,64,1024]{2,1,0:T(8,128)(2,1)}, bf16[3,64,1024]{2,1,0:T(8,128)(2,1)S(1)}, u32[]{:S(2)}, u32[]{:S(2)}) collective-permute-start(bf16[3,64,1024]{2,1,0:T(8,128)(2,1)} %get-tuple-element.60), channel_id=1, source_target_pairs={{0,2},{1,3},{2,4},{3,5},{4,6},{5,7},{6,0},{7,1},{8,10},{9,11},{10,... | collective-permute-start | bytes 1179656 | tf_op jit(solution)/shard_map/ppermute | solution.py:418
  131.9 10.5 %collective-permute-start.12 = (bf16[3,64,1024]{2,1,0:T(8,128)(2,1)}, bf16[3,64,1024]{2,1,0:T(8,128)(2,1)S(1)}, u32[]{:S(2)}, u32[]{:S(2)}) collective-permute-start(bf16[3,64,1024]{2,1,0:T(8,128)(2,1)} %get-tuple-element.61), channel_id=1, source_target_pairs={{0,6},{1,7},{2,0},{3,1},{4,2},{5,3},{6,4},{7,5},{8,14},{9,15},{10,... | collective-permute-start | bytes 1179656 | tf_op jit(solution)/shard_map/ppermute | solution.py:418
  133.4 38.3 %copy-start.10 = (bf16[3,128,1024]{2,1,0:T(8,128)(2,1)S(1)}, bf16[3,128,1024]{2,1,0:T(8,128)(2,1)}, u32[]{:S(2)}) copy-start(bf16[3,128,1024]{2,1,0:T(8,128)(2,1)} %get-tuple-element.58.refs_0_.own_ref) | copy-start | bytes 2359300
  143.5 28.2 %copy-start.11 = (bf16[3,128,1024]{2,1,0:T(8,128)(2,1)S(1)}, bf16[3,128,1024]{2,1,0:T(8,128)(2,1)}, u32[]{:S(2)}) copy-start(bf16[3,128,1024]{2,1,0:T(8,128)(2,1)} %get-tuple-element.68.refs_2_) | copy-start | bytes 2359300
  143.5 28.2 %copy-start.12 = (bf16[3,128,1024]{2,1,0:T(8,128)(2,1)S(1)}, bf16[3,128,1024]{2,1,0:T(8,128)(2,1)}, u32[]{:S(2)}) copy-start(bf16[3,128,1024]{2,1,0:T(8,128)(2,1)} %get-tuple-element.69.refs_3_) | copy-start | bytes 2359300
  143.7 34.0 %copy-start.22 = (f32[128,2]{0,1:T(2,128)S(1)}, f32[128,2]{0,1:T(2,128)}, u32[]{:S(2)}) copy-start(f32[128,2]{0,1:T(2,128)} %param.10) | copy-start | bytes 3076
  143.8 34.1 %copy-start.7 = (bf16[128,2048]{1,0:T(8,128)(2,1)S(1)}, bf16[128,2048]{1,0:T(8,128)(2,1)}, u32[]{:S(2)}) copy-start(bf16[128,2048]{1,0:T(8,128)(2,1)} %cot_ref.1) | copy-start | bytes 1572868
  143.8 34.1 %copy-start.20 = (s32[128,2]{0,1:T(2,128)S(1)}, s32[128,2]{0,1:T(2,128)}, u32[]{:S(2)}) copy-start(s32[128,2]{0,1:T(2,128)} %param.9) | copy-start | bytes 3076
  143.8 27.9 %collective-permute-start.13 = (bf16[3,128,1024]{2,1,0:T(8,128)(2,1)S(1)}, bf16[3,128,1024]{2,1,0:T(8,128)(2,1)S(1)}, u32[]{:S(2)}, u32[]{:S(2)}) collective-permute-start(bf16[3,128,1024]{2,1,0:T(8,128)(2,1)S(1)} %get-tuple-element.64), channel_id=1, source_target_pairs={{0,2},{1,3},{2,4},{3,5},{4,6},{5,7},{6,0},{7,1},{8,10},{9,11},{10,... | collective-permute-start | bytes 2359304 | tf_op jit(solution)/shard_map/ppermute | solution.py:418
  144.9 26.8 %collective-permute-start.14 = (bf16[3,128,1024]{2,1,0:T(8,128)(2,1)S(1)}, bf16[3,128,1024]{2,1,0:T(8,128)(2,1)S(1)}, u32[]{:S(2)}, u32[]{:S(2)}) collective-permute-start(bf16[3,128,1024]{2,1,0:T(8,128)(2,1)S(1)} %get-tuple-element.65), channel_id=1, source_target_pairs={{0,6},{1,7},{2,0},{3,1},{4,2},{5,3},{6,4},{7,5},{8,14},{9,15},{10,... | collective-permute-start | bytes 2359304 | tf_op jit(solution)/shard_map/ppermute | solution.py:418
  146.8 24.9 %collective-permute-start.15 = (bf16[3,64,1024]{2,1,0:T(8,128)(2,1)S(1)}, bf16[3,64,1024]{2,1,0:T(8,128)(2,1)S(1)}, u32[]{:S(2)}, u32[]{:S(2)}) collective-permute-start(bf16[3,64,1024]{2,1,0:T(8,128)(2,1)S(1)} %copy-done.27), channel_id=1, source_target_pairs={{0,2},{1,3},{2,4},{3,5},{4,6},{5,7},{6,0},{7,1},{8,10},{9,11},{10,... | collective-permute-start | bytes 1179656 | tf_op jit(solution)/shard_map/ppermute | solution.py:418
  146.8 24.9 %collective-permute-start.16 = (bf16[3,64,1024]{2,1,0:T(8,128)(2,1)S(1)}, bf16[3,64,1024]{2,1,0:T(8,128)(2,1)S(1)}, u32[]{:S(2)}, u32[]{:S(2)}) collective-permute-start(bf16[3,64,1024]{2,1,0:T(8,128)(2,1)S(1)} %copy-done.26), channel_id=1, source_target_pairs={{0,6},{1,7},{2,0},{3,1},{4,2},{5,3},{6,4},{7,5},{8,14},{9,15},{10,... | collective-permute-start | bytes 1179656 | tf_op jit(solution)/shard_map/ppermute | solution.py:418
  173.6 19.6 %copy-start.4 = (bf16[3,128,1024]{2,1,0:T(8,128)(2,1)S(1)}, bf16[3,128,1024]{2,1,0:T(8,128)(2,1)}, u32[]{:S(2)}) copy-start(bf16[3,128,1024]{2,1,0:T(8,128)(2,1)} %get-tuple-element.59.refs_0_) | copy-start | bytes 2359300
  173.6 18.5 %collective-permute-start.17 = (bf16[3,128,1024]{2,1,0:T(8,128)(2,1)}, bf16[3,128,1024]{2,1,0:T(8,128)(2,1)S(1)}, u32[]{:S(2)}, u32[]{:S(2)}) collective-permute-start(bf16[3,128,1024]{2,1,0:T(8,128)(2,1)} %get-tuple-element.70), channel_id=1, source_target_pairs={{0,2},{1,3},{2,4},{3,5},{4,6},{5,7},{6,0},{7,1},{8,10},{9,11},{10,... | collective-permute-start | bytes 2359304 | tf_op jit(solution)/shard_map/ppermute | solution.py:418
  174.1 18.0 %collective-permute-start.18 = (bf16[3,128,1024]{2,1,0:T(8,128)(2,1)}, bf16[3,128,1024]{2,1,0:T(8,128)(2,1)S(1)}, u32[]{:S(2)}, u32[]{:S(2)}) collective-permute-start(bf16[3,128,1024]{2,1,0:T(8,128)(2,1)} %get-tuple-element.71), channel_id=1, source_target_pairs={{0,6},{1,7},{2,0},{3,1},{4,2},{5,3},{6,4},{7,5},{8,14},{9,15},{10,... | collective-permute-start | bytes 2359304 | tf_op jit(solution)/shard_map/ppermute | solution.py:418
  176.2 16.9 %collective-permute-start.19 = (bf16[3,128,1024]{2,1,0:T(8,128)(2,1)}, bf16[3,128,1024]{2,1,0:T(8,128)(2,1)}, u32[]{:S(2)}, u32[]{:S(2)}) collective-permute-start(bf16[3,128,1024]{2,1,0:T(8,128)(2,1)} %get-tuple-element.72), channel_id=1, source_target_pairs={{0,8},{1,9},{2,10},{3,11},{4,12},{5,13},{6,14},{7,15},{8,0},{9,1},... | collective-permute-start | bytes 2359304 | tf_op jit(solution)/shard_map/ppermute | solution.py:429
  (22 other events, 52.9 us)

commit v3 on v2

--- a/solution.py
+++ b/solution.py
@@ -49,13 +49,18 @@
     return pl.BlockSpec(shape, index or (lambda *_: zeros))
 
 
-def call(body, out_shape, args, flops=0, in_specs=None, out_specs=None, vmem=32, scratch=()):
+def call(body, out_shape, args, flops=0, in_specs=None, out_specs=None, vmem=32, scratch=(), blocks=False):
     in_specs = in_specs or [None] * len(args)
     out_specs = out_specs or [None] * len(out_shape)
+
+    def whole(array):
+        return spec(array.shape) if blocks else VMEM
+
     return pl.pallas_call(
         body,
-        in_specs=[s or VMEM for s in in_specs],
-        out_specs=[s or VMEM for s in out_specs],
+        grid=(1,) if blocks else (),
+        in_specs=[s or whole(a) for s, a in zip(in_specs, args, strict=True)],
+        out_specs=[s or whole(a) for s, a in zip(out_specs, out_shape, strict=True)],
         out_shape=out_shape,
         scratch_shapes=scratch,
         cost_estimate=pl.CostEstimate(
@@ -108,10 +113,14 @@
     )
 
 
-def pack_d_kernel(cap, code_ref, gates_ref, rows_ref, *out_refs):
+def codes(routes, at_ref):
+    return jnp.where((routes & 1) == at_ref[1], ((routes >> 1) - at_ref[0]) & (Y - 1), -1)
+
+
+def pack_d(cap, code_ref, gates, rows, out_refs):
     first, second, slot = places(code_ref, Y)
     sel = pick(first + second, slot, cap)
-    weight = gates_ref[0:1, :] * first + gates_ref[1:2, :] * second
+    weight = gates[0:1, :] * first + gates[1:2, :] * second
     scale = jnp.concatenate(
         [
             jnp.sum(sel[e * cap : (e + 1) * cap, :] * weight[e : e + 1, :], axis=1, keepdims=True)
@@ -119,30 +128,72 @@
         ],
         axis=0,
     )
-    picked = (dot(sel.astype(BF16), rows_ref[...]) * scale).astype(BF16)
+    picked = (dot(sel.astype(BF16), rows) * scale).astype(BF16)
     for e, out_ref in enumerate(out_refs):
         out_ref[...] = picked[e * cap : (e + 1) * cap, :]
 
 
-def pack_x_kernel(cap, routes_ref, slices_ref, *refs):
-    first, second, slot = places(routes_ref, Y * Z)
-    sel = pick(first + second, slot, cap).astype(BF16)
-    out_ref = refs[-1]
-    width = slices_ref.shape[2]
-    for j in range(slices_ref.shape[0]):
-        out_ref[:, j * width : (j + 1) * width] = dot(sel, slices_ref[j]).astype(BF16)
-
-
-def hidden_grad_kernel(at_ref, *refs):
-    *d_refs, w_ref, out_ref, rows_ref, d, w, out, ins, outs = refs
+def own_kernel(cap, at_ref, routes_ref, gates_ref, cot_ref, ck_ref, code_ref, wide_ref, ck_out_ref, *out_refs):
+    features = cot_ref.shape[1]
+    wide_ref[:, 0:features] = cot_ref[...]
+    ck_out_ref[...] = ck_ref[...]
+    gates = gates_ref[...]
+    pieces, rest = [routes_ref[...].astype(F32)], gates
+    for _ in range(3):
+        pieces.append(rest.astype(BF16).astype(F32))
+        rest = rest - pieces[-1]
+    tokens = gates.shape[1]
+    columns = jnp.concatenate([*pieces, jnp.zeros((tokens - 8, tokens), F32)], axis=0)
+    wide_ref[:, features:] = columns.T.astype(BF16)
+    code_ref[...] = codes(routes_ref[...], at_ref)
+    pack_d(cap, code_ref, gates, cot_ref[...], out_refs)
+
+
+def copy_kernel(in_ref, _, out_ref):
+    out_ref[...] = in_ref[...]
+
+
+def partner_kernel(cap, at_ref, wide_ref, *refs):
+    code_ref, *out_refs = refs[-1 - Y :]
+    features = out_refs[0].shape[1]
+    columns = wide_ref[:, features:].astype(F32).T
+    code_ref[...] = codes(columns[0:2, :].astype(jnp.int32), at_ref)
+    gates = columns[2:4, :] + columns[4:6, :] + columns[6:8, :]
+    pack_d(cap, code_ref, gates, wide_ref[:, 0:features], out_refs)
+
+
+def pack_x_kernel(cap, code_o_ref, code_p_ref, slices_o_ref, slices_p_ref, *refs):
+    out_refs = refs[-Y:]
+    width = slices_o_ref.shape[2]
+    for n, (code_ref, slices_ref) in enumerate(((code_o_ref, slices_o_ref), (code_p_ref, slices_p_ref))):
+        first, second, slot = places(code_ref, Y)
+        sel = pick(first + second, slot, cap).astype(BF16)
+        for j in range(slices_ref.shape[0]):
+            picked = dot(sel, slices_ref[j]).astype(BF16)
+            for k, out_ref in enumerate(out_refs):
+                out_ref[n * cap : (n + 1) * cap, j * width : (j + 1) * width] = picked[k * cap : (k + 1) * cap, :]
+
+
+def turn(rows, start_ref, own, other):
+    width = own.shape[0] // (L * X)
+    for n, out in enumerate((own, other)):
+        for j in range(L * X):
+            begin = pl.multiple_of(start_ref[n * L * X + j], width)
+            out[j * width : (j + 1) * width, :] = rows[:, pl.ds(begin, width)].T
+
+
+def hidden_grad_kernel(at_ref, start_ref, *refs):
+    *d_refs, w_ref, out_ref, own_ref, other_ref, d, w, out, own, other, ins, outs = refs
     cap = d_refs[0].shape[0]
     cuts = [slice(0, 512), slice(512, 1024)]
     pairs = [(r, d.at[pl.ds(pl.multiple_of(at_ref[n] * cap, cap), cap)]) for n, r in enumerate(d_refs)]
     copies = started(pairs + [(w_ref.at[:, c], w.at[:, c]) for c in cuts], ins)
     for copy in copies[: len(pairs)]:
         copy.wait()
-    back = [pltpu.make_async_copy(d, rows_ref, outs.at[2])]
-    back[0].start()
+    turn(d, start_ref, own, other)
+    back = [pltpu.make_async_copy(a, b, outs.at[2 + n]) for n, (a, b) in enumerate(((own, own_ref), (other, other_ref)))]
+    for copy in back:
+        copy.start()
     for n, c in enumerate(cuts):
         copies[len(pairs) + n].wait()
         out[:, c] = dot(d[...], w[:, c])
@@ -152,19 +203,33 @@
         copy.wait()
 
 
-def hidden_kernel(x_ref, wg_ref, wu_ref, hg_ref, out_ref, x, wg, wu, hg, out, ins, outs):
+def hidden_kernel(at_ref, start_ref, *refs):
+    x_refs, refs = refs[:Y], refs[Y:]
+    wg_ref, wu_ref, hg_ref, out_ref, own_ref, other_ref, x, wg, wu, hg, out, own, other, ins, outs = refs
     cuts = [slice(0, 256), slice(256, 512), slice(512, 1024)]
-    pairs = [(x_ref, x)]
+    cap = x_refs[0].shape[0] // 2
+    pairs = [
+        (r.at[n * cap : (n + 1) * cap], x.at[pl.ds(pl.multiple_of(at_ref[n * Y + k] * cap, cap), cap)])
+        for k, r in enumerate(x_refs)
+        for n in range(2)
+    ]
+    count = len(pairs)
     for c in cuts:
         pairs += [(a.at[:, c], b.at[:, c]) for a, b in ((wg_ref, wg), (wu_ref, wu), (hg_ref, hg))]
     copies = started(pairs, ins)
-    copies[0].wait()
+    for copy in copies[:count]:
+        copy.wait()
     back = []
     for n, c in enumerate(cuts):
-        for copy in copies[1 + 3 * n : 4 + 3 * n]:
+        for copy in copies[count + 3 * n : count + 3 * n + 3]:
             copy.wait()
         pre_gate = dot(x[...], wg[:, c])
         pre_up = dot(x[...], wu[:, c])
+        if n == 0:
+            turn(x, start_ref, own, other)
+            back += [pltpu.make_async_copy(own, own_ref, outs.at[3]), pltpu.make_async_copy(other, other_ref, outs.at[4])]
+            for copy in back:
+                copy.start()
         hidden_grad = hg[:, c]
         s = 0.5 * jnp.tanh(0.5 * pre_gate) + 0.5
         silu = pre_gate * s
@@ -175,14 +240,6 @@
         back[-1].start()
     for copy in back:
         copy.wait()
-
-
-def turn_kernel(start_ref, rows_ref, own_ref, other_ref):
-    width = own_ref.shape[0] // (L * X)
-    for n, out_ref in enumerate((own_ref, other_ref)):
-        for j in range(L * X):
-            begin = pl.multiple_of(start_ref[n * L * X + j], width)
-            out_ref[j * width : (j + 1) * width, :] = rows_ref[:, pl.ds(begin, width)].T
 
 
 def terms_kernel(n, xo_ref, xp_ref, do_ref, dp_ref, ho_ref, hp_ref, *refs):
@@ -308,77 +365,78 @@
     piece_at = ((y - step[: Y * Z]) % Y * Z + (z ^ (step[: Y * Z] // Y))).astype(jnp.int32)
 
     routes_t, gates_t = routes.T, gates.T
+    at = jnp.stack([y, z]).astype(jnp.int32)
+    code_o, wide, slices, *packed = call(
+        functools.partial(own_kernel, cap),
+        [
+            struct(2, tokens, dtype=jnp.int32),
+            struct(tokens, features + tokens),
+            struct(*checkpoint.shape),
+            *[struct(cap, features)] * Y,
+        ],
+        [at, routes_t, gates_t, cotangent, checkpoint],
+        2 * Y * cap * tokens * features,
+        in_specs=[SMEM] + [None] * 4,
+        vmem=56,
+        blocks=True,
+    )
+    wide = lax.ppermute(wide, "ep", EP_SWAP)
     slices = lax.all_to_all(
-        checkpoint.reshape(dp, tokens, features // dp), "dp", split_axis=0, concat_axis=0, tiled=True
-    )
-    info = lax.ppermute(jnp.concatenate([routes_t.astype(F32), gates_t], axis=0), "ep", EP_SWAP)
-    cot_p = lax.ppermute(cotangent, "ep", EP_SWAP)
-
-    def codes(route):
-        return jnp.where(route % Z == z, (route // Z - y) % Y, -1)
-
-    code_o, code_p = codes(routes_t), codes(info[:2].astype(jnp.int32))
-
-    def pack_d(code, gate, source):
-        return call(
-            functools.partial(pack_d_kernel, cap),
-            [struct(cap, features)] * Y,
-            [code, gate, source],
-            2 * Y * cap * tokens * features,
+        slices.reshape(dp, tokens, features // dp), "dp", split_axis=0, concat_axis=0, tiled=True
+    )
+
+    def to_experts(packed):
+        return [packed[0]] + [lax.ppermute(packed[k], "ep", y_shift(k)) for k in range(1, Y)]
+
+    d_own = to_experts(packed)
+    (slices,) = call(copy_kernel, [struct(*slices.shape)], [slices, d_own[1]], in_specs=[None, ANY], vmem=16)
+    slices_p = lax.ppermute(slices, "ep", EP_SWAP)
+    code_p, *packed = call(
+        functools.partial(partner_kernel, cap),
+        [struct(2, tokens, dtype=jnp.int32), *[struct(cap, features)] * Y],
+        [at, wide],
+        2 * Y * cap * tokens * features,
+        in_specs=[SMEM, None],
+        vmem=16,
+    )
+    d_pieces = d_own + to_experts(packed)
+    x_pieces = to_experts(
+        call(
+            functools.partial(pack_x_kernel, cap),
+            [struct(2 * cap, features)] * Y,
+            [code_o, code_p, slices, slices_p, d_pieces[Y]],
+            4 * Y * cap * tokens * features,
+            in_specs=[None] * 4 + [ANY],
             vmem=16,
         )
-
-    def to_experts(packed):
-        return [packed[0]] + [lax.ppermute(packed[k], "ep", y_shift(k)) for k in range(1, Y)]
-
-    d_own = to_experts(pack_d(code_o, gates_t, cotangent))
-    (x_send,) = call(
-        functools.partial(pack_x_kernel, cap),
-        [struct(rows, features)],
-        [routes_t, slices, cot_p, info, *d_own],
-        2 * rows * tokens * features,
-        in_specs=[None, None] + [ANY] * (2 + Y),
-        vmem=16,
-    )
-    x_rows = lax.all_to_all(
-        x_send.reshape(experts, cap, features), "ep", split_axis=0, concat_axis=0, tiled=True
-    ).reshape(rows, features)
-    d_pieces = d_own + to_experts(pack_d(code_p, info[2:], cot_p))
-
-    hidden_grad, d_rows = streamed(
+    )
+
+    weight = ((features, ff), BF16)
+    turned = struct(features // C, rows)
+    scratch = [((rows, features), BF16), weight, ((rows, ff), F32), *[(turned.shape, BF16)] * 2]
+    hidden_grad, d_own, d_other = streamed(
         hidden_grad_kernel,
-        [struct(rows, ff, dtype=F32), struct(rows, features)],
-        [piece_at, *d_pieces, w_down],
+        [struct(rows, ff, dtype=F32), turned, turned],
+        [piece_at, start, *d_pieces, w_down],
         mm,
-        [((rows, features), BF16), ((features, ff), BF16), ((rows, ff), F32)],
+        scratch,
         experts + 2,
-        3,
-        in_specs=[SMEM] + [ANY] * (experts + 1),
-    )
-
-    def turn(array):
-        own, other = call(
-            turn_kernel,
-            [struct(features // C, rows)] * 2,
-            [start, array],
-            in_specs=[SMEM, None],
-            vmem=24,
-        )
-        return own, lax.ppermute(other, "dp", DP_SWAP_C)
-
-    d_turned = turn(d_rows)
-    weight = ((features, ff), BF16)
-    (hid,) = streamed(
+        4,
+        in_specs=[SMEM] * 2 + [ANY] * (experts + 1),
+    )
+    d_turned = d_own, lax.ppermute(d_other, "dp", DP_SWAP_C)
+    hid, x_own, x_other = streamed(
         hidden_kernel,
-        [struct(3, rows, ff)],
-        [x_rows, w_gate, w_up, hidden_grad],
+        [struct(3, rows, ff), turned, turned],
+        [piece_at, start, *x_pieces, w_gate, w_up, hidden_grad],
         2 * mm,
-        [((rows, features), BF16), weight, weight, ((rows, ff), F32), ((3, rows, ff), BF16)],
-        10,
-        3,
+        [scratch[0], weight, weight, scratch[2], ((3, rows, ff), BF16), *scratch[3:]],
+        experts + 9,
+        5,
+        in_specs=[SMEM] * 2 + [ANY] * (Y + 3),
     )
     hid_peer = lax.ppermute(hid, "dp", DP_SWAP_C)
-    x_turned = turn(x_rows)
+    x_turned = x_own, lax.ppermute(x_other, "dp", DP_SWAP_C)
     (outs,) = streamed(
         functools.partial(outputs_kernel, cap),
         [struct(experts, 2, cap, features)],

time: 199 us -> 188 us (0.945)
  waiting for transfers between devices: 81.2 us -> 72.7 us
  local copies, waits for them, and re-layouts: 13.2 us -> 9.03 us
  Pallas kernels: 53.7 us -> 55.8 us
    ppermute x6 -> x9, waiting for transfers between devices: 35 us -> 22.2 us  [to_experts(): lax.ppermute(packed[k], 'ep', y_shift(k))]
    ppermute x6 -> x9, starting transfers between devices: 10.1 us -> 14.7 us  [to_experts(): lax.ppermute(packed[k], 'ep', y_shift(k))]
    unnamed x64 -> x54, local copies, waits for them, and re-layouts: 13.2 us -> 9.03 us
    all_to_all x2 -> x1, starting transfers between devices: 11.2 us -> 7.16 us  [shards(): lax.all_to_all(slices.reshape(dp, tokens, features // dp), 'dp', split_ax...]
    ppermute x4, waiting for transfers between devices: 11.6 us -> 14.4 us  [the longest x1 5.46 us: shards(): slices_p = lax.ppermute(slices, 'ep', EP_SWAP)]
    pallas_call x14 -> x13, Pallas kernels: 53.7 us -> 55.8 us  [call(): pl.pallas_call(body, grid=(1,) if blocks else (), in_specs=[s or whole(a)...]
  transfers between devices with their start and end apart: 23 -> 25, of which waited for: 9 -> 12; matrix products, arithmetic and copies ran while one was open for 1% -> 1% of each run, Pallas kernels for 21% -> 22%
where the time goes in v3:
time: 188 us; the launch traced here: 185 us
  waiting for transfers between devices  72.7 us (39%)
  Pallas kernels  55.8 us (30%)
  starting transfers between devices  45.2 us (24%)
  local copies, waits for them, and re-layouts  9.03 us (5%)
    pallas_call x13, Pallas kernels, call(): pl.pallas_call(body, grid=(1,) if blocks else (), in_specs=[s or whole(a)...  55.8 us
    ppermute x8, waiting for transfers between devices, shift(): return lax.ppermute(array, 'dp', x_shift(k))  35 us
    ppermute x9, waiting for transfers between devices, to_experts(): lax.ppermute(packed[k], 'ep', y_shift(k))  22.2 us
    ppermute x9, starting transfers between devices, to_experts(): lax.ppermute(packed[k], 'ep', y_shift(k))  14.7 us
    ppermute x8, starting transfers between devices, shift(): return lax.ppermute(array, 'dp', x_shift(k))  11.1 us
    unnamed x54, local copies, waits for them, and re-layouts  9.03 us
    all_to_all x1, starting transfers between devices, shards(): lax.all_to_all(slices.reshape(dp, tokens, features // dp), 'dp', split_ax...  7.16 us
    ppermute x1, waiting for transfers between devices, shards(): slices_p = lax.ppermute(slices, 'ep', EP_SWAP)  5.46 us
  transfers between devices with their start and end apart: 25, of which 12 were waited for; matrix products, arithmetic and copies ran while one was open for 1% of the time, Pallas kernels for 22%

profile of v3, /device:TPU:1, one launch (start us, length us, event | category | flops | bytes accessed | tf_op | source)
XLA Modules:
  0.0 185.3 jit_solution(135471487064143163)
XLA Ops:
  1.3 3.1 %shard_map.118 = (s32[2,128]{1,0:T(2,128)}, bf16[128,2176]{1,0:T(8,128)(2,1)}, bf16[2048,128]{1,0:T(8,128)(2,1)}, bf16[64,2048]{1,0:T(8,128)(2,1)}, bf16[64,2048...) custom-call(s32[2]{0:T(128)} %pad_add_fusion.at_ref, s32[2,128]{1,0:T(2,128)} %bitcast.8, ...), custom_call_target="tpu_custom_call" | custom-call | flops 134217728 | bytes 1050632 | tf_op jit(solution)/shard_map/pallas_call | solution.py:59
  4.3 7.2 %all-to-all-start = ((bf16[16,128,128]{2,1,0:T(8,128)(2,1)}), bf16[16,128,128]{2,1,0:T(8,128)(2,1)S(1)}, u32[]{:S(2)}, u32[]{:S(2)}) async-start(bf16[16,128,128]{2,1,0:T(8,128)(2,1)} %bitcast.10), calls=%async_computation | async-start | bytes 1048576 | tf_op jit(solution)/shard_map/all_to_all | solution.py:384
  11.5 3.3 %collective-permute-start = (bf16[128,2176]{1,0:T(8,128)(2,1)}, bf16[128,2176]{1,0:T(8,128)(2,1)S(1)}, u32[]{:S(2)}, u32[]{:S(2)}) collective-permute-start(bf16[128,2176]{1,0:T(8,128)(2,1)} %get-tuple-element.50), channel_id=1, source_target_pairs={{0,16},{16,0},{32,48},{48,32},{64,80},{80,64},{96,112},{112,96},{1... | collective-permute-start | bytes 1671176 | tf_op jit(solution)/shard_map/ppermute | solution.py:383
  16.1 7.7 %collective-permute-done.1._.refs_1_ = bf16[64,2048]{1,0:T(8,128)(2,1)S(1)} collective-permute-done((bf16[64,2048]{1,0:T(8,128)(2,1)}, bf16[64,2048]{1,0:T(8,128)(2,1)S(1)}, u32[]{:S(2)}, u32[]{:S(2)}) %collective-permute-start.1) | collective-permute-done | bytes 262176 | tf_op jit(solution)/shard_map/ppermute | solution.py:389
  24.8 2.9 %collective-permute-start.6 = (bf16[64,2048]{1,0:T(8,128)(2,1)}, bf16[64,2048]{1,0:T(8,128)(2,1)S(1)}, u32[]{:S(2)}, u32[]{:S(2)}) collective-permute-start(bf16[64,2048]{1,0:T(8,128)(2,1)} %get-tuple-element.60), channel_id=1, source_target_pairs={{0,64},{16,80},{32,96},{48,112},{64,0},{80,16},{96,32},{112,48},{1... | collective-permute-start | bytes 786440 | tf_op jit(solution)/shard_map/ppermute | solution.py:389
  28.5 5.1 %collective-permute-done.wide_ref = bf16[128,2176]{1,0:T(8,128)(2,1)S(1)} collective-permute-done((bf16[128,2176]{1,0:T(8,128)(2,1)}, bf16[128,2176]{1,0:T(8,128)(2,1)S(1)}, u32[]{:S(2)}, u32[]{:S(2)}) %collective-permute-start) | collective-permute-done | bytes 557088 | tf_op jit(solution)/shard_map/ppermute | solution.py:383
  36.8 2.6 %collective-permute-start.9 = (bf16[64,2048]{1,0:T(8,128)(2,1)S(1)}, bf16[64,2048]{1,0:T(8,128)(2,1)S(1)}, u32[]{:S(2)}, u32[]{:S(2)}) collective-permute-start(bf16[64,2048]{1,0:T(8,128)(2,1)S(1)} %get-tuple-element.63), channel_id=1, source_target_pairs={{0,64},{16,80},{32,96},{48,112},{64,0},{80,16},{96,32},{112,48},{1... | collective-permute-start | bytes 786440 | tf_op jit(solution)/shard_map/ppermute | solution.py:389
  39.4 5.5 %collective-permute-done.2.slices_p_ref = bf16[16,128,128]{2,1,0:T(8,128)(2,1)S(1)} collective-permute-done((bf16[16,128,128]{2,1,0:T(8,128)(2,1)S(1)}, bf16[16,128,128]{2,1,0:T(8,128)(2,1)S(1)}, u32[]{:S(2)}, u32[]{:S(2)}) %collective-permute-start.2) | collective-permute-done | bytes 524320 | tf_op jit(solution)/shard_map/ppermute | solution.py:393
  44.8 2.7 %collective-permute-start.10 = (bf16[64,2048]{1,0:T(8,128)(2,1)S(1)}, bf16[64,2048]{1,0:T(8,128)(2,1)S(1)}, u32[]{:S(2)}, u32[]{:S(2)}) collective-permute-start(bf16[64,2048]{1,0:T(8,128)(2,1)S(1)} %get-tuple-element.64), channel_id=1, source_target_pairs={{0,96},{16,112},{32,0},{48,16},{64,32},{80,48},{96,64},{112,80},{1... | collective-permute-start | bytes 786440 | tf_op jit(solution)/shard_map/ppermute | solution.py:389
  49.3 1.6 collective-permute-start.4
  54.2 6.6 %shard_map.122 = (f32[512,1024]{1,0:T(8,128)}, bf16[1024,512]{1,0:T(8,128)(2,1)}, bf16[1024,512]{1,0:T(8,128)(2,1)}) custom-call(s32[8]{0:T(128)} %fusion.5.at_ref, s32[16]{0:T(128)} %fusion.3.start_ref, bf16[64,2048]{1,0:T(8,128)(2,1)} %get-tuple-element.59.refs_0_, bf16[64,2048]{1,0:T(8,128)(2,1)} %copy-done.8, bf16[64,2048]{1,0:T(8,128)(2,1)} %copy-done.21, ...), custom_call_target="tpu_custom_call" | custom-call | flops 2147483648 | bytes 6291552 | tf_op jit(solution)/shard_map/pallas_call | solution.py:59
  60.8 3.3 %collective-permute-done.3.refs_1_ = bf16[128,2048]{1,0:T(8,128)(2,1)S(1)} collective-permute-done((bf16[128,2048]{1,0:T(8,128)(2,1)S(1)}, bf16[128,2048]{1,0:T(8,128)(2,1)S(1)}, u32[]{:S(2)}, u32[]{:S(2)}) %collective-permute-start.3) | collective-permute-done | bytes 524320 | tf_op jit(solution)/shard_map/ppermute | solution.py:389
  64.1 9.2 %collective-permute-done.4.refs_2_ = bf16[128,2048]{1,0:T(8,128)(2,1)S(1)} collective-permute-done((bf16[128,2048]{1,0:T(8,128)(2,1)S(1)}, bf16[128,2048]{1,0:T(8,128)(2,1)S(1)}, u32[]{:S(2)}, u32[]{:S(2)}) %collective-permute-start.4) | collective-permute-done | bytes 524320 | tf_op jit(solution)/shard_map/ppermute | solution.py:389
  73.3 2.0 %collective-permute-done.5.refs_3_ = bf16[128,2048]{1,0:T(8,128)(2,1)S(1)} collective-permute-done((bf16[128,2048]{1,0:T(8,128)(2,1)S(1)}, bf16[128,2048]{1,0:T(8,128)(2,1)S(1)}, u32[]{:S(2)}, u32[]{:S(2)}) %collective-permute-start.5) | collective-permute-done | bytes 524320 | tf_op jit(solution)/shard_map/ppermute | solution.py:389
  76.1 10.2 %shard_map.123 = (bf16[3,512,1024]{2,1,0:T(8,128)(2,1)}, bf16[1024,512]{1,0:T(8,128)(2,1)}, bf16[1024,512]{1,0:T(8,128)(2,1)}) custom-call(s32[8]{0:T(128)} %fusion.5.at_ref, s32[16]{0:T(128)} %fusion.3.start_ref, bf16[128,2048]{1,0:T(8,128)(2,1)} %copy-done.13, bf16[128,2048]{1,0:T(8,128)(2,1)} %copy-done.18, bf16[128,2048]{1,0:T(8,128)(2,1)} %copy-done.19, ...), custom_call_target="tpu_custom_call" | custom-call | flops 4294967296 | bytes 12583008 | tf_op jit(solution)/shard_map/pallas_call | solution.py:59
  86.3 1.7 collective-permute-start.13
  88.0 11.4 %shard_map.124.refs_0_ = bf16[8,2,64,2048]{3,2,1,0:T(8,128)(2,1)} custom-call(bf16[3,512,1024]{2,1,0:T(8,128)(2,1)} %get-tuple-element.66.hid_ref.ho_ref, bf16[2048,1024]{1,0:T(8,128)(2,1)} %bitcast.17, bf16[2048,1024]{1,0:T(8,128)(2,1)} %bitcast.13, bf16[2048,1024]{1,0:T(8,128)(2,1)} %bitcast.15), custom_call_target="tpu_custom_call" | custom-call | flops 6442450944 | bytes 15728640 | tf_op jit(solution)/shard_map/pallas_call | solution.py:59
  99.4 4.6 %all-to-all-start.1 = ((bf16[8,2,64,2048]{3,2,1,0:T(8,128)(2,1)}), bf16[8,2,64,2048]{3,2,1,0:T(8,128)(2,1)}, u32[]{:S(2)}, u32[]{:S(2)}) async-start(bf16[8,2,64,2048]{3,2,1,0:T(8,128)(2,1)} %shard_map.124.refs_0_), calls=%async_computation.1 | async-start | bytes 8388608 | tf_op jit(solution)/shard_map/all_to_all | solution.py:449
  104.6 2.4 %collective-permute-done.12.dp_ref = bf16[1024,512]{1,0:T(8,128)(2,1)S(1)} collective-permute-done((bf16[1024,512]{1,0:T(8,128)(2,1)}, bf16[1024,512]{1,0:T(8,128)(2,1)S(1)}, u32[]{:S(2)}, u32[]{:S(2)}) %collective-permute-start.12) | collective-permute-done | bytes 1048608 | tf_op jit(solution)/shard_map/ppermute | solution.py:427
  106.9 1.5 collective-permute-done.11.xp_ref
  110.4 6.8 %shard_map.126 = (bf16[3,128,1024]{2,1,0:T(8,128)(2,1)}, bf16[3,128,1024]{2,1,0:T(8,128)(2,1)}, bf16[3,64,1024]{2,1,0:T(8,128)(2,1)}, bf16[3,64,1024]{2,1,0:T(8,128)(2,1)}, bf16[3,128,1024]{2,1,0:T(8,128)(2,1)}) custom-call(bf16[1024,512]{1,0:T(8,128)(2,1)} %get-tuple-element.70.xo_ref, bf16[1024,512]{1,0:T(8,128)(2,1)} %copy-done.16, ...), custom_call_target="tpu_custom_call" | custom-call | flops 3221225472 | bytes 14680064 | tf_op jit(solution)/shard_map/pallas_call | solution.py:59
  118.5 1.5 collective-permute-start.15
  120.0 6.9 %shard_map.127 = (bf16[3,128,1024]{2,1,0:T(8,128)(2,1)}, bf16[3,128,1024]{2,1,0:T(8,128)(2,1)}, bf16[3,64,1024]{2,1,0:T(8,128)(2,1)}, bf16[3,64,1024]{2,1,0:T(8,128)(2,1)}, bf16[3,128,1024]{2,1,0:T(8,128)(2,1)}) custom-call(bf16[1024,512]{1,0:T(8,128)(2,1)} %get-tuple-element.70.xo_ref, bf16[1024,512]{1,0:T(8,128)(2,1)} %copy-done.16, ...), custom_call_target="tpu_custom_call" | custom-call | flops 3221225472 | bytes 11272192 | tf_op jit(solution)/shard_map/pallas_call | solution.py:59
  127.0 2.4 %collective-permute-done.14.up_ref = bf16[3,64,1024]{2,1,0:T(8,128)(2,1)S(1)} collective-permute-done((bf16[3,64,1024]{2,1,0:T(8,128)(2,1)}, bf16[3,64,1024]{2,1,0:T(8,128)(2,1)S(1)}, u32[]{:S(2)}, u32[]{:S(2)}) %collective-permute-start.14) | collective-permute-done | bytes 393248 | tf_op jit(solution)/shard_map/ppermute | solution.py:476
  132.0 1.8 collective-permute-start.17
  133.8 2.7 %collective-permute-start.19 = (bf16[3,64,1024]{2,1,0:T(8,128)(2,1)}, bf16[3,64,1024]{2,1,0:T(8,128)(2,1)S(1)}, u32[]{:S(2)}, u32[]{:S(2)}) collective-permute-start(bf16[3,64,1024]{2,1,0:T(8,128)(2,1)} %get-tuple-element.83), channel_id=1, source_target_pairs={{0,6},{1,7},{2,0},{3,1},{4,2},{5,3},{6,4},{7,5},{8,14},{9,15},{10,... | collective-permute-start | bytes 1179656 | tf_op jit(solution)/shard_map/ppermute | solution.py:476
  136.4 22.6 %collective-permute-done.18.refs_0_ = bf16[3,64,1024]{2,1,0:T(8,128)(2,1)S(1)} collective-permute-done((bf16[3,64,1024]{2,1,0:T(8,128)(2,1)}, bf16[3,64,1024]{2,1,0:T(8,128)(2,1)S(1)}, u32[]{:S(2)}, u32[]{:S(2)}) %collective-permute-start.18) | collective-permute-done | bytes 393248 | tf_op jit(solution)/shard_map/ppermute | solution.py:476
  161.3 1.8 shard_map.129
  163.1 2.7 %collective-permute-start.21 = (bf16[3,128,1024]{2,1,0:T(8,128)(2,1)}, bf16[3,128,1024]{2,1,0:T(8,128)(2,1)S(1)}, u32[]{:S(2)}, u32[]{:S(2)}) collective-permute-start(bf16[3,128,1024]{2,1,0:T(8,128)(2,1)} %get-tuple-element.87), channel_id=1, source_target_pairs={{0,6},{1,7},{2,0},{3,1},{4,2},{5,3},{6,4},{7,5},{8,14},{9,15},{10,... | collective-permute-start | bytes 2359304 | tf_op jit(solution)/shard_map/ppermute | solution.py:476
  166.9 4.3 %shard_map.125 = (bf16[128,2048]{1,0:T(8,128)(2,1)}, bf16[128,2048]{1,0:T(8,128)(2,1)}, f32[128,2]{1,0:T(8,128)S(1)}) custom-call(s32[2,128]{1,0:T(2,128)S(1)} %bitcast.9, f32[128,2]{1,0:T(8,128)S(1)} %copy.13.gates_ref, bf16[128,2048]{1,0:T(8,128)(2,1)S(1)} %copy-done.2, bf16[8,2,64,2048]{3,2,1,0:T(8,128)(2,1)} %all-to-all-done.1.rows_ref), custom_call_target="tpu_custom_call" | custom-call | flops 805306368 | bytes 4720640 | tf_op jit(solution)/shard_map/pallas_call | solution.py:59
  171.9 10.0 %collective-permute-done.20.refs_1_ = bf16[3,128,1024]{2,1,0:T(8,128)(2,1)S(1)} collective-permute-done((bf16[3,128,1024]{2,1,0:T(8,128)(2,1)}, bf16[3,128,1024]{2,1,0:T(8,128)(2,1)S(1)}, u32[]{:S(2)}, u32[]{:S(2)}) %collective-permute-start.20) | collective-permute-done | bytes 786464 | tf_op jit(solution)/shard_map/ppermute | solution.py:476
  182.9 2.4 %shard_map.130 = (f32[1,128,1024]{2,1,0:T(8,128)}, f32[1,128,1024]{2,1,0:T(8,128)}, f32[1,128,1024]{2,1,0:T(8,128)}) custom-call(bf16[3,128,1024]{2,1,0:T(8,128)(2,1)S(1)} %copy-done.1, bf16[3,128,1024]{2,1,0:T(8,128)(2,1)S(1)} %collective-permute-done.20.refs_1_, bf16[3,128,1024]{2,1,0:T(8,128)(2,1)S(1)} %collective-permute-done.21.refs_2_, ...), custom_call_target="tpu_custom_call" | custom-call | bytes 3145728 | tf_op jit(solution)/shard_map/pallas_call | solution.py:59
  (89 shorter events, 24.0 us)
Async XLA Ops:
  4.3 19.4 %all-to-all-start = ((bf16[16,128,128]{2,1,0:T(8,128)(2,1)}), bf16[16,128,128]{2,1,0:T(8,128)(2,1)S(1)}, u32[]{:S(2)}, u32[]{:S(2)}) async-start(bf16[16,128,128]{2,1,0:T(8,128)(2,1)} %bitcast.10), calls=%async_computation | async-start | bytes 1048576 | tf_op jit(solution)/shard_map/all_to_all | solution.py:384
  11.5 22.1 %collective-permute-start = (bf16[128,2176]{1,0:T(8,128)(2,1)}, bf16[128,2176]{1,0:T(8,128)(2,1)S(1)}, u32[]{:S(2)}, u32[]{:S(2)}) collective-permute-start(bf16[128,2176]{1,0:T(8,128)(2,1)} %get-tuple-element.50), channel_id=1, source_target_pairs={{0,16},{16,0},{32,48},{48,32},{64,80},{80,64},{96,112},{112,96},{1... | collective-permute-start | bytes 1671176 | tf_op jit(solution)/shard_map/ppermute | solution.py:383
  14.8 9.0 %collective-permute-start.1 = (bf16[64,2048]{1,0:T(8,128)(2,1)}, bf16[64,2048]{1,0:T(8,128)(2,1)S(1)}, u32[]{:S(2)}, u32[]{:S(2)}) collective-permute-start(bf16[64,2048]{1,0:T(8,128)(2,1)} %get-tuple-element.53), channel_id=1, source_target_pairs={{0,32},{16,48},{32,64},{48,80},{64,96},{80,112},{96,0},{112,16},{1... | collective-permute-start | bytes 786440 | tf_op jit(solution)/shard_map/ppermute | solution.py:389
  23.8 29.6 %copy-start.8 = (bf16[64,2048]{1,0:T(8,128)(2,1)}, bf16[64,2048]{1,0:T(8,128)(2,1)S(1)}, u32[]{:S(2)}) copy-start(bf16[64,2048]{1,0:T(8,128)(2,1)S(1)} %collective-permute-done.1._.refs_1_) | copy-start | bytes 786436
  23.8 21.0 %collective-permute-start.2 = (bf16[16,128,128]{2,1,0:T(8,128)(2,1)S(1)}, bf16[16,128,128]{2,1,0:T(8,128)(2,1)S(1)}, u32[]{:S(2)}, u32[]{:S(2)}) collective-permute-start(bf16[16,128,128]{2,1,0:T(8,128)(2,1)S(1)} %shard_map.120.slices_o_ref), channel_id=1, source_target_pairs={{0,16},{16,0},{32,48},{48,32},{64,80},{80,64},{96,112},{112,96},{1... | collective-permute-start | bytes 1572872 | tf_op jit(solution)/shard_map/ppermute | solution.py:393
  24.8 24.4 %collective-permute-start.6 = (bf16[64,2048]{1,0:T(8,128)(2,1)}, bf16[64,2048]{1,0:T(8,128)(2,1)S(1)}, u32[]{:S(2)}, u32[]{:S(2)}) collective-permute-start(bf16[64,2048]{1,0:T(8,128)(2,1)} %get-tuple-element.60), channel_id=1, source_target_pairs={{0,64},{16,80},{32,96},{48,112},{64,0},{80,16},{96,32},{112,48},{1... | collective-permute-start | bytes 786440 | tf_op jit(solution)/shard_map/ppermute | solution.py:389
  27.7 21.6 %collective-permute-start.7 = (bf16[64,2048]{1,0:T(8,128)(2,1)}, bf16[64,2048]{1,0:T(8,128)(2,1)S(1)}, u32[]{:S(2)}, u32[]{:S(2)}) collective-permute-start(bf16[64,2048]{1,0:T(8,128)(2,1)} %get-tuple-element.61), channel_id=1, source_target_pairs={{0,96},{16,112},{32,0},{48,16},{64,32},{80,48},{96,64},{112,80},{1... | collective-permute-start | bytes 786440 | tf_op jit(solution)/shard_map/ppermute | solution.py:389
  35.4 15.6 %collective-permute-start.8 = (bf16[64,2048]{1,0:T(8,128)(2,1)S(1)}, bf16[64,2048]{1,0:T(8,128)(2,1)S(1)}, u32[]{:S(2)}, u32[]{:S(2)}) collective-permute-start(bf16[64,2048]{1,0:T(8,128)(2,1)S(1)} %get-tuple-element.62), channel_id=1, source_target_pairs={{0,32},{16,48},{32,64},{48,80},{64,96},{80,112},{96,0},{112,16},{1... | collective-permute-start | bytes 786440 | tf_op jit(solution)/shard_map/ppermute | solution.py:389
  36.8 16.6 %collective-permute-start.9 = (bf16[64,2048]{1,0:T(8,128)(2,1)S(1)}, bf16[64,2048]{1,0:T(8,128)(2,1)S(1)}, u32[]{:S(2)}, u32[]{:S(2)}) collective-permute-start(bf16[64,2048]{1,0:T(8,128)(2,1)S(1)} %get-tuple-element.63), channel_id=1, source_target_pairs={{0,64},{16,80},{32,96},{48,112},{64,0},{80,16},{96,32},{112,48},{1... | collective-permute-start | bytes 786440 | tf_op jit(solution)/shard_map/ppermute | solution.py:389
  44.8 8.5 %collective-permute-start.10 = (bf16[64,2048]{1,0:T(8,128)(2,1)S(1)}, bf16[64,2048]{1,0:T(8,128)(2,1)S(1)}, u32[]{:S(2)}, u32[]{:S(2)}) collective-permute-start(bf16[64,2048]{1,0:T(8,128)(2,1)S(1)} %get-tuple-element.64), channel_id=1, source_target_pairs={{0,96},{16,112},{32,0},{48,16},{64,32},{80,48},{96,64},{112,80},{1... | collective-permute-start | bytes 786440 | tf_op jit(solution)/shard_map/ppermute | solution.py:389
  49.2 26.1 %copy-start.13 = (bf16[128,2048]{1,0:T(8,128)(2,1)}, bf16[128,2048]{1,0:T(8,128)(2,1)S(1)}, u32[]{:S(2)}) copy-start(bf16[128,2048]{1,0:T(8,128)(2,1)S(1)} %get-tuple-element.55.refs_0_) | copy-start | bytes 1572868
  49.2 14.9 %collective-permute-start.3 = (bf16[128,2048]{1,0:T(8,128)(2,1)S(1)}, bf16[128,2048]{1,0:T(8,128)(2,1)S(1)}, u32[]{:S(2)}, u32[]{:S(2)}) collective-permute-start(bf16[128,2048]{1,0:T(8,128)(2,1)S(1)} %get-tuple-element.56), channel_id=1, source_target_pairs={{0,32},{16,48},{32,64},{48,80},{64,96},{80,112},{96,0},{112,16},{1... | collective-permute-start | bytes 1572872 | tf_op jit(solution)/shard_map/ppermute | solution.py:389
  49.3 24.0 %collective-permute-start.4 = (bf16[128,2048]{1,0:T(8,128)(2,1)S(1)}, bf16[128,2048]{1,0:T(8,128)(2,1)S(1)}, u32[]{:S(2)}, u32[]{:S(2)}) collective-permute-start(bf16[128,2048]{1,0:T(8,128)(2,1)S(1)} %get-tuple-element.57), channel_id=1, source_target_pairs={{0,64},{16,80},{32,96},{48,112},{64,0},{80,16},{96,32},{112,48},{1... | collective-permute-start | bytes 1572872 | tf_op jit(solution)/shard_map/ppermute | solution.py:389
  51.0 24.3 %collective-permute-start.5 = (bf16[128,2048]{1,0:T(8,128)(2,1)S(1)}, bf16[128,2048]{1,0:T(8,128)(2,1)S(1)}, u32[]{:S(2)}, u32[]{:S(2)}) collective-permute-start(bf16[128,2048]{1,0:T(8,128)(2,1)S(1)} %get-tuple-element.58), channel_id=1, source_target_pairs={{0,96},{16,112},{32,0},{48,16},{64,32},{80,48},{96,64},{112,80},{1... | collective-permute-start | bytes 1572872 | tf_op jit(solution)/shard_map/ppermute | solution.py:389
  86.3 22.2 %collective-permute-start.13 = (bf16[3,512,1024]{2,1,0:T(8,128)(2,1)}, bf16[3,512,1024]{2,1,0:T(8,128)(2,1)S(1)}, u32[]{:S(2)}, u32[]{:S(2)}) collective-permute-start(bf16[3,512,1024]{2,1,0:T(8,128)(2,1)} %get-tuple-element.66.hid_ref.ho_ref), channel_id=1, source_target_pairs={{0,1},{1,0},{2,3},{3,2},{4,5},{5,4},{6,7},{7,6},{8,9},{9,8},{10,11... | collective-permute-start | bytes 9437192 | tf_op jit(solution)/shard_map/ppermute | solution.py:438
  99.4 67.5 %all-to-all-start.1 = ((bf16[8,2,64,2048]{3,2,1,0:T(8,128)(2,1)}), bf16[8,2,64,2048]{3,2,1,0:T(8,128)(2,1)}, u32[]{:S(2)}, u32[]{:S(2)}) async-start(bf16[8,2,64,2048]{3,2,1,0:T(8,128)(2,1)} %shard_map.124.refs_0_), calls=%async_computation.1 | async-start | bytes 8388608 | tf_op jit(solution)/shard_map/all_to_all | solution.py:449
  104.0 3.0 %collective-permute-start.12 = (bf16[1024,512]{1,0:T(8,128)(2,1)}, bf16[1024,512]{1,0:T(8,128)(2,1)S(1)}, u32[]{:S(2)}, u32[]{:S(2)}) collective-permute-start(bf16[1024,512]{1,0:T(8,128)(2,1)} %get-tuple-element.73), channel_id=1, source_target_pairs={{0,1},{1,0},{2,3},{3,2},{4,5},{5,4},{6,7},{7,6},{8,9},{9,8},{10,11... | collective-permute-start | bytes 3145736 | tf_op jit(solution)/shard_map/ppermute | solution.py:427
  104.2 4.2 %collective-permute-start.11 = (bf16[1024,512]{1,0:T(8,128)(2,1)}, bf16[1024,512]{1,0:T(8,128)(2,1)S(1)}, u32[]{:S(2)}, u32[]{:S(2)}) collective-permute-start(bf16[1024,512]{1,0:T(8,128)(2,1)} %get-tuple-element.71), channel_id=1, source_target_pairs={{0,1},{1,0},{2,3},{3,2},{4,5},{5,4},{6,7},{7,6},{8,9},{9,8},{10,11... | collective-permute-start | bytes 3145736 | tf_op jit(solution)/shard_map/ppermute | solution.py:439
  117.3 12.1 %collective-permute-start.14 = (bf16[3,64,1024]{2,1,0:T(8,128)(2,1)}, bf16[3,64,1024]{2,1,0:T(8,128)(2,1)S(1)}, u32[]{:S(2)}, u32[]{:S(2)}) collective-permute-start(bf16[3,64,1024]{2,1,0:T(8,128)(2,1)} %get-tuple-element.76), channel_id=1, source_target_pairs={{0,2},{1,3},{2,4},{3,5},{4,6},{5,7},{6,0},{7,1},{8,10},{9,11},{10,... | collective-permute-start | bytes 1179656 | tf_op jit(solution)/shard_map/ppermute | solution.py:476
  118.5 10.9 %collective-permute-start.15 = (bf16[3,64,1024]{2,1,0:T(8,128)(2,1)}, bf16[3,64,1024]{2,1,0:T(8,128)(2,1)S(1)}, u32[]{:S(2)}, u32[]{:S(2)}) collective-permute-start(bf16[3,64,1024]{2,1,0:T(8,128)(2,1)} %get-tuple-element.77), channel_id=1, source_target_pairs={{0,6},{1,7},{2,0},{3,1},{4,2},{5,3},{6,4},{7,5},{8,14},{9,15},{10,... | collective-permute-start | bytes 1179656 | tf_op jit(solution)/shard_map/ppermute | solution.py:476
  120.0 39.0 %copy-start.3 = (bf16[3,128,1024]{2,1,0:T(8,128)(2,1)S(1)}, bf16[3,128,1024]{2,1,0:T(8,128)(2,1)}, u32[]{:S(2)}) copy-start(bf16[3,128,1024]{2,1,0:T(8,128)(2,1)} %get-tuple-element.74.refs_0_.own_ref) | copy-start | bytes 2359300
  120.0 46.9 %copy-start.2 = (bf16[128,2048]{1,0:T(8,128)(2,1)S(1)}, bf16[128,2048]{1,0:T(8,128)(2,1)}, u32[]{:S(2)}) copy-start(bf16[128,2048]{1,0:T(8,128)(2,1)} %cot_ref.3) | copy-start | bytes 1572868
  127.0 39.8 %copy-start.17 = (f32[128,2]{0,1:T(2,128)S(1)}, f32[128,2]{0,1:T(2,128)}, u32[]{:S(2)}) copy-start(f32[128,2]{0,1:T(2,128)} %param.10) | copy-start | bytes 3076
  127.0 39.9 %copy-start.10 = (s32[128,2]{0,1:T(2,128)S(1)}, s32[128,2]{0,1:T(2,128)}, u32[]{:S(2)}) copy-start(s32[128,2]{0,1:T(2,128)} %param.9) | copy-start | bytes 3076
  130.8 28.2 %collective-permute-start.16 = (bf16[3,128,1024]{2,1,0:T(8,128)(2,1)S(1)}, bf16[3,128,1024]{2,1,0:T(8,128)(2,1)S(1)}, u32[]{:S(2)}, u32[]{:S(2)}) collective-permute-start(bf16[3,128,1024]{2,1,0:T(8,128)(2,1)S(1)} %get-tuple-element.80), channel_id=1, source_target_pairs={{0,2},{1,3},{2,4},{3,5},{4,6},{5,7},{6,0},{7,1},{8,10},{9,11},{10,... | collective-permute-start | bytes 2359304 | tf_op jit(solution)/shard_map/ppermute | solution.py:476
  132.0 27.1 %collective-permute-start.17 = (bf16[3,128,1024]{2,1,0:T(8,128)(2,1)S(1)}, bf16[3,128,1024]{2,1,0:T(8,128)(2,1)S(1)}, u32[]{:S(2)}, u32[]{:S(2)}) collective-permute-start(bf16[3,128,1024]{2,1,0:T(8,128)(2,1)S(1)} %get-tuple-element.81), channel_id=1, source_target_pairs={{0,6},{1,7},{2,0},{3,1},{4,2},{5,3},{6,4},{7,5},{8,14},{9,15},{10,... | collective-permute-start | bytes 2359304 | tf_op jit(solution)/shard_map/ppermute | solution.py:476
  133.8 25.2 %collective-permute-start.18 = (bf16[3,64,1024]{2,1,0:T(8,128)(2,1)}, bf16[3,64,1024]{2,1,0:T(8,128)(2,1)S(1)}, u32[]{:S(2)}, u32[]{:S(2)}) collective-permute-start(bf16[3,64,1024]{2,1,0:T(8,128)(2,1)} %get-tuple-element.82), channel_id=1, source_target_pairs={{0,2},{1,3},{2,4},{3,5},{4,6},{5,7},{6,0},{7,1},{8,10},{9,11},{10,... | collective-permute-start | bytes 1179656 | tf_op jit(solution)/shard_map/ppermute | solution.py:476
  133.8 25.2 %collective-permute-start.19 = (bf16[3,64,1024]{2,1,0:T(8,128)(2,1)}, bf16[3,64,1024]{2,1,0:T(8,128)(2,1)S(1)}, u32[]{:S(2)}, u32[]{:S(2)}) collective-permute-start(bf16[3,64,1024]{2,1,0:T(8,128)(2,1)} %get-tuple-element.83), channel_id=1, source_target_pairs={{0,6},{1,7},{2,0},{3,1},{4,2},{5,3},{6,4},{7,5},{8,14},{9,15},{10,... | collective-permute-start | bytes 1179656 | tf_op jit(solution)/shard_map/ppermute | solution.py:476
  161.3 21.6 %copy-start.1 = (bf16[3,128,1024]{2,1,0:T(8,128)(2,1)S(1)}, bf16[3,128,1024]{2,1,0:T(8,128)(2,1)}, u32[]{:S(2)}) copy-start(bf16[3,128,1024]{2,1,0:T(8,128)(2,1)} %get-tuple-element.75.refs_0_) | copy-start | bytes 2359300
  163.1 18.8 %collective-permute-start.20 = (bf16[3,128,1024]{2,1,0:T(8,128)(2,1)}, bf16[3,128,1024]{2,1,0:T(8,128)(2,1)S(1)}, u32[]{:S(2)}, u32[]{:S(2)}) collective-permute-start(bf16[3,128,1024]{2,1,0:T(8,128)(2,1)} %get-tuple-element.86), channel_id=1, source_target_pairs={{0,2},{1,3},{2,4},{3,5},{4,6},{5,7},{6,0},{7,1},{8,10},{9,11},{10,... | collective-permute-start | bytes 2359304 | tf_op jit(solution)/shard_map/ppermute | solution.py:476
  163.1 18.8 %collective-permute-start.21 = (bf16[3,128,1024]{2,1,0:T(8,128)(2,1)}, bf16[3,128,1024]{2,1,0:T(8,128)(2,1)S(1)}, u32[]{:S(2)}, u32[]{:S(2)}) collective-permute-start(bf16[3,128,1024]{2,1,0:T(8,128)(2,1)} %get-tuple-element.87), channel_id=1, source_target_pairs={{0,6},{1,7},{2,0},{3,1},{4,2},{5,3},{6,4},{7,5},{8,14},{9,15},{10,... | collective-permute-start | bytes 2359304 | tf_op jit(solution)/shard_map/ppermute | solution.py:476
  165.8 17.1 %collective-permute-start.22 = (bf16[3,128,1024]{2,1,0:T(8,128)(2,1)}, bf16[3,128,1024]{2,1,0:T(8,128)(2,1)}, u32[]{:S(2)}, u32[]{:S(2)}) collective-permute-start(bf16[3,128,1024]{2,1,0:T(8,128)(2,1)} %get-tuple-element.88), channel_id=1, source_target_pairs={{0,8},{1,9},{2,10},{3,11},{4,12},{5,13},{6,14},{7,15},{8,0},{9,1},... | collective-permute-start | bytes 2359304 | tf_op jit(solution)/shard_map/ppermute | solution.py:487
  (19 other events, 72.3 us)

commit v4 on v3

--- a/solution.py
+++ b/solution.py
@@ -133,10 +133,9 @@
         out_ref[...] = picked[e * cap : (e + 1) * cap, :]
 
 
-def own_kernel(cap, at_ref, routes_ref, gates_ref, cot_ref, ck_ref, code_ref, wide_ref, ck_out_ref, *out_refs):
+def own_kernel(cap, at_ref, routes_ref, gates_ref, cot_ref, code_ref, wide_ref, *out_refs):
     features = cot_ref.shape[1]
     wide_ref[:, 0:features] = cot_ref[...]
-    ck_out_ref[...] = ck_ref[...]
     gates = gates_ref[...]
     pieces, rest = [routes_ref[...].astype(F32)], gates
     for _ in range(3):
@@ -366,23 +365,22 @@
 
     routes_t, gates_t = routes.T, gates.T
     at = jnp.stack([y, z]).astype(jnp.int32)
-    code_o, wide, slices, *packed = call(
+    code_o, wide, *packed = call(
         functools.partial(own_kernel, cap),
         [
             struct(2, tokens, dtype=jnp.int32),
             struct(tokens, features + tokens),
-            struct(*checkpoint.shape),
             *[struct(cap, features)] * Y,
         ],
-        [at, routes_t, gates_t, cotangent, checkpoint],
+        [at, routes_t, gates_t, cotangent],
         2 * Y * cap * tokens * features,
-        in_specs=[SMEM] + [None] * 4,
+        in_specs=[SMEM] + [None] * 3,
         vmem=56,
         blocks=True,
     )
     wide = lax.ppermute(wide, "ep", EP_SWAP)
     slices = lax.all_to_all(
-        slices.reshape(dp, tokens, features // dp), "dp", split_axis=0, concat_axis=0, tiled=True
+        checkpoint.reshape(dp, tokens, features // dp), "dp", split_axis=0, concat_axis=0, tiled=True
     )
 
     def to_experts(packed):

time: 188 us -> 185 us (0.984)
  transfers between devices with their start and end apart: 25 -> 25, of which waited for: 12 -> 12; matrix products, arithmetic and copies ran while one was open for 1% -> 1% of each run, Pallas kernels for 22% -> 23%
where the time goes in v4:
time: 185 us; the launch traced here: 183 us
  waiting for transfers between devices  71.9 us (39%)
  Pallas kernels  55.5 us (30%)
  starting transfers between devices  43.9 us (24%)
  local copies, waits for them, and re-layouts  9.03 us (5%)
    pallas_call x13, Pallas kernels, call(): pl.pallas_call(body, grid=(1,) if blocks else (), in_specs=[s or whole(a)...  55.5 us
    ppermute x8, waiting for transfers between devices, shift(): return lax.ppermute(array, 'dp', x_shift(k))  34.9 us
    ppermute x9, waiting for transfers between devices, to_experts(): lax.ppermute(packed[k], 'ep', y_shift(k))  22.2 us
    ppermute x9, starting transfers between devices, to_experts(): lax.ppermute(packed[k], 'ep', y_shift(k))  13.3 us
    ppermute x8, starting transfers between devices, shift(): return lax.ppermute(array, 'dp', x_shift(k))  11.1 us
    unnamed x54, local copies, waits for them, and re-layouts  9.03 us
    all_to_all x1, starting transfers between devices, shards(): lax.all_to_all(checkpoint.reshape(dp, tokens, features // dp), 'dp', spli...  7.18 us
    all_to_all x1, starting transfers between devices, shards(): back = lax.all_to_all(outs, 'ep', split_axis=0, concat_axis=0, tiled=True)  5.64 us
  transfers between devices with their start and end apart: 25, of which 12 were waited for; matrix products, arithmetic and copies ran while one was open for 1% of the time, Pallas kernels for 23%

profile of v4, /device:TPU:1, one launch (start us, length us, event | category | flops | bytes accessed | tf_op | source)
XLA Modules:
  0.0 182.9 jit_solution(10648602702490587681)
XLA Ops:
  0.6 7.2 %all-to-all-start = ((bf16[16,128,128]{2,1,0:T(8,128)(2,1)}), bf16[16,128,128]{2,1,0:T(8,128)(2,1)S(1)}, u32[]{:S(2)}, u32[]{:S(2)}) async-start(bf16[16,128,128]{2,1,0:T(8,128)(2,1)} %bitcast.10), calls=%async_computation | async-start | bytes 1048576 | tf_op jit(solution)/shard_map/all_to_all | solution.py:382
  8.4 2.8 %shard_map.118 = (s32[2,128]{1,0:T(2,128)}, bf16[128,2176]{1,0:T(8,128)(2,1)}, bf16[64,2048]{1,0:T(8,128)(2,1)}, bf16[64,2048]{1,0:T(8,128)(2,1)}, bf16[64,2048]{1,0:T(8,128)(2,1)}, /*index=5*/bf16[64,2048]{1,0:T(8,128)(2,1)}) custom-call(s32[2]{0:T(128)} %pad_add_fusion.at_ref, s32[2,128]{1,0:T(2,128)} %bitcast.8, f32[2,128]{1,0:T(2,128)} %bitcast.11, ...), custom_call_target="tpu_custom_call" | custom-call | flops 134217728 | bytes 526344 | tf_op jit(solution)/shard_map/pallas_call | solution.py:59
  11.2 3.3 %collective-permute-start = (bf16[128,2176]{1,0:T(8,128)(2,1)}, bf16[128,2176]{1,0:T(8,128)(2,1)S(1)}, u32[]{:S(2)}, u32[]{:S(2)}) collective-permute-start(bf16[128,2176]{1,0:T(8,128)(2,1)} %get-tuple-element.49), channel_id=1, source_target_pairs={{0,16},{16,0},{32,48},{48,32},{64,80},{80,64},{96,112},{112,96},{1... | collective-permute-start | bytes 1671176 | tf_op jit(solution)/shard_map/ppermute | solution.py:381
  15.8 7.7 %collective-permute-done.1._.refs_1_ = bf16[64,2048]{1,0:T(8,128)(2,1)S(1)} collective-permute-done((bf16[64,2048]{1,0:T(8,128)(2,1)}, bf16[64,2048]{1,0:T(8,128)(2,1)S(1)}, u32[]{:S(2)}, u32[]{:S(2)}) %collective-permute-start.1) | collective-permute-done | bytes 262176 | tf_op jit(solution)/shard_map/ppermute | solution.py:387
  23.9 1.6 collective-permute-start.6
  26.3 4.5 %collective-permute-done.wide_ref = bf16[128,2176]{1,0:T(8,128)(2,1)S(1)} collective-permute-done((bf16[128,2176]{1,0:T(8,128)(2,1)}, bf16[128,2176]{1,0:T(8,128)(2,1)S(1)}, u32[]{:S(2)}, u32[]{:S(2)}) %collective-permute-start) | collective-permute-done | bytes 557088 | tf_op jit(solution)/shard_map/ppermute | solution.py:381
  33.9 2.6 %collective-permute-start.9 = (bf16[64,2048]{1,0:T(8,128)(2,1)S(1)}, bf16[64,2048]{1,0:T(8,128)(2,1)S(1)}, u32[]{:S(2)}, u32[]{:S(2)}) collective-permute-start(bf16[64,2048]{1,0:T(8,128)(2,1)S(1)} %get-tuple-element.61), channel_id=1, source_target_pairs={{0,64},{16,80},{32,96},{48,112},{64,0},{80,16},{96,32},{112,48},{1... | collective-permute-start | bytes 786440 | tf_op jit(solution)/shard_map/ppermute | solution.py:387
  36.5 5.5 %collective-permute-done.2.slices_p_ref = bf16[16,128,128]{2,1,0:T(8,128)(2,1)S(1)} collective-permute-done((bf16[16,128,128]{2,1,0:T(8,128)(2,1)S(1)}, bf16[16,128,128]{2,1,0:T(8,128)(2,1)S(1)}, u32[]{:S(2)}, u32[]{:S(2)}) %collective-permute-start.2) | collective-permute-done | bytes 524320 | tf_op jit(solution)/shard_map/ppermute | solution.py:391
  42.0 2.7 %collective-permute-start.10 = (bf16[64,2048]{1,0:T(8,128)(2,1)S(1)}, bf16[64,2048]{1,0:T(8,128)(2,1)S(1)}, u32[]{:S(2)}, u32[]{:S(2)}) collective-permute-start(bf16[64,2048]{1,0:T(8,128)(2,1)S(1)} %get-tuple-element.62), channel_id=1, source_target_pairs={{0,96},{16,112},{32,0},{48,16},{64,32},{80,48},{96,64},{112,80},{1... | collective-permute-start | bytes 786440 | tf_op jit(solution)/shard_map/ppermute | solution.py:387
  46.5 1.6 collective-permute-start.4
  51.3 6.6 %shard_map.122 = (f32[512,1024]{1,0:T(8,128)}, bf16[1024,512]{1,0:T(8,128)(2,1)}, bf16[1024,512]{1,0:T(8,128)(2,1)}) custom-call(s32[8]{0:T(128)} %fusion.5.at_ref, s32[16]{0:T(128)} %fusion.3.start_ref, bf16[64,2048]{1,0:T(8,128)(2,1)} %get-tuple-element.57.refs_0_, bf16[64,2048]{1,0:T(8,128)(2,1)} %copy-done.8, bf16[64,2048]{1,0:T(8,128)(2,1)} %copy-done.21, ...), custom_call_target="tpu_custom_call" | custom-call | flops 2147483648 | bytes 6291552 | tf_op jit(solution)/shard_map/pallas_call | solution.py:59
  57.9 3.5 %collective-permute-done.3.refs_1_ = bf16[128,2048]{1,0:T(8,128)(2,1)S(1)} collective-permute-done((bf16[128,2048]{1,0:T(8,128)(2,1)S(1)}, bf16[128,2048]{1,0:T(8,128)(2,1)S(1)}, u32[]{:S(2)}, u32[]{:S(2)}) %collective-permute-start.3) | collective-permute-done | bytes 524320 | tf_op jit(solution)/shard_map/ppermute | solution.py:387
  61.4 9.2 %collective-permute-done.4.refs_2_ = bf16[128,2048]{1,0:T(8,128)(2,1)S(1)} collective-permute-done((bf16[128,2048]{1,0:T(8,128)(2,1)S(1)}, bf16[128,2048]{1,0:T(8,128)(2,1)S(1)}, u32[]{:S(2)}, u32[]{:S(2)}) %collective-permute-start.4) | collective-permute-done | bytes 524320 | tf_op jit(solution)/shard_map/ppermute | solution.py:387
  70.6 1.8 collective-permute-done.5.refs_3_
  73.2 10.2 %shard_map.123 = (bf16[3,512,1024]{2,1,0:T(8,128)(2,1)}, bf16[1024,512]{1,0:T(8,128)(2,1)}, bf16[1024,512]{1,0:T(8,128)(2,1)}) custom-call(s32[8]{0:T(128)} %fusion.5.at_ref, s32[16]{0:T(128)} %fusion.3.start_ref, bf16[128,2048]{1,0:T(8,128)(2,1)} %copy-done.13, bf16[128,2048]{1,0:T(8,128)(2,1)} %copy-done.18, bf16[128,2048]{1,0:T(8,128)(2,1)} %copy-done.19, ...), custom_call_target="tpu_custom_call" | custom-call | flops 4294967296 | bytes 12583008 | tf_op jit(solution)/shard_map/pallas_call | solution.py:59
  83.4 1.8 collective-permute-start.13
  85.1 11.4 %shard_map.124.refs_0_ = bf16[8,2,64,2048]{3,2,1,0:T(8,128)(2,1)} custom-call(bf16[3,512,1024]{2,1,0:T(8,128)(2,1)} %get-tuple-element.64.hid_ref.ho_ref, bf16[2048,1024]{1,0:T(8,128)(2,1)} %bitcast.17, bf16[2048,1024]{1,0:T(8,128)(2,1)} %bitcast.13, bf16[2048,1024]{1,0:T(8,128)(2,1)} %bitcast.15), custom_call_target="tpu_custom_call" | custom-call | flops 6442450944 | bytes 15728640 | tf_op jit(solution)/shard_map/pallas_call | solution.py:59
  96.5 5.6 %all-to-all-start.1 = ((bf16[8,2,64,2048]{3,2,1,0:T(8,128)(2,1)}), bf16[8,2,64,2048]{3,2,1,0:T(8,128)(2,1)}, u32[]{:S(2)}, u32[]{:S(2)}) async-start(bf16[8,2,64,2048]{3,2,1,0:T(8,128)(2,1)} %shard_map.124.refs_0_), calls=%async_computation.1 | async-start | bytes 8388608 | tf_op jit(solution)/shard_map/all_to_all | solution.py:447
  102.7 2.4 %collective-permute-done.12.dp_ref = bf16[1024,512]{1,0:T(8,128)(2,1)S(1)} collective-permute-done((bf16[1024,512]{1,0:T(8,128)(2,1)}, bf16[1024,512]{1,0:T(8,128)(2,1)S(1)}, u32[]{:S(2)}, u32[]{:S(2)}) %collective-permute-start.12) | collective-permute-done | bytes 1048608 | tf_op jit(solution)/shard_map/ppermute | solution.py:425
  105.0 1.5 collective-permute-done.11.xp_ref
  108.6 6.8 %shard_map.126 = (bf16[3,128,1024]{2,1,0:T(8,128)(2,1)}, bf16[3,128,1024]{2,1,0:T(8,128)(2,1)}, bf16[3,64,1024]{2,1,0:T(8,128)(2,1)}, bf16[3,64,1024]{2,1,0:T(8,128)(2,1)}, bf16[3,128,1024]{2,1,0:T(8,128)(2,1)}) custom-call(bf16[1024,512]{1,0:T(8,128)(2,1)} %get-tuple-element.68.xo_ref, bf16[1024,512]{1,0:T(8,128)(2,1)} %copy-done.16, ...), custom_call_target="tpu_custom_call" | custom-call | flops 3221225472 | bytes 14680064 | tf_op jit(solution)/shard_map/pallas_call | solution.py:59
  116.5 1.7 collective-permute-start.15
  118.1 6.9 %shard_map.127 = (bf16[3,128,1024]{2,1,0:T(8,128)(2,1)}, bf16[3,128,1024]{2,1,0:T(8,128)(2,1)}, bf16[3,64,1024]{2,1,0:T(8,128)(2,1)}, bf16[3,64,1024]{2,1,0:T(8,128)(2,1)}, bf16[3,128,1024]{2,1,0:T(8,128)(2,1)}) custom-call(bf16[1024,512]{1,0:T(8,128)(2,1)} %get-tuple-element.68.xo_ref, bf16[1024,512]{1,0:T(8,128)(2,1)} %copy-done.16, ...), custom_call_target="tpu_custom_call" | custom-call | flops 3221225472 | bytes 11272192 | tf_op jit(solution)/shard_map/pallas_call | solution.py:59
  125.1 2.3 %collective-permute-done.14.up_ref = bf16[3,64,1024]{2,1,0:T(8,128)(2,1)S(1)} collective-permute-done((bf16[3,64,1024]{2,1,0:T(8,128)(2,1)}, bf16[3,64,1024]{2,1,0:T(8,128)(2,1)S(1)}, u32[]{:S(2)}, u32[]{:S(2)}) %collective-permute-start.14) | collective-permute-done | bytes 393248 | tf_op jit(solution)/shard_map/ppermute | solution.py:474
  129.7 2.0 %collective-permute-start.17 = (bf16[3,128,1024]{2,1,0:T(8,128)(2,1)S(1)}, bf16[3,128,1024]{2,1,0:T(8,128)(2,1)S(1)}, u32[]{:S(2)}, u32[]{:S(2)}) collective-permute-start(bf16[3,128,1024]{2,1,0:T(8,128)(2,1)S(1)} %get-tuple-element.79), channel_id=1, source_target_pairs={{0,6},{1,7},{2,0},{3,1},{4,2},{5,3},{6,4},{7,5},{8,14},{9,15},{10,... | collective-permute-start | bytes 2359304 | tf_op jit(solution)/shard_map/ppermute | solution.py:474
  131.7 2.7 %collective-permute-start.19 = (bf16[3,64,1024]{2,1,0:T(8,128)(2,1)}, bf16[3,64,1024]{2,1,0:T(8,128)(2,1)S(1)}, u32[]{:S(2)}, u32[]{:S(2)}) collective-permute-start(bf16[3,64,1024]{2,1,0:T(8,128)(2,1)} %get-tuple-element.81), channel_id=1, source_target_pairs={{0,6},{1,7},{2,0},{3,1},{4,2},{5,3},{6,4},{7,5},{8,14},{9,15},{10,... | collective-permute-start | bytes 1179656 | tf_op jit(solution)/shard_map/ppermute | solution.py:474
  134.4 22.4 %collective-permute-done.18.refs_0_ = bf16[3,64,1024]{2,1,0:T(8,128)(2,1)S(1)} collective-permute-done((bf16[3,64,1024]{2,1,0:T(8,128)(2,1)}, bf16[3,64,1024]{2,1,0:T(8,128)(2,1)S(1)}, u32[]{:S(2)}, u32[]{:S(2)}) %collective-permute-start.18) | collective-permute-done | bytes 393248 | tf_op jit(solution)/shard_map/ppermute | solution.py:474
  159.1 1.8 shard_map.129
  161.1 2.5 %collective-permute-start.21 = (bf16[3,128,1024]{2,1,0:T(8,128)(2,1)}, bf16[3,128,1024]{2,1,0:T(8,128)(2,1)S(1)}, u32[]{:S(2)}, u32[]{:S(2)}) collective-permute-start(bf16[3,128,1024]{2,1,0:T(8,128)(2,1)} %get-tuple-element.85), channel_id=1, source_target_pairs={{0,6},{1,7},{2,0},{3,1},{4,2},{5,3},{6,4},{7,5},{8,14},{9,15},{10,... | collective-permute-start | bytes 2359304 | tf_op jit(solution)/shard_map/ppermute | solution.py:474
  164.4 4.3 %shard_map.125 = (bf16[128,2048]{1,0:T(8,128)(2,1)}, bf16[128,2048]{1,0:T(8,128)(2,1)}, f32[128,2]{1,0:T(8,128)S(1)}) custom-call(s32[2,128]{1,0:T(2,128)S(1)} %bitcast.9, f32[128,2]{1,0:T(8,128)S(1)} %copy.13.gates_ref, bf16[128,2048]{1,0:T(8,128)(2,1)S(1)} %copy-done.2, bf16[8,2,64,2048]{3,2,1,0:T(8,128)(2,1)} %all-to-all-done.1.rows_ref), custom_call_target="tpu_custom_call" | custom-call | flops 805306368 | bytes 4720640 | tf_op jit(solution)/shard_map/pallas_call | solution.py:59
  169.3 10.2 %collective-permute-done.20.refs_1_ = bf16[3,128,1024]{2,1,0:T(8,128)(2,1)S(1)} collective-permute-done((bf16[3,128,1024]{2,1,0:T(8,128)(2,1)}, bf16[3,128,1024]{2,1,0:T(8,128)(2,1)S(1)}, u32[]{:S(2)}, u32[]{:S(2)}) %collective-permute-start.20) | collective-permute-done | bytes 786464 | tf_op jit(solution)/shard_map/ppermute | solution.py:474
  180.5 2.4 %shard_map.130 = (f32[1,128,1024]{2,1,0:T(8,128)}, f32[1,128,1024]{2,1,0:T(8,128)}, f32[1,128,1024]{2,1,0:T(8,128)}) custom-call(bf16[3,128,1024]{2,1,0:T(8,128)(2,1)S(1)} %copy-done.1, bf16[3,128,1024]{2,1,0:T(8,128)(2,1)S(1)} %collective-permute-done.20.refs_1_, bf16[3,128,1024]{2,1,0:T(8,128)(2,1)S(1)} %collective-permute-done.21.refs_2_, ...), custom_call_target="tpu_custom_call" | custom-call | bytes 3145728 | tf_op jit(solution)/shard_map/pallas_call | solution.py:59
  (89 shorter events, 22.7 us)
Async XLA Ops:
  0.6 22.8 %all-to-all-start = ((bf16[16,128,128]{2,1,0:T(8,128)(2,1)}), bf16[16,128,128]{2,1,0:T(8,128)(2,1)S(1)}, u32[]{:S(2)}, u32[]{:S(2)}) async-start(bf16[16,128,128]{2,1,0:T(8,128)(2,1)} %bitcast.10), calls=%async_computation | async-start | bytes 1048576 | tf_op jit(solution)/shard_map/all_to_all | solution.py:382
  11.2 19.6 %collective-permute-start = (bf16[128,2176]{1,0:T(8,128)(2,1)}, bf16[128,2176]{1,0:T(8,128)(2,1)S(1)}, u32[]{:S(2)}, u32[]{:S(2)}) collective-permute-start(bf16[128,2176]{1,0:T(8,128)(2,1)} %get-tuple-element.49), channel_id=1, source_target_pairs={{0,16},{16,0},{32,48},{48,32},{64,80},{80,64},{96,112},{112,96},{1... | collective-permute-start | bytes 1671176 | tf_op jit(solution)/shard_map/ppermute | solution.py:381
  14.5 9.0 %collective-permute-start.1 = (bf16[64,2048]{1,0:T(8,128)(2,1)}, bf16[64,2048]{1,0:T(8,128)(2,1)S(1)}, u32[]{:S(2)}, u32[]{:S(2)}) collective-permute-start(bf16[64,2048]{1,0:T(8,128)(2,1)} %get-tuple-element.51), channel_id=1, source_target_pairs={{0,32},{16,48},{32,64},{48,80},{64,96},{80,112},{96,0},{112,16},{1... | collective-permute-start | bytes 786440 | tf_op jit(solution)/shard_map/ppermute | solution.py:387
  23.5 27.1 %copy-start.8 = (bf16[64,2048]{1,0:T(8,128)(2,1)}, bf16[64,2048]{1,0:T(8,128)(2,1)S(1)}, u32[]{:S(2)}) copy-start(bf16[64,2048]{1,0:T(8,128)(2,1)S(1)} %collective-permute-done.1._.refs_1_) | copy-start | bytes 786436
  23.5 18.5 %collective-permute-start.2 = (bf16[16,128,128]{2,1,0:T(8,128)(2,1)S(1)}, bf16[16,128,128]{2,1,0:T(8,128)(2,1)S(1)}, u32[]{:S(2)}, u32[]{:S(2)}) collective-permute-start(bf16[16,128,128]{2,1,0:T(8,128)(2,1)S(1)} %shard_map.120.slices_o_ref), channel_id=1, source_target_pairs={{0,16},{16,0},{32,48},{48,32},{64,80},{80,64},{96,112},{112,96},{1... | collective-permute-start | bytes 1572872 | tf_op jit(solution)/shard_map/ppermute | solution.py:391
  23.9 22.4 %collective-permute-start.6 = (bf16[64,2048]{1,0:T(8,128)(2,1)}, bf16[64,2048]{1,0:T(8,128)(2,1)S(1)}, u32[]{:S(2)}, u32[]{:S(2)}) collective-permute-start(bf16[64,2048]{1,0:T(8,128)(2,1)} %get-tuple-element.58), channel_id=1, source_target_pairs={{0,64},{16,80},{32,96},{48,112},{64,0},{80,16},{96,32},{112,48},{1... | collective-permute-start | bytes 786440 | tf_op jit(solution)/shard_map/ppermute | solution.py:387
  25.5 21.0 %collective-permute-start.7 = (bf16[64,2048]{1,0:T(8,128)(2,1)}, bf16[64,2048]{1,0:T(8,128)(2,1)S(1)}, u32[]{:S(2)}, u32[]{:S(2)}) collective-permute-start(bf16[64,2048]{1,0:T(8,128)(2,1)} %get-tuple-element.59), channel_id=1, source_target_pairs={{0,96},{16,112},{32,0},{48,16},{64,32},{80,48},{96,64},{112,80},{1... | collective-permute-start | bytes 786440 | tf_op jit(solution)/shard_map/ppermute | solution.py:387
  32.5 15.6 %collective-permute-start.8 = (bf16[64,2048]{1,0:T(8,128)(2,1)S(1)}, bf16[64,2048]{1,0:T(8,128)(2,1)S(1)}, u32[]{:S(2)}, u32[]{:S(2)}) collective-permute-start(bf16[64,2048]{1,0:T(8,128)(2,1)S(1)} %get-tuple-element.60), channel_id=1, source_target_pairs={{0,32},{16,48},{32,64},{48,80},{64,96},{80,112},{96,0},{112,16},{1... | collective-permute-start | bytes 786440 | tf_op jit(solution)/shard_map/ppermute | solution.py:387
  33.9 16.6 %collective-permute-start.9 = (bf16[64,2048]{1,0:T(8,128)(2,1)S(1)}, bf16[64,2048]{1,0:T(8,128)(2,1)S(1)}, u32[]{:S(2)}, u32[]{:S(2)}) collective-permute-start(bf16[64,2048]{1,0:T(8,128)(2,1)S(1)} %get-tuple-element.61), channel_id=1, source_target_pairs={{0,64},{16,80},{32,96},{48,112},{64,0},{80,16},{96,32},{112,48},{1... | collective-permute-start | bytes 786440 | tf_op jit(solution)/shard_map/ppermute | solution.py:387
  42.0 8.5 %collective-permute-start.10 = (bf16[64,2048]{1,0:T(8,128)(2,1)S(1)}, bf16[64,2048]{1,0:T(8,128)(2,1)S(1)}, u32[]{:S(2)}, u32[]{:S(2)}) collective-permute-start(bf16[64,2048]{1,0:T(8,128)(2,1)S(1)} %get-tuple-element.62), channel_id=1, source_target_pairs={{0,96},{16,112},{32,0},{48,16},{64,32},{80,48},{96,64},{112,80},{1... | collective-permute-start | bytes 786440 | tf_op jit(solution)/shard_map/ppermute | solution.py:387
  46.3 26.0 %copy-start.13 = (bf16[128,2048]{1,0:T(8,128)(2,1)}, bf16[128,2048]{1,0:T(8,128)(2,1)S(1)}, u32[]{:S(2)}) copy-start(bf16[128,2048]{1,0:T(8,128)(2,1)S(1)} %get-tuple-element.53.refs_0_) | copy-start | bytes 1572868
  46.4 15.0 %collective-permute-start.3 = (bf16[128,2048]{1,0:T(8,128)(2,1)S(1)}, bf16[128,2048]{1,0:T(8,128)(2,1)S(1)}, u32[]{:S(2)}, u32[]{:S(2)}) collective-permute-start(bf16[128,2048]{1,0:T(8,128)(2,1)S(1)} %get-tuple-element.54), channel_id=1, source_target_pairs={{0,32},{16,48},{32,64},{48,80},{64,96},{80,112},{96,0},{112,16},{1... | collective-permute-start | bytes 1572872 | tf_op jit(solution)/shard_map/ppermute | solution.py:387
  46.5 24.1 %collective-permute-start.4 = (bf16[128,2048]{1,0:T(8,128)(2,1)S(1)}, bf16[128,2048]{1,0:T(8,128)(2,1)S(1)}, u32[]{:S(2)}, u32[]{:S(2)}) collective-permute-start(bf16[128,2048]{1,0:T(8,128)(2,1)S(1)} %get-tuple-element.55), channel_id=1, source_target_pairs={{0,64},{16,80},{32,96},{48,112},{64,0},{80,16},{96,32},{112,48},{1... | collective-permute-start | bytes 1572872 | tf_op jit(solution)/shard_map/ppermute | solution.py:387
  48.1 24.3 %collective-permute-start.5 = (bf16[128,2048]{1,0:T(8,128)(2,1)S(1)}, bf16[128,2048]{1,0:T(8,128)(2,1)S(1)}, u32[]{:S(2)}, u32[]{:S(2)}) collective-permute-start(bf16[128,2048]{1,0:T(8,128)(2,1)S(1)} %get-tuple-element.56), channel_id=1, source_target_pairs={{0,96},{16,112},{32,0},{48,16},{64,32},{80,48},{96,64},{112,80},{1... | collective-permute-start | bytes 1572872 | tf_op jit(solution)/shard_map/ppermute | solution.py:387
  83.4 23.2 %collective-permute-start.13 = (bf16[3,512,1024]{2,1,0:T(8,128)(2,1)}, bf16[3,512,1024]{2,1,0:T(8,128)(2,1)S(1)}, u32[]{:S(2)}, u32[]{:S(2)}) collective-permute-start(bf16[3,512,1024]{2,1,0:T(8,128)(2,1)} %get-tuple-element.64.hid_ref.ho_ref), channel_id=1, source_target_pairs={{0,1},{1,0},{2,3},{3,2},{4,5},{5,4},{6,7},{7,6},{8,9},{9,8},{10,11... | collective-permute-start | bytes 9437192 | tf_op jit(solution)/shard_map/ppermute | solution.py:436
  96.5 67.8 %all-to-all-start.1 = ((bf16[8,2,64,2048]{3,2,1,0:T(8,128)(2,1)}), bf16[8,2,64,2048]{3,2,1,0:T(8,128)(2,1)}, u32[]{:S(2)}, u32[]{:S(2)}) async-start(bf16[8,2,64,2048]{3,2,1,0:T(8,128)(2,1)} %shard_map.124.refs_0_), calls=%async_computation.1 | async-start | bytes 8388608 | tf_op jit(solution)/shard_map/all_to_all | solution.py:447
  102.2 2.9 %collective-permute-start.12 = (bf16[1024,512]{1,0:T(8,128)(2,1)}, bf16[1024,512]{1,0:T(8,128)(2,1)S(1)}, u32[]{:S(2)}, u32[]{:S(2)}) collective-permute-start(bf16[1024,512]{1,0:T(8,128)(2,1)} %get-tuple-element.71), channel_id=1, source_target_pairs={{0,1},{1,0},{2,3},{3,2},{4,5},{5,4},{6,7},{7,6},{8,9},{9,8},{10,11... | collective-permute-start | bytes 3145736 | tf_op jit(solution)/shard_map/ppermute | solution.py:425
  102.5 4.1 %collective-permute-start.11 = (bf16[1024,512]{1,0:T(8,128)(2,1)}, bf16[1024,512]{1,0:T(8,128)(2,1)S(1)}, u32[]{:S(2)}, u32[]{:S(2)}) collective-permute-start(bf16[1024,512]{1,0:T(8,128)(2,1)} %get-tuple-element.69), channel_id=1, source_target_pairs={{0,1},{1,0},{2,3},{3,2},{4,5},{5,4},{6,7},{7,6},{8,9},{9,8},{10,11... | collective-permute-start | bytes 3145736 | tf_op jit(solution)/shard_map/ppermute | solution.py:437
  115.4 12.0 %collective-permute-start.14 = (bf16[3,64,1024]{2,1,0:T(8,128)(2,1)}, bf16[3,64,1024]{2,1,0:T(8,128)(2,1)S(1)}, u32[]{:S(2)}, u32[]{:S(2)}) collective-permute-start(bf16[3,64,1024]{2,1,0:T(8,128)(2,1)} %get-tuple-element.74), channel_id=1, source_target_pairs={{0,2},{1,3},{2,4},{3,5},{4,6},{5,7},{6,0},{7,1},{8,10},{9,11},{10,... | collective-permute-start | bytes 1179656 | tf_op jit(solution)/shard_map/ppermute | solution.py:474
  116.5 10.9 %collective-permute-start.15 = (bf16[3,64,1024]{2,1,0:T(8,128)(2,1)}, bf16[3,64,1024]{2,1,0:T(8,128)(2,1)S(1)}, u32[]{:S(2)}, u32[]{:S(2)}) collective-permute-start(bf16[3,64,1024]{2,1,0:T(8,128)(2,1)} %get-tuple-element.75), channel_id=1, source_target_pairs={{0,6},{1,7},{2,0},{3,1},{4,2},{5,3},{6,4},{7,5},{8,14},{9,15},{10,... | collective-permute-start | bytes 1179656 | tf_op jit(solution)/shard_map/ppermute | solution.py:474
  118.1 38.7 %copy-start.3 = (bf16[3,128,1024]{2,1,0:T(8,128)(2,1)S(1)}, bf16[3,128,1024]{2,1,0:T(8,128)(2,1)}, u32[]{:S(2)}) copy-start(bf16[3,128,1024]{2,1,0:T(8,128)(2,1)} %get-tuple-element.72.refs_0_.own_ref) | copy-start | bytes 2359300
  118.1 46.2 %copy-start.2 = (bf16[128,2048]{1,0:T(8,128)(2,1)S(1)}, bf16[128,2048]{1,0:T(8,128)(2,1)}, u32[]{:S(2)}) copy-start(bf16[128,2048]{1,0:T(8,128)(2,1)} %cot_ref.3) | copy-start | bytes 1572868
  125.1 39.1 %copy-start.17 = (f32[128,2]{0,1:T(2,128)S(1)}, f32[128,2]{0,1:T(2,128)}, u32[]{:S(2)}) copy-start(f32[128,2]{0,1:T(2,128)} %param.10) | copy-start | bytes 3076
  125.1 39.2 %copy-start.10 = (s32[128,2]{0,1:T(2,128)S(1)}, s32[128,2]{0,1:T(2,128)}, u32[]{:S(2)}) copy-start(s32[128,2]{0,1:T(2,128)} %param.9) | copy-start | bytes 3076
  128.7 28.1 %collective-permute-start.16 = (bf16[3,128,1024]{2,1,0:T(8,128)(2,1)S(1)}, bf16[3,128,1024]{2,1,0:T(8,128)(2,1)S(1)}, u32[]{:S(2)}, u32[]{:S(2)}) collective-permute-start(bf16[3,128,1024]{2,1,0:T(8,128)(2,1)S(1)} %get-tuple-element.78), channel_id=1, source_target_pairs={{0,2},{1,3},{2,4},{3,5},{4,6},{5,7},{6,0},{7,1},{8,10},{9,11},{10,... | collective-permute-start | bytes 2359304 | tf_op jit(solution)/shard_map/ppermute | solution.py:474
  129.7 27.1 %collective-permute-start.17 = (bf16[3,128,1024]{2,1,0:T(8,128)(2,1)S(1)}, bf16[3,128,1024]{2,1,0:T(8,128)(2,1)S(1)}, u32[]{:S(2)}, u32[]{:S(2)}) collective-permute-start(bf16[3,128,1024]{2,1,0:T(8,128)(2,1)S(1)} %get-tuple-element.79), channel_id=1, source_target_pairs={{0,6},{1,7},{2,0},{3,1},{4,2},{5,3},{6,4},{7,5},{8,14},{9,15},{10,... | collective-permute-start | bytes 2359304 | tf_op jit(solution)/shard_map/ppermute | solution.py:474
  131.7 25.1 %collective-permute-start.18 = (bf16[3,64,1024]{2,1,0:T(8,128)(2,1)}, bf16[3,64,1024]{2,1,0:T(8,128)(2,1)S(1)}, u32[]{:S(2)}, u32[]{:S(2)}) collective-permute-start(bf16[3,64,1024]{2,1,0:T(8,128)(2,1)} %get-tuple-element.80), channel_id=1, source_target_pairs={{0,2},{1,3},{2,4},{3,5},{4,6},{5,7},{6,0},{7,1},{8,10},{9,11},{10,... | collective-permute-start | bytes 1179656 | tf_op jit(solution)/shard_map/ppermute | solution.py:474
  131.7 25.1 %collective-permute-start.19 = (bf16[3,64,1024]{2,1,0:T(8,128)(2,1)}, bf16[3,64,1024]{2,1,0:T(8,128)(2,1)S(1)}, u32[]{:S(2)}, u32[]{:S(2)}) collective-permute-start(bf16[3,64,1024]{2,1,0:T(8,128)(2,1)} %get-tuple-element.81), channel_id=1, source_target_pairs={{0,6},{1,7},{2,0},{3,1},{4,2},{5,3},{6,4},{7,5},{8,14},{9,15},{10,... | collective-permute-start | bytes 1179656 | tf_op jit(solution)/shard_map/ppermute | solution.py:474
  159.1 21.4 %copy-start.1 = (bf16[3,128,1024]{2,1,0:T(8,128)(2,1)S(1)}, bf16[3,128,1024]{2,1,0:T(8,128)(2,1)}, u32[]{:S(2)}) copy-start(bf16[3,128,1024]{2,1,0:T(8,128)(2,1)} %get-tuple-element.73.refs_0_) | copy-start | bytes 2359300
  160.9 18.6 %collective-permute-start.20 = (bf16[3,128,1024]{2,1,0:T(8,128)(2,1)}, bf16[3,128,1024]{2,1,0:T(8,128)(2,1)S(1)}, u32[]{:S(2)}, u32[]{:S(2)}) collective-permute-start(bf16[3,128,1024]{2,1,0:T(8,128)(2,1)} %get-tuple-element.84), channel_id=1, source_target_pairs={{0,2},{1,3},{2,4},{3,5},{4,6},{5,7},{6,0},{7,1},{8,10},{9,11},{10,... | collective-permute-start | bytes 2359304 | tf_op jit(solution)/shard_map/ppermute | solution.py:474
  161.1 18.4 %collective-permute-start.21 = (bf16[3,128,1024]{2,1,0:T(8,128)(2,1)}, bf16[3,128,1024]{2,1,0:T(8,128)(2,1)S(1)}, u32[]{:S(2)}, u32[]{:S(2)}) collective-permute-start(bf16[3,128,1024]{2,1,0:T(8,128)(2,1)} %get-tuple-element.85), channel_id=1, source_target_pairs={{0,6},{1,7},{2,0},{3,1},{4,2},{5,3},{6,4},{7,5},{8,14},{9,15},{10,... | collective-permute-start | bytes 2359304 | tf_op jit(solution)/shard_map/ppermute | solution.py:474
  163.6 16.9 %collective-permute-start.22 = (bf16[3,128,1024]{2,1,0:T(8,128)(2,1)}, bf16[3,128,1024]{2,1,0:T(8,128)(2,1)}, u32[]{:S(2)}, u32[]{:S(2)}) collective-permute-start(bf16[3,128,1024]{2,1,0:T(8,128)(2,1)} %get-tuple-element.86), channel_id=1, source_target_pairs={{0,8},{1,9},{2,10},{3,11},{4,12},{5,13},{6,14},{7,15},{8,0},{9,1},... | collective-permute-start | bytes 2359304 | tf_op jit(solution)/shard_map/ppermute | solution.py:485
  (19 other events, 71.6 us)

commit v5 on v4

--- a/solution.py
+++ b/solution.py
@@ -205,7 +205,7 @@
 def hidden_kernel(at_ref, start_ref, *refs):
     x_refs, refs = refs[:Y], refs[Y:]
     wg_ref, wu_ref, hg_ref, out_ref, own_ref, other_ref, x, wg, wu, hg, out, own, other, ins, outs = refs
-    cuts = [slice(0, 256), slice(256, 512), slice(512, 1024)]
+    cuts = [slice(0, 512), slice(512, 1024)]
     cap = x_refs[0].shape[0] // 2
     pairs = [
         (r.at[n * cap : (n + 1) * cap], x.at[pl.ds(pl.multiple_of(at_ref[n * Y + k] * cap, cap), cap)])
@@ -302,7 +302,7 @@
 
 
 def outputs_kernel(cap, hid_ref, wd_ref, wg_ref, wu_ref, out_ref, hid, wd, wg, wu, out, ins, outs):
-    cuts = [slice(n * 512, (n + 1) * 512) for n in range(wd.shape[0] // 512)]
+    cuts = [slice(n * 1024, (n + 1) * 1024) for n in range(wd.shape[0] // 1024)]
     pairs = [(hid_ref.at[2], hid.at[2]), (wd_ref.at[cuts[0]], wd.at[cuts[0]])]
     pairs += [(hid_ref.at[0:2], hid.at[0:2])]
     pairs += [(wg_ref.at[cuts[0]], wg.at[cuts[0]]), (wu_ref.at[cuts[0]], wu.at[cuts[0]])]
@@ -387,7 +387,7 @@
         return [packed[0]] + [lax.ppermute(packed[k], "ep", y_shift(k)) for k in range(1, Y)]
 
     d_own = to_experts(packed)
-    (slices,) = call(copy_kernel, [struct(*slices.shape)], [slices, d_own[1]], in_specs=[None, ANY], vmem=16)
+    (slices,) = call(copy_kernel, [struct(*slices.shape)], [slices, d_own[2]], in_specs=[None, ANY], vmem=16)
     slices_p = lax.ppermute(slices, "ep", EP_SWAP)
     code_p, *packed = call(
         functools.partial(partner_kernel, cap),

time: 185 us -> 186 us (level)
    ppermute x9, starting transfers between devices: 13.3 us -> 15.3 us  [to_experts(): lax.ppermute(packed[k], 'ep', y_shift(k))]
where the time goes in v5:
time: 186 us; the launch traced here: 183 us
  waiting for transfers between devices  70.6 us (38%)
  Pallas kernels  55.9 us (30%)
  starting transfers between devices  44.7 us (24%)
  local copies, waits for them, and re-layouts  9.03 us (5%)
    pallas_call x13, Pallas kernels, call(): pl.pallas_call(body, grid=(1,) if blocks else (), in_specs=[s or whole(a)...  55.9 us
    ppermute x8, waiting for transfers between devices, shift(): return lax.ppermute(array, 'dp', x_shift(k))  35.6 us
    ppermute x9, waiting for transfers between devices, to_experts(): lax.ppermute(packed[k], 'ep', y_shift(k))  20.7 us
    ppermute x9, starting transfers between devices, to_experts(): lax.ppermute(packed[k], 'ep', y_shift(k))  15.3 us
    ppermute x8, starting transfers between devices, shift(): return lax.ppermute(array, 'dp', x_shift(k))  11.1 us
    unnamed x54, local copies, waits for them, and re-layouts  9.03 us
    all_to_all x1, starting transfers between devices, shards(): lax.all_to_all(checkpoint.reshape(dp, tokens, features // dp), 'dp', spli...  7.18 us
    ppermute x1, waiting for transfers between devices, shards(): slices_p = lax.ppermute(slices, 'ep', EP_SWAP)  5.47 us
  transfers between devices with their start and end apart: 25, of which 12 were waited for; matrix products, arithmetic and copies ran while one was open for 1% of the time, Pallas kernels for 23%

profile of v5, /device:TPU:1, one launch (start us, length us, event | category | flops | bytes accessed | tf_op | source)
XLA Modules:
  0.0 182.9 jit_solution(14270592552451511950)
XLA Ops:
  0.6 7.2 %all-to-all-start = ((bf16[16,128,128]{2,1,0:T(8,128)(2,1)}), bf16[16,128,128]{2,1,0:T(8,128)(2,1)S(1)}, u32[]{:S(2)}, u32[]{:S(2)}) async-start(bf16[16,128,128]{2,1,0:T(8,128)(2,1)} %bitcast.10), calls=%async_computation | async-start | bytes 1048576 | tf_op jit(solution)/shard_map/all_to_all | solution.py:382
  8.4 2.8 %shard_map.118 = (s32[2,128]{1,0:T(2,128)}, bf16[128,2176]{1,0:T(8,128)(2,1)}, bf16[64,2048]{1,0:T(8,128)(2,1)}, bf16[64,2048]{1,0:T(8,128)(2,1)}, bf16[64,2048]{1,0:T(8,128)(2,1)}, /*index=5*/bf16[64,2048]{1,0:T(8,128)(2,1)}) custom-call(s32[2]{0:T(128)} %pad_add_fusion.at_ref, s32[2,128]{1,0:T(2,128)} %bitcast.8, f32[2,128]{1,0:T(2,128)} %bitcast.11, ...), custom_call_target="tpu_custom_call" | custom-call | flops 134217728 | bytes 526344 | tf_op jit(solution)/shard_map/pallas_call | solution.py:59
  11.2 3.3 %collective-permute-start = (bf16[128,2176]{1,0:T(8,128)(2,1)}, bf16[128,2176]{1,0:T(8,128)(2,1)S(1)}, u32[]{:S(2)}, u32[]{:S(2)}) collective-permute-start(bf16[128,2176]{1,0:T(8,128)(2,1)} %get-tuple-element.49), channel_id=1, source_target_pairs={{0,16},{16,0},{32,48},{48,32},{64,80},{80,64},{96,112},{112,96},{1... | collective-permute-start | bytes 1671176 | tf_op jit(solution)/shard_map/ppermute | solution.py:381
  14.5 2.9 %collective-permute-start.1 = (bf16[64,2048]{1,0:T(8,128)(2,1)}, bf16[64,2048]{1,0:T(8,128)(2,1)S(1)}, u32[]{:S(2)}, u32[]{:S(2)}) collective-permute-start(bf16[64,2048]{1,0:T(8,128)(2,1)} %get-tuple-element.51), channel_id=1, source_target_pairs={{0,64},{16,80},{32,96},{48,112},{64,0},{80,16},{96,32},{112,48},{1... | collective-permute-start | bytes 786440 | tf_op jit(solution)/shard_map/ppermute | solution.py:387
  17.4 6.3 %collective-permute-done.1._.refs_2_ = bf16[64,2048]{1,0:T(8,128)(2,1)S(1)} collective-permute-done((bf16[64,2048]{1,0:T(8,128)(2,1)}, bf16[64,2048]{1,0:T(8,128)(2,1)S(1)}, u32[]{:S(2)}, u32[]{:S(2)}) %collective-permute-start.1) | collective-permute-done | bytes 262176 | tf_op jit(solution)/shard_map/ppermute | solution.py:387
  26.8 3.9 %collective-permute-done.wide_ref = bf16[128,2176]{1,0:T(8,128)(2,1)S(1)} collective-permute-done((bf16[128,2176]{1,0:T(8,128)(2,1)}, bf16[128,2176]{1,0:T(8,128)(2,1)S(1)}, u32[]{:S(2)}, u32[]{:S(2)}) %collective-permute-start) | collective-permute-done | bytes 557088 | tf_op jit(solution)/shard_map/ppermute | solution.py:381
  33.9 2.6 %collective-permute-start.9 = (bf16[64,2048]{1,0:T(8,128)(2,1)S(1)}, bf16[64,2048]{1,0:T(8,128)(2,1)S(1)}, u32[]{:S(2)}, u32[]{:S(2)}) collective-permute-start(bf16[64,2048]{1,0:T(8,128)(2,1)S(1)} %get-tuple-element.61), channel_id=1, source_target_pairs={{0,64},{16,80},{32,96},{48,112},{64,0},{80,16},{96,32},{112,48},{1... | collective-permute-start | bytes 786440 | tf_op jit(solution)/shard_map/ppermute | solution.py:387
  36.5 5.5 %collective-permute-done.2.slices_p_ref = bf16[16,128,128]{2,1,0:T(8,128)(2,1)S(1)} collective-permute-done((bf16[16,128,128]{2,1,0:T(8,128)(2,1)S(1)}, bf16[16,128,128]{2,1,0:T(8,128)(2,1)S(1)}, u32[]{:S(2)}, u32[]{:S(2)}) %collective-permute-start.2) | collective-permute-done | bytes 524320 | tf_op jit(solution)/shard_map/ppermute | solution.py:391
  42.0 2.7 %collective-permute-start.10 = (bf16[64,2048]{1,0:T(8,128)(2,1)S(1)}, bf16[64,2048]{1,0:T(8,128)(2,1)S(1)}, u32[]{:S(2)}, u32[]{:S(2)}) collective-permute-start(bf16[64,2048]{1,0:T(8,128)(2,1)S(1)} %get-tuple-element.62), channel_id=1, source_target_pairs={{0,96},{16,112},{32,0},{48,16},{64,32},{80,48},{96,64},{112,80},{1... | collective-permute-start | bytes 786440 | tf_op jit(solution)/shard_map/ppermute | solution.py:387
  46.5 1.6 collective-permute-start.4
  51.3 6.6 %shard_map.122 = (f32[512,1024]{1,0:T(8,128)}, bf16[1024,512]{1,0:T(8,128)(2,1)}, bf16[1024,512]{1,0:T(8,128)(2,1)}) custom-call(s32[8]{0:T(128)} %fusion.5.at_ref, s32[16]{0:T(128)} %fusion.3.start_ref, bf16[64,2048]{1,0:T(8,128)(2,1)} %get-tuple-element.57.refs_0_, bf16[64,2048]{1,0:T(8,128)(2,1)} %copy-done.21, bf16[64,2048]{1,0:T(8,128)(2,1)} %copy-done.8, ...), custom_call_target="tpu_custom_call" | custom-call | flops 2147483648 | bytes 6291552 | tf_op jit(solution)/shard_map/pallas_call | solution.py:59
  57.9 3.5 %collective-permute-done.3.refs_1_ = bf16[128,2048]{1,0:T(8,128)(2,1)S(1)} collective-permute-done((bf16[128,2048]{1,0:T(8,128)(2,1)S(1)}, bf16[128,2048]{1,0:T(8,128)(2,1)S(1)}, u32[]{:S(2)}, u32[]{:S(2)}) %collective-permute-start.3) | collective-permute-done | bytes 524320 | tf_op jit(solution)/shard_map/ppermute | solution.py:387
  61.4 9.2 %collective-permute-done.4.refs_2_ = bf16[128,2048]{1,0:T(8,128)(2,1)S(1)} collective-permute-done((bf16[128,2048]{1,0:T(8,128)(2,1)S(1)}, bf16[128,2048]{1,0:T(8,128)(2,1)S(1)}, u32[]{:S(2)}, u32[]{:S(2)}) %collective-permute-start.4) | collective-permute-done | bytes 524320 | tf_op jit(solution)/shard_map/ppermute | solution.py:387
  70.6 1.8 collective-permute-done.5.refs_3_
  73.2 10.6 %shard_map.123 = (bf16[3,512,1024]{2,1,0:T(8,128)(2,1)}, bf16[1024,512]{1,0:T(8,128)(2,1)}, bf16[1024,512]{1,0:T(8,128)(2,1)}) custom-call(s32[8]{0:T(128)} %fusion.5.at_ref, s32[16]{0:T(128)} %fusion.3.start_ref, bf16[128,2048]{1,0:T(8,128)(2,1)} %copy-done.13, bf16[128,2048]{1,0:T(8,128)(2,1)} %copy-done.18, bf16[128,2048]{1,0:T(8,128)(2,1)} %copy-done.19, ...), custom_call_target="tpu_custom_call" | custom-call | flops 4294967296 | bytes 12583008 | tf_op jit(solution)/shard_map/pallas_call | solution.py:59
  83.8 1.8 collective-permute-start.13
  85.5 11.4 %shard_map.124.refs_0_ = bf16[8,2,64,2048]{3,2,1,0:T(8,128)(2,1)} custom-call(bf16[3,512,1024]{2,1,0:T(8,128)(2,1)} %get-tuple-element.64.hid_ref.ho_ref, bf16[2048,1024]{1,0:T(8,128)(2,1)} %bitcast.17, bf16[2048,1024]{1,0:T(8,128)(2,1)} %bitcast.13, bf16[2048,1024]{1,0:T(8,128)(2,1)} %bitcast.15), custom_call_target="tpu_custom_call" | custom-call | flops 6442450944 | bytes 15728640 | tf_op jit(solution)/shard_map/pallas_call | solution.py:59
  96.9 4.6 %all-to-all-start.1 = ((bf16[8,2,64,2048]{3,2,1,0:T(8,128)(2,1)}), bf16[8,2,64,2048]{3,2,1,0:T(8,128)(2,1)}, u32[]{:S(2)}, u32[]{:S(2)}) async-start(bf16[8,2,64,2048]{3,2,1,0:T(8,128)(2,1)} %shard_map.124.refs_0_), calls=%async_computation.1 | async-start | bytes 8388608 | tf_op jit(solution)/shard_map/all_to_all | solution.py:447
  102.1 2.4 %collective-permute-done.12.dp_ref = bf16[1024,512]{1,0:T(8,128)(2,1)S(1)} collective-permute-done((bf16[1024,512]{1,0:T(8,128)(2,1)}, bf16[1024,512]{1,0:T(8,128)(2,1)S(1)}, u32[]{:S(2)}, u32[]{:S(2)}) %collective-permute-start.12) | collective-permute-done | bytes 1048608 | tf_op jit(solution)/shard_map/ppermute | solution.py:425
  104.5 1.5 collective-permute-done.11.xp_ref
  108.0 6.8 %shard_map.126 = (bf16[3,128,1024]{2,1,0:T(8,128)(2,1)}, bf16[3,128,1024]{2,1,0:T(8,128)(2,1)}, bf16[3,64,1024]{2,1,0:T(8,128)(2,1)}, bf16[3,64,1024]{2,1,0:T(8,128)(2,1)}, bf16[3,128,1024]{2,1,0:T(8,128)(2,1)}) custom-call(bf16[1024,512]{1,0:T(8,128)(2,1)} %get-tuple-element.68.xo_ref, bf16[1024,512]{1,0:T(8,128)(2,1)} %copy-done.16, ...), custom_call_target="tpu_custom_call" | custom-call | flops 3221225472 | bytes 14680064 | tf_op jit(solution)/shard_map/pallas_call | solution.py:59
  115.3 2.3 %collective-permute-start.15 = (bf16[3,64,1024]{2,1,0:T(8,128)(2,1)}, bf16[3,64,1024]{2,1,0:T(8,128)(2,1)S(1)}, u32[]{:S(2)}, u32[]{:S(2)}) collective-permute-start(bf16[3,64,1024]{2,1,0:T(8,128)(2,1)} %get-tuple-element.75), channel_id=1, source_target_pairs={{0,6},{1,7},{2,0},{3,1},{4,2},{5,3},{6,4},{7,5},{8,14},{9,15},{10,... | collective-permute-start | bytes 1179656 | tf_op jit(solution)/shard_map/ppermute | solution.py:474
  117.6 6.9 %shard_map.127 = (bf16[3,128,1024]{2,1,0:T(8,128)(2,1)}, bf16[3,128,1024]{2,1,0:T(8,128)(2,1)}, bf16[3,64,1024]{2,1,0:T(8,128)(2,1)}, bf16[3,64,1024]{2,1,0:T(8,128)(2,1)}, bf16[3,128,1024]{2,1,0:T(8,128)(2,1)}) custom-call(bf16[1024,512]{1,0:T(8,128)(2,1)} %get-tuple-element.68.xo_ref, bf16[1024,512]{1,0:T(8,128)(2,1)} %copy-done.16, ...), custom_call_target="tpu_custom_call" | custom-call | flops 3221225472 | bytes 11272192 | tf_op jit(solution)/shard_map/pallas_call | solution.py:59
  124.5 2.4 %collective-permute-done.14.up_ref = bf16[3,64,1024]{2,1,0:T(8,128)(2,1)S(1)} collective-permute-done((bf16[3,64,1024]{2,1,0:T(8,128)(2,1)}, bf16[3,64,1024]{2,1,0:T(8,128)(2,1)S(1)}, u32[]{:S(2)}, u32[]{:S(2)}) %collective-permute-start.14) | collective-permute-done | bytes 393248 | tf_op jit(solution)/shard_map/ppermute | solution.py:474
  128.9 2.5 %collective-permute-start.17 = (bf16[3,128,1024]{2,1,0:T(8,128)(2,1)S(1)}, bf16[3,128,1024]{2,1,0:T(8,128)(2,1)S(1)}, u32[]{:S(2)}, u32[]{:S(2)}) collective-permute-start(bf16[3,128,1024]{2,1,0:T(8,128)(2,1)S(1)} %get-tuple-element.79), channel_id=1, source_target_pairs={{0,6},{1,7},{2,0},{3,1},{4,2},{5,3},{6,4},{7,5},{8,14},{9,15},{10,... | collective-permute-start | bytes 2359304 | tf_op jit(solution)/shard_map/ppermute | solution.py:474
  131.3 2.7 %collective-permute-start.19 = (bf16[3,64,1024]{2,1,0:T(8,128)(2,1)}, bf16[3,64,1024]{2,1,0:T(8,128)(2,1)S(1)}, u32[]{:S(2)}, u32[]{:S(2)}) collective-permute-start(bf16[3,64,1024]{2,1,0:T(8,128)(2,1)} %get-tuple-element.81), channel_id=1, source_target_pairs={{0,6},{1,7},{2,0},{3,1},{4,2},{5,3},{6,4},{7,5},{8,14},{9,15},{10,... | collective-permute-start | bytes 1179656 | tf_op jit(solution)/shard_map/ppermute | solution.py:474
  134.0 22.6 %collective-permute-done.18.refs_0_ = bf16[3,64,1024]{2,1,0:T(8,128)(2,1)S(1)} collective-permute-done((bf16[3,64,1024]{2,1,0:T(8,128)(2,1)}, bf16[3,64,1024]{2,1,0:T(8,128)(2,1)S(1)}, u32[]{:S(2)}, u32[]{:S(2)}) %collective-permute-start.18) | collective-permute-done | bytes 393248 | tf_op jit(solution)/shard_map/ppermute | solution.py:474
  158.9 1.8 shard_map.129
  160.9 2.5 %collective-permute-start.21 = (bf16[3,128,1024]{2,1,0:T(8,128)(2,1)}, bf16[3,128,1024]{2,1,0:T(8,128)(2,1)S(1)}, u32[]{:S(2)}, u32[]{:S(2)}) collective-permute-start(bf16[3,128,1024]{2,1,0:T(8,128)(2,1)} %get-tuple-element.85), channel_id=1, source_target_pairs={{0,6},{1,7},{2,0},{3,1},{4,2},{5,3},{6,4},{7,5},{8,14},{9,15},{10,... | collective-permute-start | bytes 2359304 | tf_op jit(solution)/shard_map/ppermute | solution.py:474
  163.9 4.3 %shard_map.125 = (bf16[128,2048]{1,0:T(8,128)(2,1)}, bf16[128,2048]{1,0:T(8,128)(2,1)}, f32[128,2]{1,0:T(8,128)S(1)}) custom-call(s32[2,128]{1,0:T(2,128)S(1)} %bitcast.9, f32[128,2]{1,0:T(8,128)S(1)} %copy.13.gates_ref, bf16[128,2048]{1,0:T(8,128)(2,1)S(1)} %copy-done.2, bf16[8,2,64,2048]{3,2,1,0:T(8,128)(2,1)} %all-to-all-done.1.rows_ref), custom_call_target="tpu_custom_call" | custom-call | flops 805306368 | bytes 4720640 | tf_op jit(solution)/shard_map/pallas_call | solution.py:59
  168.9 10.6 %collective-permute-done.20.refs_1_ = bf16[3,128,1024]{2,1,0:T(8,128)(2,1)S(1)} collective-permute-done((bf16[3,128,1024]{2,1,0:T(8,128)(2,1)}, bf16[3,128,1024]{2,1,0:T(8,128)(2,1)S(1)}, u32[]{:S(2)}, u32[]{:S(2)}) %collective-permute-start.20) | collective-permute-done | bytes 786464 | tf_op jit(solution)/shard_map/ppermute | solution.py:474
  180.5 2.4 %shard_map.130 = (f32[1,128,1024]{2,1,0:T(8,128)}, f32[1,128,1024]{2,1,0:T(8,128)}, f32[1,128,1024]{2,1,0:T(8,128)}) custom-call(bf16[3,128,1024]{2,1,0:T(8,128)(2,1)S(1)} %copy-done.1, bf16[3,128,1024]{2,1,0:T(8,128)(2,1)S(1)} %collective-permute-done.20.refs_1_, bf16[3,128,1024]{2,1,0:T(8,128)(2,1)S(1)} %collective-permute-done.21.refs_2_, ...), custom_call_target="tpu_custom_call" | custom-call | bytes 3145728 | tf_op jit(solution)/shard_map/pallas_call | solution.py:59
  (89 shorter events, 22.2 us)
Async XLA Ops:
  0.6 23.0 %all-to-all-start = ((bf16[16,128,128]{2,1,0:T(8,128)(2,1)}), bf16[16,128,128]{2,1,0:T(8,128)(2,1)S(1)}, u32[]{:S(2)}, u32[]{:S(2)}) async-start(bf16[16,128,128]{2,1,0:T(8,128)(2,1)} %bitcast.10), calls=%async_computation | async-start | bytes 1048576 | tf_op jit(solution)/shard_map/all_to_all | solution.py:382
  11.2 19.6 %collective-permute-start = (bf16[128,2176]{1,0:T(8,128)(2,1)}, bf16[128,2176]{1,0:T(8,128)(2,1)S(1)}, u32[]{:S(2)}, u32[]{:S(2)}) collective-permute-start(bf16[128,2176]{1,0:T(8,128)(2,1)} %get-tuple-element.49), channel_id=1, source_target_pairs={{0,16},{16,0},{32,48},{48,32},{64,80},{80,64},{96,112},{112,96},{1... | collective-permute-start | bytes 1671176 | tf_op jit(solution)/shard_map/ppermute | solution.py:381
  14.5 9.2 %collective-permute-start.1 = (bf16[64,2048]{1,0:T(8,128)(2,1)}, bf16[64,2048]{1,0:T(8,128)(2,1)S(1)}, u32[]{:S(2)}, u32[]{:S(2)}) collective-permute-start(bf16[64,2048]{1,0:T(8,128)(2,1)} %get-tuple-element.51), channel_id=1, source_target_pairs={{0,64},{16,80},{32,96},{48,112},{64,0},{80,16},{96,32},{112,48},{1... | collective-permute-start | bytes 786440 | tf_op jit(solution)/shard_map/ppermute | solution.py:387
  23.6 26.9 %copy-start.8 = (bf16[64,2048]{1,0:T(8,128)(2,1)}, bf16[64,2048]{1,0:T(8,128)(2,1)S(1)}, u32[]{:S(2)}) copy-start(bf16[64,2048]{1,0:T(8,128)(2,1)S(1)} %collective-permute-done.1._.refs_2_) | copy-start | bytes 786436
  23.7 18.3 %collective-permute-start.2 = (bf16[16,128,128]{2,1,0:T(8,128)(2,1)S(1)}, bf16[16,128,128]{2,1,0:T(8,128)(2,1)S(1)}, u32[]{:S(2)}, u32[]{:S(2)}) collective-permute-start(bf16[16,128,128]{2,1,0:T(8,128)(2,1)S(1)} %shard_map.120.slices_o_ref), channel_id=1, source_target_pairs={{0,16},{16,0},{32,48},{48,32},{64,80},{80,64},{96,112},{112,96},{1... | collective-permute-start | bytes 1572872 | tf_op jit(solution)/shard_map/ppermute | solution.py:391
  24.1 22.3 %collective-permute-start.6 = (bf16[64,2048]{1,0:T(8,128)(2,1)}, bf16[64,2048]{1,0:T(8,128)(2,1)S(1)}, u32[]{:S(2)}, u32[]{:S(2)}) collective-permute-start(bf16[64,2048]{1,0:T(8,128)(2,1)} %get-tuple-element.58), channel_id=1, source_target_pairs={{0,32},{16,48},{32,64},{48,80},{64,96},{80,112},{96,0},{112,16},{1... | collective-permute-start | bytes 786440 | tf_op jit(solution)/shard_map/ppermute | solution.py:387
  25.4 21.1 %collective-permute-start.7 = (bf16[64,2048]{1,0:T(8,128)(2,1)}, bf16[64,2048]{1,0:T(8,128)(2,1)S(1)}, u32[]{:S(2)}, u32[]{:S(2)}) collective-permute-start(bf16[64,2048]{1,0:T(8,128)(2,1)} %get-tuple-element.59), channel_id=1, source_target_pairs={{0,96},{16,112},{32,0},{48,16},{64,32},{80,48},{96,64},{112,80},{1... | collective-permute-start | bytes 786440 | tf_op jit(solution)/shard_map/ppermute | solution.py:387
  32.5 15.6 %collective-permute-start.8 = (bf16[64,2048]{1,0:T(8,128)(2,1)S(1)}, bf16[64,2048]{1,0:T(8,128)(2,1)S(1)}, u32[]{:S(2)}, u32[]{:S(2)}) collective-permute-start(bf16[64,2048]{1,0:T(8,128)(2,1)S(1)} %get-tuple-element.60), channel_id=1, source_target_pairs={{0,32},{16,48},{32,64},{48,80},{64,96},{80,112},{96,0},{112,16},{1... | collective-permute-start | bytes 786440 | tf_op jit(solution)/shard_map/ppermute | solution.py:387
  33.9 16.6 %collective-permute-start.9 = (bf16[64,2048]{1,0:T(8,128)(2,1)S(1)}, bf16[64,2048]{1,0:T(8,128)(2,1)S(1)}, u32[]{:S(2)}, u32[]{:S(2)}) collective-permute-start(bf16[64,2048]{1,0:T(8,128)(2,1)S(1)} %get-tuple-element.61), channel_id=1, source_target_pairs={{0,64},{16,80},{32,96},{48,112},{64,0},{80,16},{96,32},{112,48},{1... | collective-permute-start | bytes 786440 | tf_op jit(solution)/shard_map/ppermute | solution.py:387
  42.0 8.5 %collective-permute-start.10 = (bf16[64,2048]{1,0:T(8,128)(2,1)S(1)}, bf16[64,2048]{1,0:T(8,128)(2,1)S(1)}, u32[]{:S(2)}, u32[]{:S(2)}) collective-permute-start(bf16[64,2048]{1,0:T(8,128)(2,1)S(1)} %get-tuple-element.62), channel_id=1, source_target_pairs={{0,96},{16,112},{32,0},{48,16},{64,32},{80,48},{96,64},{112,80},{1... | collective-permute-start | bytes 786440 | tf_op jit(solution)/shard_map/ppermute | solution.py:387
  46.3 26.0 %copy-start.13 = (bf16[128,2048]{1,0:T(8,128)(2,1)}, bf16[128,2048]{1,0:T(8,128)(2,1)S(1)}, u32[]{:S(2)}) copy-start(bf16[128,2048]{1,0:T(8,128)(2,1)S(1)} %get-tuple-element.53.refs_0_) | copy-start | bytes 1572868
  46.4 15.0 %collective-permute-start.3 = (bf16[128,2048]{1,0:T(8,128)(2,1)S(1)}, bf16[128,2048]{1,0:T(8,128)(2,1)S(1)}, u32[]{:S(2)}, u32[]{:S(2)}) collective-permute-start(bf16[128,2048]{1,0:T(8,128)(2,1)S(1)} %get-tuple-element.54), channel_id=1, source_target_pairs={{0,32},{16,48},{32,64},{48,80},{64,96},{80,112},{96,0},{112,16},{1... | collective-permute-start | bytes 1572872 | tf_op jit(solution)/shard_map/ppermute | solution.py:387
  46.5 24.1 %collective-permute-start.4 = (bf16[128,2048]{1,0:T(8,128)(2,1)S(1)}, bf16[128,2048]{1,0:T(8,128)(2,1)S(1)}, u32[]{:S(2)}, u32[]{:S(2)}) collective-permute-start(bf16[128,2048]{1,0:T(8,128)(2,1)S(1)} %get-tuple-element.55), channel_id=1, source_target_pairs={{0,64},{16,80},{32,96},{48,112},{64,0},{80,16},{96,32},{112,48},{1... | collective-permute-start | bytes 1572872 | tf_op jit(solution)/shard_map/ppermute | solution.py:387
  48.1 24.3 %collective-permute-start.5 = (bf16[128,2048]{1,0:T(8,128)(2,1)S(1)}, bf16[128,2048]{1,0:T(8,128)(2,1)S(1)}, u32[]{:S(2)}, u32[]{:S(2)}) collective-permute-start(bf16[128,2048]{1,0:T(8,128)(2,1)S(1)} %get-tuple-element.56), channel_id=1, source_target_pairs={{0,96},{16,112},{32,0},{48,16},{64,32},{80,48},{96,64},{112,80},{1... | collective-permute-start | bytes 1572872 | tf_op jit(solution)/shard_map/ppermute | solution.py:387
  83.8 22.2 %collective-permute-start.13 = (bf16[3,512,1024]{2,1,0:T(8,128)(2,1)}, bf16[3,512,1024]{2,1,0:T(8,128)(2,1)S(1)}, u32[]{:S(2)}, u32[]{:S(2)}) collective-permute-start(bf16[3,512,1024]{2,1,0:T(8,128)(2,1)} %get-tuple-element.64.hid_ref.ho_ref), channel_id=1, source_target_pairs={{0,1},{1,0},{2,3},{3,2},{4,5},{5,4},{6,7},{7,6},{8,9},{9,8},{10,11... | collective-permute-start | bytes 9437192 | tf_op jit(solution)/shard_map/ppermute | solution.py:436
  96.9 67.0 %all-to-all-start.1 = ((bf16[8,2,64,2048]{3,2,1,0:T(8,128)(2,1)}), bf16[8,2,64,2048]{3,2,1,0:T(8,128)(2,1)}, u32[]{:S(2)}, u32[]{:S(2)}) async-start(bf16[8,2,64,2048]{3,2,1,0:T(8,128)(2,1)} %shard_map.124.refs_0_), calls=%async_computation.1 | async-start | bytes 8388608 | tf_op jit(solution)/shard_map/all_to_all | solution.py:447
  101.5 3.0 %collective-permute-start.12 = (bf16[1024,512]{1,0:T(8,128)(2,1)}, bf16[1024,512]{1,0:T(8,128)(2,1)S(1)}, u32[]{:S(2)}, u32[]{:S(2)}) collective-permute-start(bf16[1024,512]{1,0:T(8,128)(2,1)} %get-tuple-element.71), channel_id=1, source_target_pairs={{0,1},{1,0},{2,3},{3,2},{4,5},{5,4},{6,7},{7,6},{8,9},{9,8},{10,11... | collective-permute-start | bytes 3145736 | tf_op jit(solution)/shard_map/ppermute | solution.py:425
  101.8 4.2 %collective-permute-start.11 = (bf16[1024,512]{1,0:T(8,128)(2,1)}, bf16[1024,512]{1,0:T(8,128)(2,1)S(1)}, u32[]{:S(2)}, u32[]{:S(2)}) collective-permute-start(bf16[1024,512]{1,0:T(8,128)(2,1)} %get-tuple-element.69), channel_id=1, source_target_pairs={{0,1},{1,0},{2,3},{3,2},{4,5},{5,4},{6,7},{7,6},{8,9},{9,8},{10,11... | collective-permute-start | bytes 3145736 | tf_op jit(solution)/shard_map/ppermute | solution.py:437
  114.8 12.1 %collective-permute-start.14 = (bf16[3,64,1024]{2,1,0:T(8,128)(2,1)}, bf16[3,64,1024]{2,1,0:T(8,128)(2,1)S(1)}, u32[]{:S(2)}, u32[]{:S(2)}) collective-permute-start(bf16[3,64,1024]{2,1,0:T(8,128)(2,1)} %get-tuple-element.74), channel_id=1, source_target_pairs={{0,2},{1,3},{2,4},{3,5},{4,6},{5,7},{6,0},{7,1},{8,10},{9,11},{10,... | collective-permute-start | bytes 1179656 | tf_op jit(solution)/shard_map/ppermute | solution.py:474
  115.3 11.7 %collective-permute-start.15 = (bf16[3,64,1024]{2,1,0:T(8,128)(2,1)}, bf16[3,64,1024]{2,1,0:T(8,128)(2,1)S(1)}, u32[]{:S(2)}, u32[]{:S(2)}) collective-permute-start(bf16[3,64,1024]{2,1,0:T(8,128)(2,1)} %get-tuple-element.75), channel_id=1, source_target_pairs={{0,6},{1,7},{2,0},{3,1},{4,2},{5,3},{6,4},{7,5},{8,14},{9,15},{10,... | collective-permute-start | bytes 1179656 | tf_op jit(solution)/shard_map/ppermute | solution.py:474
  117.6 39.0 %copy-start.3 = (bf16[3,128,1024]{2,1,0:T(8,128)(2,1)S(1)}, bf16[3,128,1024]{2,1,0:T(8,128)(2,1)}, u32[]{:S(2)}) copy-start(bf16[3,128,1024]{2,1,0:T(8,128)(2,1)} %get-tuple-element.72.refs_0_.own_ref) | copy-start | bytes 2359300
  117.6 46.3 %copy-start.2 = (bf16[128,2048]{1,0:T(8,128)(2,1)S(1)}, bf16[128,2048]{1,0:T(8,128)(2,1)}, u32[]{:S(2)}) copy-start(bf16[128,2048]{1,0:T(8,128)(2,1)} %cot_ref.3) | copy-start | bytes 1572868
  124.5 39.3 %copy-start.17 = (f32[128,2]{0,1:T(2,128)S(1)}, f32[128,2]{0,1:T(2,128)}, u32[]{:S(2)}) copy-start(f32[128,2]{0,1:T(2,128)} %param.10) | copy-start | bytes 3076
  124.5 39.4 %copy-start.10 = (s32[128,2]{0,1:T(2,128)S(1)}, s32[128,2]{0,1:T(2,128)}, u32[]{:S(2)}) copy-start(s32[128,2]{0,1:T(2,128)} %param.9) | copy-start | bytes 3076
  128.3 28.3 %collective-permute-start.16 = (bf16[3,128,1024]{2,1,0:T(8,128)(2,1)S(1)}, bf16[3,128,1024]{2,1,0:T(8,128)(2,1)S(1)}, u32[]{:S(2)}, u32[]{:S(2)}) collective-permute-start(bf16[3,128,1024]{2,1,0:T(8,128)(2,1)S(1)} %get-tuple-element.78), channel_id=1, source_target_pairs={{0,2},{1,3},{2,4},{3,5},{4,6},{5,7},{6,0},{7,1},{8,10},{9,11},{10,... | collective-permute-start | bytes 2359304 | tf_op jit(solution)/shard_map/ppermute | solution.py:474
  128.9 27.7 %collective-permute-start.17 = (bf16[3,128,1024]{2,1,0:T(8,128)(2,1)S(1)}, bf16[3,128,1024]{2,1,0:T(8,128)(2,1)S(1)}, u32[]{:S(2)}, u32[]{:S(2)}) collective-permute-start(bf16[3,128,1024]{2,1,0:T(8,128)(2,1)S(1)} %get-tuple-element.79), channel_id=1, source_target_pairs={{0,6},{1,7},{2,0},{3,1},{4,2},{5,3},{6,4},{7,5},{8,14},{9,15},{10,... | collective-permute-start | bytes 2359304 | tf_op jit(solution)/shard_map/ppermute | solution.py:474
  131.3 25.2 %collective-permute-start.18 = (bf16[3,64,1024]{2,1,0:T(8,128)(2,1)}, bf16[3,64,1024]{2,1,0:T(8,128)(2,1)S(1)}, u32[]{:S(2)}, u32[]{:S(2)}) collective-permute-start(bf16[3,64,1024]{2,1,0:T(8,128)(2,1)} %get-tuple-element.80), channel_id=1, source_target_pairs={{0,2},{1,3},{2,4},{3,5},{4,6},{5,7},{6,0},{7,1},{8,10},{9,11},{10,... | collective-permute-start | bytes 1179656 | tf_op jit(solution)/shard_map/ppermute | solution.py:474
  131.3 25.2 %collective-permute-start.19 = (bf16[3,64,1024]{2,1,0:T(8,128)(2,1)}, bf16[3,64,1024]{2,1,0:T(8,128)(2,1)S(1)}, u32[]{:S(2)}, u32[]{:S(2)}) collective-permute-start(bf16[3,64,1024]{2,1,0:T(8,128)(2,1)} %get-tuple-element.81), channel_id=1, source_target_pairs={{0,6},{1,7},{2,0},{3,1},{4,2},{5,3},{6,4},{7,5},{8,14},{9,15},{10,... | collective-permute-start | bytes 1179656 | tf_op jit(solution)/shard_map/ppermute | solution.py:474
  158.9 21.6 %copy-start.1 = (bf16[3,128,1024]{2,1,0:T(8,128)(2,1)S(1)}, bf16[3,128,1024]{2,1,0:T(8,128)(2,1)}, u32[]{:S(2)}) copy-start(bf16[3,128,1024]{2,1,0:T(8,128)(2,1)} %get-tuple-element.73.refs_0_) | copy-start | bytes 2359300
  160.7 18.8 %collective-permute-start.20 = (bf16[3,128,1024]{2,1,0:T(8,128)(2,1)}, bf16[3,128,1024]{2,1,0:T(8,128)(2,1)S(1)}, u32[]{:S(2)}, u32[]{:S(2)}) collective-permute-start(bf16[3,128,1024]{2,1,0:T(8,128)(2,1)} %get-tuple-element.84), channel_id=1, source_target_pairs={{0,2},{1,3},{2,4},{3,5},{4,6},{5,7},{6,0},{7,1},{8,10},{9,11},{10,... | collective-permute-start | bytes 2359304 | tf_op jit(solution)/shard_map/ppermute | solution.py:474
  160.9 18.6 %collective-permute-start.21 = (bf16[3,128,1024]{2,1,0:T(8,128)(2,1)}, bf16[3,128,1024]{2,1,0:T(8,128)(2,1)S(1)}, u32[]{:S(2)}, u32[]{:S(2)}) collective-permute-start(bf16[3,128,1024]{2,1,0:T(8,128)(2,1)} %get-tuple-element.85), channel_id=1, source_target_pairs={{0,6},{1,7},{2,0},{3,1},{4,2},{5,3},{6,4},{7,5},{8,14},{9,15},{10,... | collective-permute-start | bytes 2359304 | tf_op jit(solution)/shard_map/ppermute | solution.py:474
  163.4 17.1 %collective-permute-start.22 = (bf16[3,128,1024]{2,1,0:T(8,128)(2,1)}, bf16[3,128,1024]{2,1,0:T(8,128)(2,1)}, u32[]{:S(2)}, u32[]{:S(2)}) collective-permute-start(bf16[3,128,1024]{2,1,0:T(8,128)(2,1)} %get-tuple-element.86), channel_id=1, source_target_pairs={{0,8},{1,9},{2,10},{3,11},{4,12},{5,13},{6,14},{7,15},{8,0},{9,1},... | collective-permute-start | bytes 2359304 | tf_op jit(solution)/shard_map/ppermute | solution.py:485
  (19 other events, 71.9 us)
